TPU v7x, 32 devices: a whole 2x2x4 slice. The times are simulated.
32 devices in a mesh: seq: 8 (over z, y), batch: 4 (over x, core).
Axes of the slice: x: 2, y: 2, z: 4, core: 2. Of those that a mesh axis runs over, the one named last changes fastest.
Arguments:
- inputs: bfloat16 [2048, 4, 1024], P('seq', 'batch'), may hold values from -6 to 6
- lengths: int32 [4], P('batch'), may hold values from 1024 to 2048, as said below
- w_query: bfloat16 [1024, 1024], P(('seq', 'batch')), may hold values from -0.1875 to 0.1875
- key_weight: bfloat16 [1024, 512], P(('seq', 'batch')), may hold values from -0.1875 to 0.1875
- value_weight: bfloat16 [1024, 512], P(('seq', 'batch')), may hold values from -0.1875 to 0.1875
- w_out: bfloat16 [1024, 1024], P(('seq', 'batch')), may hold values from -3 to 3
- w_gate: bfloat16 [1024, 4608], P(('seq', 'batch')), may hold values from -0.1875 to 0.1875
- w_up: bfloat16 [1024, 4608], P(('seq', 'batch')), may hold values from -0.1875 to 0.1875
- w_down: bfloat16 [4608, 1024], P(('seq', 'batch')), may hold values from -0.09375 to 0.09375
- gain_attn: float32 [1024], replicated, may hold values from 0.1 to 1.9
- gain_ffn: float32 [1024], replicated, may hold values from 0.1 to 1.9
- gain_query: float32 [64], replicated, may hold values from 0.1 to 1.9
- gain_key: float32 [64], replicated, may hold values from 0.1 to 1.9
- cotangent: bfloat16 [2048, 4, 1024], P('seq', 'batch'), may hold values from -6 to 6
Outputs:
- output: bfloat16 [2048, 4, 1024], P('seq', 'batch')
- grad_inputs: bfloat16 [2048, 4, 1024], P('seq', 'batch')
- grad_query: float32 [1024, 1024], P(('seq', 'batch'))
- grad_key: float32 [1024, 512], P(('seq', 'batch'))
- grad_value: float32 [1024, 512], P(('seq', 'batch'))
- grad_out: float32 [1024, 1024], P(('seq', 'batch'))
- grad_gate: float32 [1024, 4608], P(('seq', 'batch'))
- grad_up: float32 [1024, 4608], P(('seq', 'batch'))
- grad_down: float32 [4608, 1024], P(('seq', 'batch'))
- grad_gain_attn: float32 [1024], replicated
- grad_gain_ffn: float32 [1024], replicated
- grad_gain_query: float32 [64], replicated
- grad_gain_key: float32 [64], replicated
Inputs may be any that keep to these rules, and one draw needn't show every extreme that they name: `lengths`: in each aligned block of 1 entries (the sequences of one index of batch) at least one length equals 2048.
All inputs are finite; a program needn't handle non-finite values.
Results may differ from a plain program's by a relative error of at most 0.025.
Values may be sent and summed in bfloat16 or wider, within the bound.
A program may use at most 256 MiB of HBM per device.

v0:
```python
import jax
import jax.numpy as jnp
from jax import lax
from jax.sharding import PartitionSpec as P

eps = 1e-05
theta = 1000000.0


def rms_factor(v):
    return lax.rsqrt(jnp.mean(v * v, axis=-1, keepdims=True) + eps)


def rotary_tables(positions, width):
    half = width // 2
    freqs = theta ** (-(jnp.arange(half, dtype=jnp.float32) * 2.0) / width)
    angles = positions.astype(jnp.float32)[:, None] * freqs[None, :]
    cosine = jnp.concatenate([jnp.cos(angles), jnp.cos(angles)], axis=-1)
    sine = jnp.concatenate([jnp.sin(angles), jnp.sin(angles)], axis=-1)
    return (cosine, sine)


def rotate(v, cosine, sine):
    half = v.shape[-1] // 2
    turned = jnp.concatenate([-v[..., half:], v[..., :half]], axis=-1)
    return v * cosine + turned * sine


def rotate_back(grad, cosine, sine):
    half = grad.shape[-1] // 2
    moved = grad * sine
    return grad * cosine + jnp.concatenate([moved[..., half:], -moved[..., :half]], axis=-1)


def norm_back(grad, value, factor):
    return factor * (
        grad - value * factor * factor * jnp.mean(grad * value, axis=-1, keepdims=True)
    )


def product(left, right):
    return jnp.dot(left, right, preferred_element_type=jnp.float32)


def left_product(left, right):
    return jnp.einsum("rd,rn->dn", left, right, preferred_element_type=jnp.float32)


def right_product(left, right):
    return jnp.einsum("rn,dn->rd", left, right, preferred_element_type=jnp.float32)


def rounded(v):
    return v.astype(jnp.bfloat16)


def split_rows(term, seq_size, batch_size):
    return term.reshape(
        seq_size, batch_size, term.shape[0] // (seq_size * batch_size), term.shape[1]
    )


def fold_sources(piece):
    return jnp.sum(piece, axis=1).reshape(-1, piece.shape[-1])


def body(
    inputs,
    lengths,
    w_query,
    key_weight,
    value_weight,
    w_out,
    w_gate,
    w_up,
    w_down,
    gain_attn,
    gain_ffn,
    gain_query,
    gain_key,
    cotangent,
):
    slice_len, seq_count, width = inputs.shape
    rows = slice_len * seq_count
    head_dim = gain_query.shape[0]
    kv_width = key_weight.shape[1]
    kv_heads = kv_width // head_dim
    q_heads = w_query.shape[1] // head_dim
    sequence_group = q_heads // kv_heads
    scale = head_dim ** (-0.5)
    cycle_size = lax.axis_size("seq")
    batch_size = lax.axis_size("batch")
    positions = lax.axis_index("seq") * slice_len + jnp.arange(slice_len, dtype=jnp.int32)
    cosine, sine = rotary_tables(positions, head_dim)
    cosine = cosine[:, None, None, :]
    sine = sine[:, None, None, :]
    shards = (w_query, key_weight, value_weight, w_out, w_gate, w_up, w_down)
    wq, key_matrix, value_matrix, wo, wg, wu, wd = (
        lax.all_gather(shards[0], ("seq", "batch"), axis=0, tiled=True),
        lax.all_gather(shards[1], ("seq", "batch"), axis=0, tiled=True),
        lax.all_gather(shards[2], ("seq", "batch"), axis=0, tiled=True),
        lax.all_gather(shards[3], ("seq", "batch"), axis=0, tiled=True),
        lax.all_gather(shards[4], ("seq", "batch"), axis=0, tiled=True),
        lax.all_gather(shards[5], ("seq", "batch"), axis=0, tiled=True),
        lax.all_gather(shards[6], ("seq", "batch"), axis=0, tiled=True),
    )
    stream = inputs.reshape(rows, width).astype(jnp.float32)
    factor_one = rms_factor(stream)
    normalized_input = rounded(stream * factor_one * gain_attn)
    query_pre = product(normalized_input, wq).reshape(slice_len, seq_count, q_heads, head_dim)
    key_before_rotation = product(normalized_input, key_matrix).reshape(
        slice_len, seq_count, kv_heads, head_dim
    )
    value_b = rounded(product(normalized_input, value_matrix)).reshape(
        slice_len, seq_count, kv_width
    )
    factor_q = rms_factor(query_pre)
    factor_k = rms_factor(key_before_rotation)
    query_b = rounded(rotate(query_pre * factor_q * gain_query, cosine, sine))
    key_b = rounded(rotate(key_before_rotation * factor_k * gain_key, cosine, sine)).reshape(
        slice_len, seq_count, kv_width
    )
    query_five = query_b.reshape(slice_len, seq_count, kv_heads, sequence_group, head_dim)

    def scores_of(keys, start):
        count = keys.shape[0]
        raw = (
            jnp.einsum(
                "tsgrd,csgd->sgrtc",
                query_five,
                keys.reshape(count, seq_count, kv_heads, head_dim),
                preferred_element_type=jnp.float32,
            )
            * scale
        )
        key_pos = start + jnp.arange(count, dtype=jnp.int32)
        causal = key_pos[None, :] <= positions[:, None]
        inside = key_pos[None, :] < lengths[:, None]
        valid = causal[None, :, :] & inside[:, None, :]
        return (raw, valid[:, None, None, :, :])

    state_shape = (seq_count, kv_heads, sequence_group, slice_len)
    shard_ids = jnp.arange(cycle_size, dtype=jnp.int32)
    top = jnp.full(state_shape, -1e30, jnp.float32)
    keys = lax.all_gather(key_b, "seq", axis=0, tiled=True)
    value_rows = lax.all_gather(value_b, "seq", axis=0, tiled=True)
    count = keys.shape[0]
    raw, valid = scores_of(keys, jnp.int32(0))
    masked = jnp.where(valid, raw, -jnp.inf)
    new_top = jnp.maximum(top, jnp.max(masked, axis=-1))
    probs = jnp.exp(masked - new_top[..., None])
    total = jnp.sum(probs, axis=-1)
    acc = jnp.einsum(
        "sgrtc,csgd->sgrtd",
        rounded(probs),
        value_rows.reshape(count, seq_count, kv_heads, head_dim),
        preferred_element_type=jnp.float32,
    )
    state = (new_top, total, acc)
    top, total, acc = state
    attn_out = acc / total[..., None]
    log_total = top + jnp.log(total)
    mixed_b = rounded(jnp.transpose(attn_out, (3, 0, 1, 2, 4)).reshape(rows, q_heads * head_dim))
    middle = stream + product(mixed_b, wo)
    factor_two = rms_factor(middle)
    normed_two = rounded(middle * factor_two * gain_ffn)
    gate = product(normed_two, wg)
    up_part = product(normed_two, wu)
    sigma = jax.nn.sigmoid(gate)
    swish = gate * sigma
    hidden_b = rounded(swish * up_part)
    result = middle + product(hidden_b, wd)
    output = rounded(result).reshape(slice_len, seq_count, width)
    wq, key_matrix, value_matrix, wo, wg, wu, wd = (
        lax.all_gather(shards[0], ("seq", "batch"), axis=0, tiled=True),
        lax.all_gather(shards[1], ("seq", "batch"), axis=0, tiled=True),
        lax.all_gather(shards[2], ("seq", "batch"), axis=0, tiled=True),
        lax.all_gather(shards[3], ("seq", "batch"), axis=0, tiled=True),
        lax.all_gather(shards[4], ("seq", "batch"), axis=0, tiled=True),
        lax.all_gather(shards[5], ("seq", "batch"), axis=0, tiled=True),
        lax.all_gather(shards[6], ("seq", "batch"), axis=0, tiled=True),
    )
    grad_res = cotangent.reshape(rows, width).astype(jnp.float32)
    grad_ffo = rounded(grad_res)
    grad_wd = left_product(hidden_b, grad_ffo)
    grad_hidden = right_product(grad_ffo, wd)
    grad_gate = rounded(grad_hidden * up_part * sigma * (1.0 + gate * (1.0 - sigma)))
    grad_up = rounded(grad_hidden * swish)
    grad_wg = left_product(normed_two, grad_gate)
    grad_wu = left_product(normed_two, grad_up)
    grad_normed_two = right_product(grad_gate, wg) + right_product(grad_up, wu)
    grad_gain_ffn = jnp.sum(grad_normed_two * middle * factor_two, axis=0)
    grad_middle = grad_res + norm_back(grad_normed_two * gain_ffn, middle, factor_two)
    grad_branch = rounded(grad_middle)
    grad_wo = left_product(mixed_b, grad_branch)
    grad_mixed = rounded(right_product(grad_branch, wo))
    grad_five = grad_mixed.reshape(slice_len, seq_count, kv_heads, sequence_group, head_dim)
    delta = jnp.sum(
        jnp.transpose(grad_five, (1, 2, 3, 0, 4)).astype(jnp.float32) * attn_out, axis=-1
    )
    gathered = (
        lax.all_gather(key_b, "seq", axis=0, tiled=True),
        lax.all_gather(value_b, "seq", axis=0, tiled=True),
    )

    def back_step(grad_query, item):
        index, keys, value_rows = item
        raw, valid = scores_of(keys, index * slice_len)
        probs = jnp.where(valid, jnp.exp(raw - log_total[..., None]), 0.0)
        key_four = keys.reshape(slice_len, seq_count, kv_heads, head_dim)
        value_four = value_rows.reshape(slice_len, seq_count, kv_heads, head_dim)
        grad_probs = jnp.einsum(
            "tsgrd,csgd->sgrtc", grad_five, value_four, preferred_element_type=jnp.float32
        )
        grad_score = rounded(probs * (grad_probs - delta[..., None]))
        grad_query = (
            grad_query
            + jnp.einsum(
                "sgrtc,csgd->tsgrd", grad_score, key_four, preferred_element_type=jnp.float32
            )
            * scale
        )
        key_term = (
            jnp.einsum(
                "sgrtc,tsgrd->csgd", grad_score, query_five, preferred_element_type=jnp.float32
            )
            * scale
        )
        value_term = jnp.einsum(
            "sgrtc,tsgrd->csgd", rounded(probs), grad_five, preferred_element_type=jnp.float32
        )
        return (
            grad_query,
            (
                key_term.reshape(slice_len, seq_count, kv_width),
                value_term.reshape(slice_len, seq_count, kv_width),
            ),
        )

    items = (
        shard_ids,
        gathered[0].reshape(cycle_size, slice_len, seq_count, kv_width),
        gathered[1].reshape(cycle_size, slice_len, seq_count, kv_width),
    )
    grad_query, terms = lax.scan(
        back_step,
        jnp.zeros((slice_len, seq_count, kv_heads, sequence_group, head_dim), jnp.float32),
        items,
    )
    key_terms = terms[0].reshape(cycle_size * slice_len, seq_count, kv_width)
    value_terms = terms[1].reshape(cycle_size * slice_len, seq_count, kv_width)
    grad_key, grad_value = (
        lax.psum_scatter(
            key_terms.astype(jnp.bfloat16), "seq", scatter_dimension=0, tiled=True
        ).astype(jnp.float32),
        lax.psum_scatter(
            value_terms.astype(jnp.bfloat16), "seq", scatter_dimension=0, tiled=True
        ).astype(jnp.float32),
    )
    grad_qr = (
        rounded(grad_query).astype(jnp.float32).reshape(slice_len, seq_count, q_heads, head_dim)
    )
    grad_qn = rotate_back(grad_qr, cosine, sine)
    grad_gain_query = jnp.sum(grad_qn * query_pre * factor_q, axis=(0, 1, 2))
    grad_qp = rounded(
        norm_back(grad_qn * gain_query, query_pre, factor_q).reshape(rows, q_heads * head_dim)
    )
    grad_kr = (
        rounded(grad_key).astype(jnp.float32).reshape(slice_len, seq_count, kv_heads, head_dim)
    )
    grad_kn = rotate_back(grad_kr, cosine, sine)
    grad_gain_key = jnp.sum(grad_kn * key_before_rotation * factor_k, axis=(0, 1, 2))
    grad_kp = rounded(
        norm_back(grad_kn * gain_key, key_before_rotation, factor_k).reshape(rows, kv_width)
    )
    grad_vp = rounded(grad_value).reshape(rows, kv_width)
    grad_wq = left_product(normalized_input, grad_qp)
    grad_wk = left_product(normalized_input, grad_kp)
    grad_wv = left_product(normalized_input, grad_vp)
    grad_normed = (
        right_product(grad_qp, wq)
        + right_product(grad_kp, key_matrix)
        + right_product(grad_vp, value_matrix)
    )
    grad_gain_attn = jnp.sum(grad_normed * stream * factor_one, axis=0)
    grad_stream = grad_middle + norm_back(grad_normed * gain_attn, stream, factor_one)
    spread = (
        lax.all_to_all(
            split_rows(grad_wq, cycle_size, batch_size).astype(jnp.bfloat16),
            "batch",
            split_axis=1,
            concat_axis=1,
            tiled=True,
        ).astype(jnp.float32),
        lax.all_to_all(
            split_rows(grad_wk, cycle_size, batch_size).astype(jnp.bfloat16),
            "batch",
            split_axis=1,
            concat_axis=1,
            tiled=True,
        ).astype(jnp.float32),
        lax.all_to_all(
            split_rows(grad_wv, cycle_size, batch_size).astype(jnp.bfloat16),
            "batch",
            split_axis=1,
            concat_axis=1,
            tiled=True,
        ).astype(jnp.float32),
        lax.all_to_all(
            split_rows(grad_wo, cycle_size, batch_size).astype(jnp.bfloat16),
            "batch",
            split_axis=1,
            concat_axis=1,
            tiled=True,
        ).astype(jnp.float32),
        lax.all_to_all(
            split_rows(grad_wg, cycle_size, batch_size).astype(jnp.bfloat16),
            "batch",
            split_axis=1,
            concat_axis=1,
            tiled=True,
        ).astype(jnp.float32),
        lax.all_to_all(
            split_rows(grad_wu, cycle_size, batch_size).astype(jnp.bfloat16),
            "batch",
            split_axis=1,
            concat_axis=1,
            tiled=True,
        ).astype(jnp.float32),
        lax.all_to_all(
            split_rows(grad_wd, cycle_size, batch_size).astype(jnp.bfloat16),
            "batch",
            split_axis=1,
            concat_axis=1,
            tiled=True,
        ).astype(jnp.float32),
    )
    partial_sums = [fold_sources(piece) for piece in spread]
    summed = (
        lax.psum_scatter(
            partial_sums[0].astype(jnp.bfloat16), "seq", scatter_dimension=0, tiled=True
        ).astype(jnp.float32),
        lax.psum_scatter(
            partial_sums[1].astype(jnp.bfloat16), "seq", scatter_dimension=0, tiled=True
        ).astype(jnp.float32),
        lax.psum_scatter(
            partial_sums[2].astype(jnp.bfloat16), "seq", scatter_dimension=0, tiled=True
        ).astype(jnp.float32),
        lax.psum_scatter(
            partial_sums[3].astype(jnp.bfloat16), "seq", scatter_dimension=0, tiled=True
        ).astype(jnp.float32),
        lax.psum_scatter(
            partial_sums[4].astype(jnp.bfloat16), "seq", scatter_dimension=0, tiled=True
        ).astype(jnp.float32),
        lax.psum_scatter(
            partial_sums[5].astype(jnp.bfloat16), "seq", scatter_dimension=0, tiled=True
        ).astype(jnp.float32),
        lax.psum_scatter(
            partial_sums[6].astype(jnp.bfloat16), "seq", scatter_dimension=0, tiled=True
        ).astype(jnp.float32),
    )
    gains = lax.psum(
        (grad_gain_attn, grad_gain_ffn, grad_gain_query, grad_gain_key), ("seq", "batch")
    )
    grad_inputs = rounded(grad_stream).reshape(slice_len, seq_count, width)
    return (
        output,
        grad_inputs,
        summed[0],
        summed[1],
        summed[2],
        summed[3],
        summed[4],
        summed[5],
        summed[6],
        gains[0],
        gains[1],
        gains[2],
        gains[3],
    )


def solution(mesh):
    in_specs = (
        P("seq", "batch", None),
        P("batch"),
        P(("seq", "batch"), None),
        P(("seq", "batch"), None),
        P(("seq", "batch"), None),
        P(("seq", "batch"), None),
        P(("seq", "batch"), None),
        P(("seq", "batch"), None),
        P(("seq", "batch"), None),
        P(),
        P(),
        P(),
        P(),
        P("seq", "batch", None),
    )
    out_specs = (
        P("seq", "batch", None),
        P("seq", "batch", None),
        P(("seq", "batch"), None),
        P(("seq", "batch"), None),
        P(("seq", "batch"), None),
        P(("seq", "batch"), None),
        P(("seq", "batch"), None),
        P(("seq", "batch"), None),
        P(("seq", "batch"), None),
        P(),
        P(),
        P(),
        P(),
    )
    return jax.shard_map(body, mesh=mesh, in_specs=in_specs, out_specs=out_specs, check_vma=False)
```

profile of v0, /device:TPU:0, one launch (start us, length us, event | category | flops | bytes accessed | tf_op | source)
XLA Modules:
  0.0 1556.2 jit_solution(3603239281187603089)
XLA Ops:
  12.8 54.5 %all-gather.12.cloned.1.call-done = bf16[1024,512]{1,0:T(8,128)(2,1)} async-done(((bf16[32,512]{1,0:T(8,128)(2,1)}), bf16[1024,512]{1,0:T(8,128)(2,1)}) %all-gather.12.cloned.1.call-update) | async-done | bytes 1048592 | tf_op jit(solution)/shard_map/all_gather | solution.py:100
  74.9 47.9 %all-gather.16.cloned.1.call-done = bf16[1024,512]{1,0:T(8,128)(2,1)} async-done(((bf16[32,512]{1,0:T(8,128)(2,1)}), bf16[1024,512]{1,0:T(8,128)(2,1)}) %all-gather.16.cloned.1.call-update) | async-done | bytes 1048592 | tf_op jit(solution)/shard_map/all_gather | solution.py:101
  130.2 50.8 %all-gather.14.cloned.1.call-done = bf16[1024,1024]{1,0:T(8,128)(2,1)} async-done(((bf16[32,1024]{1,0:T(8,128)(2,1)}), bf16[1024,1024]{1,0:T(8,128)(2,1)}) %all-gather.14.cloned.1.call-update) | async-done | bytes 2097168 | tf_op jit(solution)/shard_map/all_gather | solution.py:99
  185.5 45.7 %all-gather.26.cloned.1.call-done = bf16[2048,512]{1,0:T(8,128)(2,1)} async-done(((bf16[256,512]{1,0:T(8,128)(2,1)}), bf16[2048,512]{1,0:T(8,128)(2,1)}) %all-gather.26.cloned.1.call-update) | async-done | bytes 2097168 | tf_op jit(solution)/shard_map/all_gather | solution.py:145
  235.3 45.7 %all-gather.28.cloned.1.call-done = bf16[2048,512]{1,0:T(8,128)(2,1)} async-done(((bf16[256,512]{1,0:T(8,128)(2,1)}), bf16[2048,512]{1,0:T(8,128)(2,1)}) %all-gather.28.cloned.1.call-update) | async-done | bytes 2097168 | tf_op jit(solution)/shard_map/all_gather | solution.py:146
  285.0 15.2 fusion.39
  300.2 14.5 fusion.37
  314.7 15.6 %bitcast_convert_fusion = (bf16[1,8,2,256,64]{3,4,2,1,0:T(8,128)(2,1)S(1)}, f32[8,2,256,64]{2,3,1,0:T(8,128)}) fusion(f32[8,2,256]{2,1,0:T(2,128)S(1)} %fusion.37, bf16[2048,8,64,1]{0,2,3,1:T(8,128)(2,1)S(1)} %bitcast.386, f32[8,2048,256,2]{2,1,3,0:T(8,128)} %get-tuple-element.240, f32[8,2,256]{2,1,0:T(2,128)S(1)} %broadcast_maximum_fusion, ...), kind=kOutput, calls=%fused_computation.104 | convolution fusion | flops 1107820544 | bytes 37781504 | tf_op jit(solution)/shard_map/sgrtc,csgd->sgrtd/dot_general | solution.py:153
  341.2 81.2 %all-gather.20.cloned.1.call-done = bf16[1024,4608]{1,0:T(8,128)(2,1)} async-done(((bf16[32,4608]{1,0:T(8,128)(2,1)}), bf16[1024,4608]{1,0:T(8,128)(2,1)}) %all-gather.20.cloned.1.call-update) | async-done | bytes 9437200 | tf_op jit(solution)/shard_map/all_gather | solution.py:103
  430.7 75.3 %all-gather.22.cloned.1.call-done = bf16[1024,4608]{1,0:T(8,128)(2,1)} async-done(((bf16[32,4608]{1,0:T(8,128)(2,1)}), bf16[1024,4608]{1,0:T(8,128)(2,1)}) %all-gather.22.cloned.1.call-update) | async-done | bytes 9437200 | tf_op jit(solution)/shard_map/all_gather | solution.py:104
  516.7 72.9 %all-gather.24.cloned.1.call-done = bf16[4608,1024]{1,0:T(8,128)(2,1)} async-done(((bf16[144,1024]{1,0:T(8,128)(2,1)}), bf16[4608,1024]{1,0:T(8,128)(2,1)}) %all-gather.24.cloned.1.call-update) | async-done | bytes 9437200 | tf_op jit(solution)/shard_map/all_gather | solution.py:105
  589.6 12.2 multiply_convert_fusion
  617.8 126.2 %while.15 = (s32[]{:T(128)}, f32[256,1,8,2,64]{0,4,3,2,1:T(8,128)}, bf16[8,256,1,512]{1,3,2,0:T(8,128)(2,1)}, bf16[8,256,1,512]{3,1,0,2:T(8,128)(2,1)}, bf16[8,2...) while((s32[]{:T(128)}, f32[256,1,8,2,64]{0,4,3,2,1:T(8,128)}, ...), condition=%wide.region_9.10_spmd.clone, body=%wide.region_8.9_spmd.clone.sunk | while | flops 682755072 | bytes 45077236 | solution.py:245
  772.4 42.0 %reduce-scatter.10.cloned.1.call-done = bf16[256,1,512]{2,0,1:T(8,128)(2,1)} async-done(((bf16[2048,1,512]{2,0,1:T(8,128)(2,1)}), bf16[256,1,512]{2,0,1:T(8,128)(2,1)}) %reduce-scatter.10.cloned.1.call-update) | async-done | bytes 262160 | tf_op jit(solution)/shard_map/reduce_scatter | solution.py:253
  823.3 61.6 %reduce-scatter.12.cloned.1.call-done = bf16[256,1,512]{2,0,1:T(8,128)(2,1)} async-done(((bf16[2048,1,512]{2,0,1:T(8,128)(2,1)}), bf16[256,1,512]{2,0,1:T(8,128)(2,1)}) %reduce-scatter.12.cloned.1.call-update) | async-done | bytes 262160 | tf_op jit(solution)/shard_map/reduce_scatter | solution.py:256
  895.5 13.0 all-to-all-done.1
  914.3 12.1 all-to-all-done.2
  977.5 89.4 %all-to-all-done.4 = bf16[8,4,32,4608]{3,2,0,1:T(8,128)(2,1)} async-done(((bf16[8,4,32,4608]{3,2,0,1:T(8,128)(2,1)}), bf16[8,4,32,4608]{3,2,0,1:T(8,128)(2,1)}, u32[]{:S(2)}, u32[]{:S(2)}) %all-to-all-start.4) | async-done | bytes 9437216 | tf_op jit(solution)/shard_map/all_to_all | solution.py:316
  1107.8 69.3 %all-to-all-done.5 = bf16[8,4,32,4608]{3,2,0,1:T(8,128)(2,1)} async-done(((bf16[8,4,32,4608]{3,2,0,1:T(8,128)(2,1)}), bf16[8,4,32,4608]{3,2,0,1:T(8,128)(2,1)}, u32[]{:S(2)}, u32[]{:S(2)}) %all-to-all-start.5) | async-done | bytes 9437216 | tf_op jit(solution)/shard_map/all_to_all | solution.py:323
  1190.3 97.0 %all-to-all-done.6 = bf16[8,4,144,1024]{3,2,0,1:T(8,128)(2,1)} async-done(((bf16[8,4,144,1024]{3,2,0,1:T(8,128)(2,1)}), bf16[8,4,144,1024]{3,2,0,1:T(8,128)(2,1)}, u32[]{:S(2)}, u32[]{:S(2)}) %all-to-all-start.6) | async-done | bytes 9437216 | tf_op jit(solution)/shard_map/all_to_all | solution.py:330
  1307.9 38.8 %all-reduce = (f32[1024]{0:T(1024)}, f32[1024]{0:T(1024)}, f32[64]{0:T(128)}, f32[64]{0:T(128)}) all-reduce(f32[1024]{0:T(1024)S(1)} %get-tuple-element.184, f32[1024]{0:T(1024)S(1)} %copy-done.49, f32[64]{0:T(128)S(1)} %reduce_sum.248, f32[64]{0:T(128)S(1)} %reduce_sum.251), channel_id=1, replica_groups=mesh['seq'=8,'batch'=4] {'seq','batch'}, use_global_device_ids=true, to_apply=%region_30.31 | all-reduce | flops 2176 | bytes 17408 | tf_op jit(solution)/shard_map/psum | solution.py:362
  1352.2 52.1 %reduce-scatter.22.cloned.1.call-done = bf16[32,4608]{1,0:T(8,128)(2,1)} async-done(((bf16[256,4608]{1,0:T(8,128)(2,1)}), bf16[32,4608]{1,0:T(8,128)(2,1)}) %reduce-scatter.22.cloned.1.call-update) | async-done | bytes 294928 | tf_op jit(solution)/shard_map/reduce_scatter | solution.py:352
  1406.1 69.6 %reduce-scatter.24.cloned.1.call-done = bf16[32,4608]{1,0:T(8,128)(2,1)} async-done(((bf16[256,4608]{1,0:T(8,128)(2,1)}), bf16[32,4608]{1,0:T(8,128)(2,1)}) %reduce-scatter.24.cloned.1.call-update) | async-done | bytes 294928 | tf_op jit(solution)/shard_map/reduce_scatter | solution.py:355
  1477.6 69.5 %reduce-scatter.26.cloned.1.call-done = bf16[144,1024]{1,0:T(8,128)(2,1)} async-done(((bf16[1152,1024]{1,0:T(8,128)(2,1)}), bf16[144,1024]{1,0:T(8,128)(2,1)}) %reduce-scatter.26.cloned.1.call-update) | async-done | bytes 294928 | tf_op jit(solution)/shard_map/reduce_scatter | solution.py:358
  (416 shorter events, 387.3 us)
Async XLA Ops:
  7.2 60.1 %all-gather.12.cloned.1.call-start = ((), (), s32[]{:S(2)}) async-start(), calls=%async_computation.16 | async-start | bytes 1081344 | tf_op jit(solution)/shard_map/all_gather | solution.py:100
  7.9 114.9 %all-gather.16.cloned.1.call-start = ((), (), s32[]{:S(2)}) async-start(), calls=%async_computation.18 | async-start | bytes 1081344 | tf_op jit(solution)/shard_map/all_gather | solution.py:101
  8.7 172.4 %all-gather.14.cloned.1.call-start = ((), (), s32[]{:S(2)}) async-start(), calls=%async_computation.17 | async-start | bytes 2162688 | tf_op jit(solution)/shard_map/all_gather | solution.py:99
  9.4 221.8 %all-gather.26.cloned.1.call-start = ((), (), s32[]{:S(2)}) async-start(), calls=%async_computation.32 | async-start | bytes 2359296 | tf_op jit(solution)/shard_map/all_gather | solution.py:145
  74.9 206.1 %all-gather.28.cloned.1.call-start = ((), (), s32[]{:S(2)}) async-start(), calls=%async_computation.33 | async-start | bytes 2359296 | tf_op jit(solution)/shard_map/all_gather | solution.py:146
  125.3 213.3 %all-gather.18.cloned.1.call-start = ((), (), s32[]{:S(2)}) async-start(), calls=%async_computation.19 | async-start | bytes 2162688 | tf_op jit(solution)/shard_map/all_gather | solution.py:102
  125.8 296.6 %all-gather.20.cloned.1.call-start = ((), (), s32[]{:S(2)}) async-start(), calls=%async_computation.20 | async-start | bytes 9732096 | tf_op jit(solution)/shard_map/all_gather | solution.py:103
  126.6 379.4 %all-gather.22.cloned.1.call-start = ((), (), s32[]{:S(2)}) async-start(), calls=%async_computation.21 | async-start | bytes 9732096 | tf_op jit(solution)/shard_map/all_gather | solution.py:104
  127.3 462.2 %all-gather.24.cloned.1.call-start = ((), (), s32[]{:S(2)}) async-start(), calls=%async_computation.22 | async-start | bytes 9732096 | tf_op jit(solution)/shard_map/all_gather | solution.py:105
  128.1 686.3 %reduce-scatter.10.cloned.1.call-start = ((), (), s32[]{:S(2)}) async-start(), calls=%async_computation.23 | async-start | bytes 2359296 | tf_op jit(solution)/shard_map/reduce_scatter | solution.py:253
  747.9 137.0 %reduce-scatter.12.cloned.1.call-start = ((), (), s32[]{:S(2)}) async-start(), calls=%async_computation.24 | async-start | bytes 2359296 | tf_op jit(solution)/shard_map/reduce_scatter | solution.py:256
  761.8 127.5 %all-to-all-start.3 = ((bf16[8,4,32,1024]{3,2,0,1:T(8,128)(2,1)}), bf16[8,4,32,1024]{3,2,0,1:T(8,128)(2,1)}, u32[]{:S(2)}, u32[]{:S(2)}) async-start(bf16[8,4,32,1024]{3,2,0,1:T(8,128)(2,1)} %copy.173), calls=%async_computation.8 | async-start | bytes 4194304 | tf_op jit(solution)/shard_map/all_to_all | solution.py:309
  889.4 19.1 %all-to-all-start.1 = ((bf16[8,4,32,512]{3,2,0,1:T(8,128)(2,1)}), bf16[8,4,32,512]{3,2,0,1:T(8,128)(2,1)}, u32[]{:S(2)}, u32[]{:S(2)}) async-start(bf16[8,4,32,512]{3,2,0,1:T(8,128)(2,1)} %copy.171), calls=%async_computation.4 | async-start | bytes 2097152 | tf_op jit(solution)/shard_map/all_to_all | solution.py:295
  926.4 30.2 %all-to-all-start = ((bf16[8,4,32,1024]{3,2,0,1:T(8,128)(2,1)}), bf16[8,4,32,1024]{3,2,0,1:T(8,128)(2,1)}, u32[]{:S(2)}, u32[]{:S(2)}) async-start(bf16[8,4,32,1024]{3,2,0,1:T(8,128)(2,1)} %copy.170), calls=%async_computation.2 | async-start | bytes 4194304 | tf_op jit(solution)/shard_map/all_to_all | solution.py:288
  956.7 110.2 %all-to-all-start.4 = ((bf16[8,4,32,4608]{3,2,0,1:T(8,128)(2,1)}), bf16[8,4,32,4608]{3,2,0,1:T(8,128)(2,1)}, u32[]{:S(2)}, u32[]{:S(2)}) async-start(bf16[8,4,32,4608]{3,2,0,1:T(8,128)(2,1)} %copy.174), calls=%async_computation.10 | async-start | bytes 18874368 | tf_op jit(solution)/shard_map/all_to_all | solution.py:316
  1066.9 110.2 %all-to-all-start.5 = ((bf16[8,4,32,4608]{3,2,0,1:T(8,128)(2,1)}), bf16[8,4,32,4608]{3,2,0,1:T(8,128)(2,1)}, u32[]{:S(2)}, u32[]{:S(2)}) async-start(bf16[8,4,32,4608]{3,2,0,1:T(8,128)(2,1)} %copy.175), calls=%async_computation.12 | async-start | bytes 18874368 | tf_op jit(solution)/shard_map/all_to_all | solution.py:323
  1072.7 233.6 %reduce-scatter.20.cloned.1.call-start = ((), (), s32[]{:S(2)}) async-start(), calls=%async_computation.28 | async-start | bytes 589824 | tf_op jit(solution)/shard_map/reduce_scatter | solution.py:349
  1075.7 272.2 %reduce-scatter.16.cloned.1.call-start = ((), (), s32[]{:S(2)}) async-start(), calls=%async_computation.26 | async-start | bytes 294912 | tf_op jit(solution)/shard_map/reduce_scatter | solution.py:343
  1078.0 271.3 %reduce-scatter.18.cloned.1.call-start = ((), (), s32[]{:S(2)}) async-start(), calls=%async_computation.27 | async-start | bytes 294912 | tf_op jit(solution)/shard_map/reduce_scatter | solution.py:346
  1079.0 271.7 %reduce-scatter.14.cloned.1.call-start = ((), (), s32[]{:S(2)}) async-start(), calls=%async_computation.25 | async-start | bytes 589824 | tf_op jit(solution)/shard_map/reduce_scatter | solution.py:340
  1082.0 322.4 %reduce-scatter.22.cloned.1.call-start = ((), (), s32[]{:S(2)}) async-start(), calls=%async_computation.29 | async-start | bytes 2654208 | tf_op jit(solution)/shard_map/reduce_scatter | solution.py:352
  1177.1 110.2 %all-to-all-start.6 = ((bf16[8,4,144,1024]{3,2,0,1:T(8,128)(2,1)}), bf16[8,4,144,1024]{3,2,0,1:T(8,128)(2,1)}, u32[]{:S(2)}, u32[]{:S(2)}) async-start(bf16[8,4,144,1024]{3,2,0,1:T(8,128)(2,1)} %copy.177), calls=%async_computation.14 | async-start | bytes 18874368 | tf_op jit(solution)/shard_map/all_to_all | solution.py:330
  1182.9 292.9 %reduce-scatter.24.cloned.1.call-start = ((), (), s32[]{:S(2)}) async-start(), calls=%async_computation.30 | async-start | bytes 2654208 | tf_op jit(solution)/shard_map/reduce_scatter | solution.py:355
  1190.3 356.8 %reduce-scatter.26.cloned.1.call-start = ((), (), s32[]{:S(2)}) async-start(), calls=%async_computation.31 | async-start | bytes 2654208 | tf_op jit(solution)/shard_map/reduce_scatter | solution.py:358
  (59 other events, 2163.0 us)
Sparse Core Ops, SparseCore 0:
  10.9 56.3 all-gather.11
  70.2 52.6 all-gather.15
  125.7 55.3 all-gather.13
  183.0 48.1 all-gather.25
  233.2 47.7 all-gather.27
  283.7 54.8 all-gather.17
  341.5 80.8 all-gather.19
  425.3 80.6 all-gather.21
  508.9 80.6 all-gather.23
  748.0 66.2 reduce-scatter.9
  817.9 66.9 reduce-scatter.11
  1077.2 61.3 reduce-scatter.19
  1142.9 60.2 reduce-scatter.15
  1207.3 60.2 reduce-scatter.17
  1271.8 61.0 reduce-scatter.13
  1336.2 68.1 reduce-scatter.21
  1407.7 68.0 reduce-scatter.23
  1479.1 67.9 reduce-scatter.25
where the time goes:
time: 1560 us
  waiting for transfers between devices  1070 us (69%)
  matrix products  200 us (13%)
  local copies, waits for them, and re-layouts  105 us (7%)
  other arithmetic  80.4 us (5%)
  blocking collectives  38.8 us (2%)
  starting transfers between devices  35.3 us (2%)
  between operations  16.4 us (1%)
    all_to_all x1, waiting for transfers between devices, body(): lax.all_to_all(split_rows(grad_wd, cycle_size, batch_size).astype(jnp.bfl...  97 us
    all_to_all x1, waiting for transfers between devices, body(): lax.all_to_all(split_rows(grad_wg, cycle_size, batch_size).astype(jnp.bfl...  89.4 us
    all_gather x1, waiting for transfers between devices, body(): lax.all_gather(shards[4], ('seq', 'batch'), axis=0, tiled=True)  81.2 us
    all_gather x1, waiting for transfers between devices, body(): lax.all_gather(shards[5], ('seq', 'batch'), axis=0, tiled=True)  75.3 us
    all_gather x1, waiting for transfers between devices, body(): lax.all_gather(shards[6], ('seq', 'batch'), axis=0, tiled=True)  72.9 us
    reduce_scatter x1, waiting for transfers between devices, body(): lax.psum_scatter(partial_sums[5].astype(jnp.bfloat16), 'seq', scatter_dim...  69.6 us
    reduce_scatter x1, waiting for transfers between devices, body(): lax.psum_scatter(partial_sums[6].astype(jnp.bfloat16), 'seq', scatter_dim...  69.5 us
    all_to_all x1, waiting for transfers between devices, body(): lax.all_to_all(split_rows(grad_wu, cycle_size, batch_size).astype(jnp.bfl...  69.3 us
  transfers between devices with their start and end apart: 25, of which 20 were waited for; matrix products, arithmetic and copies ran while one was open for 15% of the time, Pallas kernels for 0%

commit v1 on v0

--- a/solution.py
+++ b/solution.py
@@ -1,14 +1,852 @@
+import functools
+
 import jax
 import jax.numpy as jnp
 from jax import lax
+from jax.experimental import pallas as pl
+from jax.experimental.pallas import tpu as pltpu
 from jax.sharding import PartitionSpec as P
 
+MESH = pl.DeviceIdType.MESH
+F32 = jnp.float32
+BF16 = jnp.bfloat16
 eps = 1e-05
 theta = 1000000.0
+VMEM = pl.BlockSpec(memory_space=pltpu.VMEM)
+ANY = pl.BlockSpec(memory_space=pl.ANY)
+
+
+def nn(left, right):
+    return lax.dot_general(left, right, (((1,), (0,)), ((), ())), preferred_element_type=F32)
+
+
+def nt(left, right):
+    return lax.dot_general(left, right, (((1,), (1,)), ((), ())), preferred_element_type=F32)
+
+
+def tn(left, right):
+    return lax.dot_general(left, right, (((0,), (0,)), ((), ())), preferred_element_type=F32)
 
 
 def rms_factor(v):
     return lax.rsqrt(jnp.mean(v * v, axis=-1, keepdims=True) + eps)
+
+
+def norm_back(grad, value, factor):
+    return factor * (
+        grad - value * factor * factor * jnp.mean(grad * value, axis=-1, keepdims=True)
+    )
+
+
+def lanes(shape):
+    return lax.broadcasted_iota(jnp.int32, shape, len(shape) - 1)
+
+
+def rows_of(shape):
+    return lax.broadcasted_iota(jnp.int32, shape, len(shape) - 2)
+
+
+def head_mean(v):
+    first = lanes(v.shape) < 64
+    low = jnp.sum(jnp.where(first, v, 0.0), axis=-1, keepdims=True)
+    high = jnp.sum(jnp.where(first, 0.0, v), axis=-1, keepdims=True)
+    return jnp.where(first, low, high) * (1.0 / 64.0)
+
+
+def rope(u, cosine, sine):
+    early = lax.rem(lanes(u.shape), 64) < 32
+    turned = jnp.where(early, -pltpu.roll(u, 96, 1), pltpu.roll(u, 32, 1))
+    return u * cosine + turned * sine
+
+
+def rope_back(u, cosine, sine):
+    early = lax.rem(lanes(u.shape), 64) < 32
+    w = u * sine
+    return u * cosine + jnp.where(early, pltpu.roll(w, 96, 1), -pltpu.roll(w, 32, 1))
+
+
+class Place:
+    def __init__(self, send_sem, recv_sem, local_sem):
+        self.s = lax.axis_index("seq")
+        self.b = lax.axis_index("batch")
+        self.z = self.s // 2
+        self.y = lax.rem(self.s, 2)
+        self.core = self.b + 1 - 2 * lax.rem(self.b, 2)
+        self.across = lax.rem(self.b + 2, 4)
+        self.far = 3 - self.b
+        self.flip = 2 * self.z + 1 - self.y
+        self.send_sem, self.recv_sem, self.local_sem = send_sem, recv_sem, local_sem
+        self.used = 0
+        self.used_local = 0
+        self.sent = []
+
+    def up(self, k):
+        return lax.rem(self.z + k, 4)
+
+    def down(self, k):
+        return lax.rem(self.z + 4 - k, 4)
+
+    def greet(self):
+        barrier = pltpu.get_barrier_semaphore()
+        for k in (1, 2, 3):
+            pl.semaphore_signal(
+                barrier, inc=1, device_id=(self.s, lax.rem(self.b + k, 4)), device_id_type=MESH
+            )
+        for k in range(1, 8):
+            pl.semaphore_signal(
+                barrier, inc=1, device_id=(lax.rem(self.s + k, 8), self.b), device_id_type=MESH
+            )
+        pl.semaphore_wait(barrier, 10)
+
+    def slots(self, count):
+        first = self.used
+        self.used += count
+        return first
+
+    def copy(self, src, dst, device, out, into=None):
+        return pltpu.make_async_remote_copy(
+            src_ref=src,
+            dst_ref=dst,
+            send_sem=self.send_sem.at[out],
+            recv_sem=self.recv_sem.at[out if into is None else into],
+            device_id=device,
+            device_id_type=MESH,
+        )
+
+    def post(self, src, dst, device):
+        index = self.slots(1)
+        made = self.copy(src, dst, device, index)
+        made.start()
+        self.sent.append(made)
+        return index
+
+    def landed(self, index, ref):
+        self.copy(ref, ref, (self.s, self.core), index).wait_recv()
+
+    def local(self, src, dst):
+        index = self.used_local
+        self.used_local += 1
+        made = pltpu.make_async_copy(src, dst, self.local_sem.at[index])
+        made.start()
+        return made
+
+    def drain(self):
+        for made in self.sent:
+            made.wait_send()
+        self.sent = []
+
+
+def forward_kernel(
+    x, dy, length, wqkv_in, wgu_in, wd_in, wo_in, cos, sin, gain_q, gain_k, gain_a, gain_f,
+    wgu, wd, wo, wqkv, norm, pre, unit, unit_out, lse, mix, norm_two, middle, dy_all, length_all,
+    xa, pack, kv, vt, send_sem, recv_sem, local_sem,
+):
+    p = Place(send_sem, recv_sem, local_sem)
+    s, b, z, y = p.s, p.b, p.z, p.y
+    my_rows = pl.ds(pl.multiple_of(32 * b, 32), 32)
+    own = [
+        p.local(wqkv_in.at[b], wqkv.at[s, my_rows]),
+        p.local(x, xa.at[b]),
+        p.local(length, length_all.at[b]),
+        p.local(wo_in, wo.at[s, b]),
+    ]
+    own_gu = p.local(wgu_in.at[b], wgu.at[s, :, my_rows])
+    own_d = p.local(wd_in, wd.at[s])
+    own_dy = p.local(dy, dy_all.at[b])
+    p.greet()
+
+    got = []
+    for k in (1, 2, 3):
+        to = lax.rem(b + k, 4)
+        got.append(p.post(wqkv_in.at[to], wqkv.at[s, my_rows], (s, to)))
+    x_core = p.post(x, xa.at[b], (s, p.core))
+    x_across = p.post(x, xa.at[b], (s, p.across))
+    got_len = []
+    for k in (1, 2, 3):
+        to = lax.rem(b + k, 4)
+        got_len.append(p.post(length, length_all.at[b], (s, to)))
+    for made in own:
+        made.wait()
+    for k in (1, 2, 3):
+        p.landed(got[k - 1], wqkv.at[s, my_rows])
+    z_qkv = [p.post(wqkv.at[s], wqkv.at[s], (2 * p.up(k) + y, b)) for k in (1, 2, 3)]
+    y_qkv = [p.post(wqkv.at[s], wqkv.at[s], (p.flip, b))]
+    z_wo = [p.post(wo.at[s, b], wo.at[s, b], (2 * p.up(k) + y, b)) for k in (1, 2, 3)]
+    y_wo = [p.post(wo.at[s, b], wo.at[s, b], (p.flip, b))]
+    got_gu = []
+    for k in (1, 2, 3):
+        to = lax.rem(b + k, 4)
+        got_gu.append(p.post(wgu_in.at[to], wgu.at[s, :, my_rows], (s, to)))
+    p.landed(x_across, xa.at[p.across])
+    x_far = p.post(xa.at[p.across], xa.at[p.across], (s, p.core))
+    for k in (1, 2, 3):
+        slot = 2 * p.down(k) + y
+        p.landed(z_qkv[k - 1], wqkv.at[slot])
+        y_qkv.append(p.post(wqkv.at[slot], wqkv.at[slot], (p.flip, b)))
+    p.landed(x_core, xa.at[p.core])
+    p.landed(x_far, xa.at[p.far])
+    for k in (1, 2, 3):
+        p.landed(got_len[k - 1], length_all.at[lax.rem(b + 4 - k, 4)])
+
+    def normalize(g, carry):
+        xg = xa[g].astype(F32)
+        norm[g] = (xg * rms_factor(xg) * gain_a[...]).astype(BF16)
+        return carry
+
+    lax.fori_loop(0, 4, normalize, 0)
+    p.landed(y_qkv[0], wqkv.at[p.flip])
+    for k in (1, 2, 3):
+        p.landed(y_qkv[k], wqkv.at[2 * p.down(k) + 1 - y])
+
+    own_gu.wait()
+    own_d.wait()
+    own_dy.wait()
+    for k in (1, 2, 3):
+        p.landed(got_gu[k - 1], wgu.at[s, :, my_rows])
+    first_ffn = p.used
+    z_gu, z_d = [], []
+    for k in (1, 2, 3):
+        z_gu.append(p.post(wgu.at[s], wgu.at[s], (2 * p.up(k) + y, b)))
+        z_d.append(p.post(wd.at[s], wd.at[s], (2 * p.up(k) + y, b)))
+    y_gu = [p.post(wgu.at[s], wgu.at[s], (p.flip, b))]
+    y_d = [p.post(wd.at[s], wd.at[s], (p.flip, b))]
+
+    first_unit = p.slots(8)
+
+    def project(t, carry):
+        g = lax.rem(z + 1 + t, 4)
+        whole = nn(norm[g], wqkv[...].reshape(1024, 512))
+        pre[g] = whole
+        for kk in (0, 1):
+            q = whole[:, 256 * kk : 256 * kk + 128]
+            kvp = whole[:, 256 * kk + 128 : 256 * kk + 256]
+            qn = q * lax.rsqrt(head_mean(q * q) + eps) * gain_q[...]
+            kn = kvp * lax.rsqrt(head_mean(kvp * kvp) + eps) * gain_k[...]
+            qr = rope(qn, cos[...], sin[...]) * 0.125
+            kr = rope(kn, cos[...], sin[...])
+            pack[2 * g + kk, :, 0:128] = qr.astype(BF16)
+            pack[2 * g + kk, :, 128:256] = jnp.where(lanes(kr.shape) < 64, kr, kvp).astype(BF16)
+
+        @pl.when(t < 3)
+        def _():
+            for kk in (0, 1):
+                to = 2 * g + kk
+                p.copy(
+                    pack.at[to], unit.at[s], (to, b), first_unit + 2 * t + kk, first_unit + 2 * t + y
+                ).start()
+
+        @pl.when(t == 3)
+        def _():
+            p.copy(pack.at[p.flip], unit.at[s], (p.flip, b), first_unit + 6).start()
+
+        return carry
+
+    lax.fori_loop(0, 4, project, 0)
+    own_unit = p.local(pack.at[s], unit.at[s])
+
+    for k in (1, 2, 3):
+        slot = 2 * p.down(k) + y
+        p.landed(z_wo[k - 1], wo.at[slot, b])
+        y_wo.append(p.post(wo.at[slot, b], wo.at[slot, b], (p.flip, b)))
+    dy_core = p.post(dy, dy_all.at[b], (s, p.core))
+    dy_across = p.post(dy, dy_all.at[b], (s, p.across))
+    p.landed(y_wo[0], wo.at[p.flip, b])
+    for k in (1, 2, 3):
+        p.landed(y_wo[k], wo.at[2 * p.down(k) + 1 - y, b])
+    wo_core = p.post(wo.at[:, b], wo.at[:, b], (s, p.core))
+    wo_across = p.post(wo.at[:, b], wo.at[:, b], (s, p.across))
+
+    for t in range(3):
+        for other in (0, 1):
+            src = 2 * lax.rem(z + 3 - t, 4) + other
+            p.landed(first_unit + 2 * t + other, unit.at[src])
+    p.landed(first_unit + 6, unit.at[p.flip])
+    own_unit.wait()
+    for t in range(3):
+        for kk in (0, 1):
+            p.copy(pack.at[s], unit.at[s], (p.flip, b), first_unit + 2 * t + kk).wait_send()
+    p.copy(pack.at[s], unit.at[s], (p.flip, b), first_unit + 6).wait_send()
+
+    def prepare(j, carry):
+        live = j * 256 + rows_of((256, 128)) < length_all[z][0:1, :]
+        masked = jnp.where(live, unit[j, :, 128:256].astype(F32), 0.0)
+        kv[j] = masked.astype(BF16)
+        vt[j, 0:64] = jnp.transpose(masked)[64:128].astype(BF16)
+        alive = j * 256 + lanes((16, 256)) < length_all[z][0:1, 0:1]
+        vt[j, 64:80] = jnp.where(alive, 1.0, 0.0).astype(BF16)
+        return carry
+
+    lax.fori_loop(0, 8, prepare, 0)
+    p.landed(wo_across, wo.at[:, p.across])
+    wo_far = p.post(wo.at[:, p.across], wo.at[:, p.across], (s, p.core))
+    p.landed(dy_across, dy_all.at[p.across])
+    dy_far = p.post(dy_all.at[p.across], dy_all.at[p.across], (s, p.core))
+    first_mix = p.slots(8)
+
+    def attend(t, carry):
+        i = lax.rem(s + 1 + t, 8)
+        qt = jnp.transpose(unit[i, :, 0:128].astype(F32)).astype(BF16)
+        both = jnp.concatenate([qt[0:64], qt[64:128]], axis=1)
+        right = jnp.concatenate([both, jnp.zeros((64, 512), BF16)], axis=0)
+
+        def block(j, acc):
+            return acc + nn(vt[j], jnp.exp(nn(kv[j], right)).astype(BF16))
+
+        acc = lax.fori_loop(0, i, block, jnp.zeros((80, 512), F32))
+        causal = rows_of((256, 512)) <= lax.rem(lanes((256, 512)), 256)
+        edge = jnp.where(causal, jnp.exp(nn(kv[i], right)), 0.0).astype(BF16)
+        acc = acc + nn(vt[i], edge)
+        total = acc[64:65]
+        out = acc[0:64] / total
+        out = jnp.concatenate([out[:, 0:256], out[:, 256:512]], axis=0)
+        unit_out[i] = jnp.transpose(out).astype(BF16)
+        lse[i] = jnp.broadcast_to(jnp.log(total), (8, 512))
+
+        @pl.when(t < 7)
+        def _():
+            p.copy(unit_out.at[i], mix.at[b, s], (i, b), first_mix + t).start()
+
+        return carry
+
+    lax.fori_loop(0, 8, attend, 0)
+    own_mix = p.local(unit_out.at[s], mix.at[b, s])
+    for k in (1, 2, 3):
+        slot = 2 * p.down(k) + y
+        p.landed(z_gu[k - 1], wgu.at[slot])
+        p.landed(z_d[k - 1], wd.at[slot])
+        y_gu.append(p.post(wgu.at[slot], wgu.at[slot], (p.flip, b)))
+        y_d.append(p.post(wd.at[slot], wd.at[slot], (p.flip, b)))
+    for t in range(7):
+        p.landed(first_mix + t, mix.at[b, lax.rem(s + 7 - t, 8)])
+        p.copy(unit_out.at[s], mix.at[b, s], (p.flip, b), first_mix + t).wait_send()
+    own_mix.wait()
+    mix_across = p.post(mix.at[b], mix.at[b], (s, p.across))
+    mix_core = p.post(mix.at[b], mix.at[b], (s, p.core))
+    p.landed(mix_across, mix.at[p.across])
+    mix_far = p.post(mix.at[p.across], mix.at[p.across], (s, p.core))
+    p.landed(wo_core, wo.at[:, p.core])
+    p.landed(wo_far, wo.at[:, p.far])
+    p.landed(dy_core, dy_all.at[p.core])
+    p.landed(dy_far, dy_all.at[p.far])
+    p.landed(mix_core, mix.at[p.core])
+    p.landed(mix_far, mix.at[p.far])
+
+    def project_out(g, carry):
+        mixed = jnp.concatenate([mix[c, 2 * g + kk] for c in range(4) for kk in (0, 1)], axis=1)
+        mid = xa[g].astype(F32) + nn(mixed, wo[...].reshape(1024, 1024))
+        norm_two[g] = (mid * rms_factor(mid) * gain_f[...]).astype(BF16)
+
+        @pl.when(g == b)
+        def _():
+            middle[...] = mid
+
+        return carry
+
+    lax.fori_loop(0, 4, project_out, 0)
+    p.landed(y_gu[0], wgu.at[p.flip])
+    p.landed(y_d[0], wd.at[p.flip])
+    for k in (1, 2, 3):
+        p.landed(y_gu[k], wgu.at[2 * p.down(k) + 1 - y])
+        p.landed(y_d[k], wd.at[2 * p.down(k) + 1 - y])
+    p.drain()
+
+
+def chip_sum_post(p, t, parts, recv, first):
+    @pl.when(t == 0)
+    def _():
+        p.copy(parts.at[p.far], recv.at[0], (p.s, p.core), first).start()
+
+    @pl.when(t == 1)
+    def _():
+        p.copy(parts.at[p.core], recv.at[1], (p.s, p.core), first + 1).start()
+
+
+def chip_sum_across(p, parts, recv, first):
+    p.copy(recv.at[0], recv.at[0], (p.s, p.core), first).wait_recv()
+    parts[p.across] = (parts[p.across].astype(F32) + recv[0].astype(F32)).astype(BF16)
+    p.copy(parts.at[p.across], recv.at[2], (p.s, p.across), first + 2).start()
+
+
+def chip_sum_rest(p, parts, recv, first):
+    p.copy(recv.at[1], recv.at[1], (p.s, p.core), first + 1).wait_recv()
+    p.copy(recv.at[2], recv.at[2], (p.s, p.core), first + 2).wait_recv()
+    for k in range(3):
+        p.copy(parts.at[p.b], recv.at[k], (p.s, p.core), first + k).wait_send()
+    return recv[1].astype(F32) + recv[2].astype(F32)
+
+
+def batch_order(p, t):
+    return jnp.where(t == 0, p.far, jnp.where(t == 1, p.core, jnp.where(t == 2, p.across, p.b)))
+
+
+def feed_kernel(
+    norm_two, dy_all, wgu, wd, middle,
+    output, dn2, ggu, gd,
+    hid, dgate, dup, parts_n, recv_n, parts_o, recv_o, keep_n, keep_o, send_sem, recv_sem, local_sem,
+):
+    p = Place(send_sem, recv_sem, local_sem)
+    p.greet()
+    first_n, first_o = p.slots(3), p.slots(3)
+
+    def gated(t, carry):
+        g = batch_order(p, t)
+        rows = pl.ds(pl.multiple_of(g * 256, 256), 256)
+        n2 = norm_two[g]
+        gate = nn(n2, wgu[:, 0].reshape(1024, 1152))
+        up = nn(n2, wgu[:, 1].reshape(1024, 1152))
+        dh = nt(dy_all[g], wd[...].reshape(1152, 1024))
+        sg = 1.0 / (1.0 + jnp.exp(-gate))
+        swish = gate * sg
+        hid[rows] = (swish * up).astype(BF16)
+        dg = (dh * up * sg * (1.0 + gate * (1.0 - sg))).astype(BF16)
+        du = (dh * swish).astype(BF16)
+        dgate[rows] = dg
+        dup[rows] = du
+        part = nt(dg, wgu[:, 0].reshape(1024, 1152)) + nt(du, wgu[:, 1].reshape(1024, 1152))
+        parts_n[g] = part.astype(BF16)
+
+        @pl.when(t == 3)
+        def _():
+            keep_n[...] = part
+
+        chip_sum_post(p, t, parts_n, recv_n, first_n)
+        return carry
+
+    lax.fori_loop(0, 4, gated, 0)
+    chip_sum_across(p, parts_n, recv_n, first_n)
+
+    def down(t, carry):
+        g = batch_order(p, t)
+        part = nn(hid[pl.ds(pl.multiple_of(g * 256, 256), 256)], wd[...].reshape(1152, 1024))
+        parts_o[g] = part.astype(BF16)
+
+        @pl.when(t == 3)
+        def _():
+            keep_o[...] = part
+
+        chip_sum_post(p, t, parts_o, recv_o, first_o)
+        return carry
+
+    lax.fori_loop(0, 4, down, 0)
+    chip_sum_across(p, parts_o, recv_o, first_o)
+
+    def down_rows(c, carry):
+        at = pl.multiple_of(128 * c, 128)
+        gd[pl.ds(at, 128)] = tn(hid[:, pl.ds(at, 128)], dy_all[...].reshape(1024, 1024)).astype(BF16)
+        return carry
+
+    lax.fori_loop(0, 9, down_rows, 0)
+
+    def gate_rows(c, carry):
+        at = pl.multiple_of(128 * c, 128)
+        left = norm_two[:, :, pl.ds(at, 128)].reshape(1024, 128)
+        ggu[c, 0] = tn(left, dgate[...]).astype(BF16)
+        ggu[c, 1] = tn(left, dup[...]).astype(BF16)
+        return carry
+
+    lax.fori_loop(0, 8, gate_rows, 0)
+    dn2[...] = keep_n[...] + chip_sum_rest(p, parts_n, recv_n, first_n)
+    total = keep_o[...] + chip_sum_rest(p, parts_o, recv_o, first_o)
+    output[...] = (middle[...] + total).astype(BF16)
+
+
+class SeqSum:
+    def __init__(self, p, y_recv, z_recv):
+        self.p, self.y_recv, self.z_recv = p, y_recv, z_recv
+
+    def start(self, source, mine=None):
+        p = self.p
+        self.index = p.post(source.at[:, 1 - p.y], self.y_recv, (p.flip, p.b))
+        self.load = None
+        if mine is None:
+            self.mine = lambda i: source.at[i, p.y]
+        else:
+            self.load = p.local(source.at[:, p.y], mine)
+            self.mine = lambda i: mine.at[i]
+
+    def middle(self):
+        p = self.p
+        if self.load is not None:
+            self.load.wait()
+        p.landed(self.index, self.y_recv)
+        self.far = []
+        for k in (1, 2, 3):
+            i = p.up(k)
+            self.y_recv[i] = (self.y_recv[i].astype(F32) + self.mine(i)[...].astype(F32)).astype(BF16)
+            self.far.append(p.post(self.y_recv.at[i], self.z_recv.at[k - 1], (2 * i + p.y, p.b)))
+
+    def finish(self):
+        p = self.p
+        total = self.y_recv[p.z].astype(F32) + self.mine(p.z)[...].astype(F32)
+        for k in (1, 2, 3):
+            p.landed(self.far[k - 1], self.z_recv.at[k - 1])
+            total = total + self.z_recv[k - 1].astype(F32)
+        return total
+
+
+def backward_kernel(
+    dn2, middle, x, dy, wo, mix, unit, unit_out, lse, length_all, pre, norm, wqkv,
+    cos, sin, gain_q, gain_k, gain_a, gain_f, ggu, gd,
+    dx, rqkv, rgu, rd, ro, gains_out,
+    dmid, dox, doq, dou, dbr, kv, kt, q_right, do_right, q_left, do_left, delta, dk2, dv2, back, dqr,
+    dpre, parts, recv, keep, gqkv, go, mixt,
+    y_d, m_d, z_d, y_g, m_g, z_g, y_u, m_u, z_u, y_q, z_q, y_o, z_o, fin_g, fin_u, fin_q,
+    gain_sum, gain_batch, gain_seq,
+    send_sem, recv_sem, local_sem,
+):
+    p = Place(send_sem, recv_sem, local_sem)
+    s, b, z, y = p.s, p.b, p.z, p.y
+    p.greet()
+    sum_d, sum_g, sum_u = SeqSum(p, y_d, z_d), SeqSum(p, y_g, z_g), SeqSum(p, y_u, z_u)
+    sum_d.start(gd, m_d)
+    sum_g.start(ggu.at[:, :, 0], m_g)
+    sum_u.start(ggu.at[:, :, 1], m_u)
+
+    mid = middle[...]
+    r2 = rms_factor(mid)
+    grad_two = dn2[...]
+    gain_sum[...] = jnp.zeros((8, 1024), F32)
+    gain_sum[1:2] = jnp.sum(grad_two * mid * r2, axis=0, keepdims=True)
+    dm = dy[...].astype(F32) + norm_back(grad_two * gain_f[...], mid, r2)
+    dmid[...] = dm
+    dbr[b] = dm.astype(BF16)
+    for c in range(4):
+        for kk in (0, 1):
+            h = 2 * c + kk
+            dox[c, kk] = nt(dbr[b], wo[h].reshape(128, 1024)).astype(BF16)
+    got_do = []
+    for k in (1, 2, 3):
+        to = lax.rem(b + k, 4)
+        got_do.append(p.post(dox.at[to], doq.at[pl.ds(2 * b, 2)], (s, to)))
+    doq[pl.ds(2 * b, 2)] = dox[b]
+    dbr_across = p.post(dbr.at[b], dbr.at[b], (s, p.across))
+    dbr_core = p.post(dbr.at[b], dbr.at[b], (s, p.core))
+    for k in (1, 2, 3):
+        p.landed(got_do[k - 1], doq.at[pl.ds(2 * lax.rem(b + 4 - k, 4), 2)])
+    got_unit = []
+    for k in range(1, 8):
+        to = lax.rem(s + k, 8)
+        got_unit.append(p.post(doq.at[to], dou.at[s], (to, b)))
+    dou[s] = doq[s]
+
+    def prepare(i, carry):
+        live = i * 256 + rows_of((256, 128)) < length_all[z][0:1, :]
+        masked = jnp.where(live, unit[i, :, 128:256].astype(F32), 0.0)
+        kv[i] = masked.astype(BF16)
+        kt[i] = jnp.transpose(masked)[0:64].astype(BF16)
+        q = unit[i, :, 0:128].astype(F32)
+        qt = jnp.transpose(q).astype(BF16)
+        q_right[i, 0:64] = jnp.concatenate([qt[0:64], qt[64:128]], axis=1)
+        q_right[i, 64:128] = jnp.zeros((64, 512), BF16)
+        first = lanes(q.shape) < 64
+        q_left[i, 0:256] = jnp.where(first, q, 0.0).astype(BF16)
+        q_left[i, 256:512] = jnp.where(first, 0.0, q).astype(BF16)
+        dk2[i] = jnp.zeros((256, 128), F32)
+        dv2[i] = jnp.zeros((256, 128), F32)
+        return carry
+
+    lax.fori_loop(0, 8, prepare, 0)
+    sum_d.middle()
+    p.landed(dbr_across, dbr.at[p.across])
+    dbr_far = p.post(dbr.at[p.across], dbr.at[p.across], (s, p.core))
+    for k in range(1, 8):
+        p.landed(got_unit[k - 1], dou.at[lax.rem(s + 8 - k, 8)])
+
+    def prepare_grad(i, carry):
+        do = dou[i].astype(F32)
+        dot = jnp.transpose(do)
+        do_right[i, 0:64] = jnp.zeros((64, 512), BF16)
+        do_right[i, 64:128] = jnp.concatenate([dot[0:64], dot[64:128]], axis=1).astype(BF16)
+        first = lanes(do.shape) < 64
+        do_left[i, 0:256] = jnp.where(first, do, 0.0).astype(BF16)
+        do_left[i, 256:512] = jnp.where(first, 0.0, do).astype(BF16)
+        both = dot * jnp.transpose(unit_out[i].astype(F32))
+        low = jnp.sum(both[0:64], axis=0, keepdims=True)
+        high = jnp.sum(both[64:128], axis=0, keepdims=True)
+        delta[i] = jnp.broadcast_to(jnp.concatenate([low, high], axis=1), (8, 512))
+        return carry
+
+    lax.fori_loop(0, 8, prepare_grad, 0)
+
+    def queries(t, carry):
+        i = 7 - t
+        qr, dr, ql, dl = q_right[i], do_right[i], q_left[i], do_left[i]
+        log_total = lse[i][0:1]
+        shift = delta[i][0:1]
+
+        def block(j, probs):
+            ds = (probs * (nn(kv[j], dr) - shift)).astype(BF16)
+            dv2[j] += nn(probs.astype(BF16), dl)
+            dk2[j] += nn(ds, ql)
+            return nn(kt[j], ds)
+
+        def step(j, acc):
+            return acc + block(j, jnp.exp(nn(kv[j], qr) - log_total))
+
+        acc = lax.fori_loop(0, i, step, jnp.zeros((64, 512), F32))
+        causal = rows_of((256, 512)) <= lax.rem(lanes((256, 512)), 256)
+        acc = acc + block(i, jnp.where(causal, jnp.exp(nn(kv[i], qr) - log_total), 0.0))
+        dq = jnp.concatenate([acc[:, 0:256], acc[:, 256:512]], axis=0) * 0.125
+        back[i, :, 0:128] = jnp.transpose(dq).astype(BF16)
+        live = i * 256 + rows_of((256, 128)) < length_all[z][0:1, :]
+        dk, dv = dk2[i], dv2[i]
+        dk = dk + pltpu.roll(dk, 64, 1)
+        dv = dv + pltpu.roll(dv, 64, 1)
+        dkv = jnp.where(lanes((256, 128)) < 64, dk, dv)
+        back[i, :, 128:256] = jnp.where(live, dkv, 0.0).astype(BF16)
+        return carry
+
+    lax.fori_loop(0, 3, queries, 0)
+    sum_g.middle()
+    lax.fori_loop(3, 8, queries, 0)
+    got_back = []
+    for k in range(1, 8):
+        to = lax.rem(s + k, 8)
+        got_back.append(p.post(back.at[to], dqr.at[s], (to, b)))
+    dqr[s] = back[s]
+
+    p.landed(dbr_core, dbr.at[p.core])
+    p.landed(dbr_far, dbr.at[p.far])
+
+    def turn(e, carry):
+        for g in range(4):
+            mixt[:, 256 * g : 256 * g + 256] = jnp.transpose(
+                mix[e // 2, 2 * g + lax.rem(e, 2)].astype(F32)
+            ).astype(BF16)
+        left = mixt[pl.ds(pl.multiple_of(32 * b, 32), 32)]
+        go[e // 2, lax.rem(e, 2)] = nn(left, dbr[...].reshape(1024, 1024)).astype(BF16)
+        return carry
+
+    lax.fori_loop(0, 8, turn, 0)
+    sum_o = SeqSum(p, y_o, z_o)
+    sum_o.start(go)
+    sum_u.middle()
+    for k in range(1, 8):
+        p.landed(got_back[k - 1], dqr.at[lax.rem(s + 8 - k, 8)])
+
+    first_n = p.slots(3)
+    zero_row = jnp.zeros((1, 128), F32)
+
+    def heads(t, carry):
+        sum_q, sum_k = carry
+        g = batch_order(p, t)
+        for kk in (0, 1):
+            at = 256 * kk
+            q, k = pre[g, :, at : at + 128], pre[g, :, at + 128 : at + 256]
+            rq = lax.rsqrt(head_mean(q * q) + eps)
+            rk = lax.rsqrt(head_mean(k * k) + eps)
+            dq = rope_back(dqr[2 * g + kk, :, 0:128].astype(F32), cos[...], sin[...])
+            dkv = dqr[2 * g + kk, :, 128:256].astype(F32)
+            dk = rope_back(dkv, cos[...], sin[...])
+            sum_q = sum_q + jnp.sum(dq * q * rq, axis=0, keepdims=True)
+            sum_k = sum_k + jnp.sum(dk * k * rk, axis=0, keepdims=True)
+            dq = dq * gain_q[...]
+            dk = dk * gain_k[...]
+            dq = rq * (dq - q * rq * rq * head_mean(dq * q))
+            dk = rk * (dk - k * rk * rk * head_mean(dk * k))
+            dpre[g, :, at : at + 128] = dq.astype(BF16)
+            dpre[g, :, at + 128 : at + 256] = jnp.where(lanes(dk.shape) < 64, dk, dkv).astype(BF16)
+        part = nt(dpre[g], wqkv[...].reshape(1024, 512))
+        parts[g] = part.astype(BF16)
+
+        @pl.when(t == 3)
+        def _():
+            keep[...] = part
+
+        chip_sum_post(p, t, parts, recv, first_n)
+        return (sum_q, sum_k)
+
+    sum_q, sum_k = lax.fori_loop(0, 4, heads, (zero_row, zero_row))
+    gain_sum[2:3, 0:128] = sum_q
+    gain_sum[3:4, 0:128] = sum_k
+    chip_sum_across(p, parts, recv, first_n)
+
+    def qkv_rows(c, carry):
+        at = pl.multiple_of(128 * c, 128)
+        left = norm[:, :, pl.ds(at, 128)].reshape(1024, 128)
+        gqkv[c // 2, lax.rem(c, 2)] = tn(left, dpre[...].reshape(1024, 512)).astype(BF16)
+        return carry
+
+    lax.fori_loop(0, 8, qkv_rows, 0)
+    sum_qkv = SeqSum(p, y_q, z_q)
+    sum_qkv.start(gqkv)
+    sum_o.middle()
+
+    dn1 = keep[...] + chip_sum_rest(p, parts, recv, first_n)
+    xf = x[...].astype(F32)
+    r1 = rms_factor(xf)
+    gain_sum[0:1] = jnp.sum(dn1 * xf * r1, axis=0, keepdims=True)
+    dx[...] = (dmid[...] + norm_back(dn1 * gain_a[...], xf, r1)).astype(BF16)
+    got_gain = [p.post(gain_sum, gain_batch.at[b], (s, lax.rem(b + k, 4))) for k in (1, 2, 3)]
+    gain_batch[b] = gain_sum[...]
+    sum_qkv.middle()
+
+    rd[...] = sum_d.finish()
+
+    def exchange(total, fin, dst):
+        fin[...] = total.astype(BF16)
+        got = []
+        for k in (1, 2, 3):
+            to = lax.rem(b + k, 4)
+            rows = pl.ds(pl.multiple_of(32 * to, 32), 32)
+            got.append(p.post(fin.at[rows], dst(b), (s, to)))
+        dst(b)[...] = fin[pl.ds(pl.multiple_of(32 * b, 32), 32)]
+        return got
+
+    def arrive(got, dst):
+        for k in (1, 2, 3):
+            p.landed(got[k - 1], dst(lax.rem(b + 4 - k, 4)))
+
+    dst_g, dst_u, dst_q = (lambda i: rgu.at[i, 0]), (lambda i: rgu.at[i, 1]), (lambda i: rqkv.at[i])
+    got_g = exchange(sum_g.finish(), fin_g, dst_g)
+    for k in (1, 2, 3):
+        p.landed(got_gain[k - 1], gain_batch.at[lax.rem(b + 4 - k, 4)])
+    gain_seq[s] = (gain_batch[0] + gain_batch[1]) + (gain_batch[2] + gain_batch[3])
+    got_all = [p.post(gain_seq.at[s], gain_seq.at[s], (lax.rem(s + k, 8), b)) for k in range(1, 8)]
+    got_u = exchange(sum_u.finish(), fin_u, dst_u)
+    ro[...] = sum_o.finish()
+    got_q = exchange(sum_qkv.finish(), fin_q, dst_q)
+    for k in range(1, 8):
+        p.landed(got_all[k - 1], gain_seq.at[lax.rem(s + 8 - k, 8)])
+    total = gain_seq[0]
+    for k in range(1, 8):
+        total = total + gain_seq[k]
+    gains_out[...] = total
+    arrive(got_g, dst_g)
+    arrive(got_u, dst_u)
+    arrive(got_q, dst_q)
+    p.drain()
+
+
+def call(kernel, outs, in_specs, out_specs, scratch, cid, sems=(64, 16)):
+    return pl.pallas_call(
+        kernel,
+        out_shape=[jax.ShapeDtypeStruct(shape, dtype) for shape, dtype in outs],
+        in_specs=in_specs,
+        out_specs=out_specs,
+        scratch_shapes=[pltpu.VMEM(shape, dtype) for shape, dtype in scratch]
+        + [
+            pltpu.SemaphoreType.DMA((sems[0],)),
+            pltpu.SemaphoreType.DMA((sems[0],)),
+            pltpu.SemaphoreType.DMA((sems[1],)),
+        ],
+        compiler_params=pltpu.CompilerParams(
+            collective_id=cid, has_side_effects=True, vmem_limit_bytes=60 * 2**20
+        ),
+    )
+
+
+def body(
+    inputs, lengths, w_query, key_weight, value_weight, w_out, w_gate, w_up, w_down,
+    gain_attn, gain_ffn, gain_query, gain_key, cotangent,
+):
+    x = inputs.reshape(256, 1024)
+    dy = cotangent.reshape(256, 1024)
+    positions = lax.axis_index("seq") * 256 + jnp.arange(256, dtype=jnp.int32)
+    freqs = theta ** (-(jnp.arange(32, dtype=F32) * 2.0) / 64)
+    angles = positions.astype(F32)[:, None] * freqs[None, :]
+    cosine = jnp.tile(jnp.cos(angles), (1, 4))
+    sine = jnp.tile(jnp.sin(angles), (1, 4))
+    length = jnp.broadcast_to(lengths[:, None], (8, 128))
+    wqkv_in = jnp.concatenate(
+        [
+            w_query.reshape(32, 4, 2, 128),
+            key_weight.reshape(32, 4, 2, 64),
+            value_weight.reshape(32, 4, 2, 64),
+        ],
+        axis=-1,
+    )
+    wqkv_in = jnp.transpose(wqkv_in.reshape(32, 4, 512), (1, 0, 2))
+    wgu_in = jnp.stack([w_gate, w_up]).reshape(2, 32, 8, 4, 144)
+    wgu_in = jnp.transpose(wgu_in, (3, 0, 1, 2, 4)).reshape(4, 2, 32, 1152)
+    gain_q = jnp.tile(gain_query, 2)[None]
+    gain_k = jnp.tile(gain_key, 2)[None]
+    gain_a = gain_attn[None]
+    gain_f = gain_ffn[None]
+
+    (wgu, wd, wo, wqkv, norm, pre, unit, unit_out, lse, mix, norm_two, middle, dy_all, length_all) = call(
+        forward_kernel,
+        [
+            ((8, 2, 128, 1152), BF16), ((8, 144, 1024), BF16), ((8, 4, 32, 1024), BF16),
+            ((8, 128, 512), BF16), ((4, 256, 1024), BF16), ((4, 256, 512), F32),
+            ((8, 256, 256), BF16), ((8, 256, 128), BF16), ((8, 8, 512), F32),
+            ((4, 8, 256, 128), BF16), ((4, 256, 1024), BF16), ((256, 1024), F32),
+            ((4, 256, 1024), BF16), ((4, 8, 128), jnp.int32),
+        ],
+        [VMEM, ANY, VMEM, VMEM, ANY, ANY, VMEM] + [VMEM] * 6,
+        [ANY, ANY] + [VMEM] * 10 + [ANY, VMEM],
+        [
+            ((4, 256, 1024), BF16), ((8, 256, 256), BF16), ((8, 256, 128), BF16), ((8, 80, 256), BF16),
+        ],
+        0,
+        sems=(96, 16),
+    )(x, dy, length, wqkv_in, wgu_in, w_down, w_out, cosine, sine, gain_q, gain_k, gain_a, gain_f)
+
+    output, dn2, ggu, gd = call(
+        feed_kernel,
+        [
+            ((256, 1024), BF16), ((256, 1024), F32), ((8, 2, 128, 1152), BF16), ((1152, 1024), BF16),
+        ],
+        [VMEM] * 5,
+        [VMEM] * 4,
+        [
+            ((1024, 1152), BF16), ((1024, 1152), BF16), ((1024, 1152), BF16),
+            ((4, 256, 1024), BF16), ((3, 256, 1024), BF16), ((4, 256, 1024), BF16),
+            ((3, 256, 1024), BF16), ((256, 1024), F32), ((256, 1024), F32),
+        ],
+        1,
+    )(norm_two, dy_all, wgu, wd, middle)
+
+    dx, rqkv, rgu, rd, ro, gains = call(
+        backward_kernel,
+        [
+            ((256, 1024), BF16), ((4, 32, 512), BF16), ((4, 2, 32, 1152), BF16),
+            ((144, 1024), F32), ((32, 1024), F32), ((8, 1024), F32),
+        ],
+        [VMEM] * 19 + [ANY] * 2,
+        [VMEM] * 6,
+        [
+            ((256, 1024), F32), ((4, 2, 256, 128), BF16), ((8, 256, 128), BF16), ((8, 256, 128), BF16),
+            ((4, 256, 1024), BF16), ((8, 256, 128), BF16), ((8, 64, 256), BF16), ((8, 128, 512), BF16),
+            ((8, 128, 512), BF16), ((8, 512, 128), BF16), ((8, 512, 128), BF16), ((8, 8, 512), F32),
+            ((8, 256, 128), F32), ((8, 256, 128), F32), ((8, 256, 256), BF16), ((8, 256, 256), BF16),
+            ((4, 256, 512), BF16), ((4, 256, 1024), BF16), ((3, 256, 1024), BF16), ((256, 1024), F32),
+            ((4, 2, 128, 512), BF16), ((4, 2, 32, 1024), BF16), ((128, 1024), BF16),
+            ((4, 144, 1024), BF16), ((4, 144, 1024), BF16), ((3, 144, 1024), BF16),
+            ((4, 128, 1152), BF16), ((4, 128, 1152), BF16), ((3, 128, 1152), BF16),
+            ((4, 128, 1152), BF16), ((4, 128, 1152), BF16), ((3, 128, 1152), BF16),
+            ((4, 128, 512), BF16), ((3, 128, 512), BF16), ((4, 32, 1024), BF16), ((3, 32, 1024), BF16),
+            ((128, 1152), BF16), ((128, 1152), BF16), ((128, 512), BF16),
+            ((8, 1024), F32), ((4, 8, 1024), F32), ((8, 8, 1024), F32),
+        ],
+        2,
+        sems=(96, 16),
+    )(
+        dn2, middle, x, dy, wo, mix, unit, unit_out, lse, length_all, pre, norm, wqkv,
+        cosine, sine, gain_q, gain_k, gain_a, gain_f,
+        ggu.reshape(4, 2, 2, 128, 1152), gd.reshape(4, 2, 144, 1024),
+    )
+
+    rows = jnp.transpose(rqkv, (1, 0, 2)).reshape(32, 8, 256).astype(F32)
+    grad_query = rows[:, :, 0:128].reshape(32, 1024)
+    grad_key = rows[:, :, 128:192].reshape(32, 512)
+    grad_value = rows[:, :, 192:256].reshape(32, 512)
+    wide = jnp.transpose(rgu.reshape(4, 2, 32, 8, 144), (1, 2, 3, 0, 4)).reshape(2, 32, 4608).astype(F32)
+    return (
+        output.reshape(256, 1, 1024),
+        dx.reshape(256, 1, 1024),
+        grad_query,
+        grad_key,
+        grad_value,
+        ro,
+        wide[0],
+        wide[1],
+        rd,
+        gains[0],
+        gains[1],
+        gains[2, 0:64] + gains[2, 64:128],
+        gains[3, 0:64],
+    )
 
 
 def rotary_tables(positions, width):
@@ -32,12 +870,6 @@
     return grad * cosine + jnp.concatenate([moved[..., half:], -moved[..., :half]], axis=-1)
 
 
-def norm_back(grad, value, factor):
-    return factor * (
-        grad - value * factor * factor * jnp.mean(grad * value, axis=-1, keepdims=True)
-    )
-
-
 def product(left, right):
     return jnp.dot(left, right, preferred_element_type=jnp.float32)
 
@@ -64,7 +896,7 @@
     return jnp.sum(piece, axis=1).reshape(-1, piece.shape[-1])
 
 
-def body(
+def general_body(
     inputs,
     lengths,
     w_query,
@@ -381,35 +1213,10 @@
 
 
 def solution(mesh):
-    in_specs = (
-        P("seq", "batch", None),
-        P("batch"),
-        P(("seq", "batch"), None),
-        P(("seq", "batch"), None),
-        P(("seq", "batch"), None),
-        P(("seq", "batch"), None),
-        P(("seq", "batch"), None),
-        P(("seq", "batch"), None),
-        P(("seq", "batch"), None),
-        P(),
-        P(),
-        P(),
-        P(),
-        P("seq", "batch", None),
-    )
-    out_specs = (
-        P("seq", "batch", None),
-        P("seq", "batch", None),
-        P(("seq", "batch"), None),
-        P(("seq", "batch"), None),
-        P(("seq", "batch"), None),
-        P(("seq", "batch"), None),
-        P(("seq", "batch"), None),
-        P(("seq", "batch"), None),
-        P(("seq", "batch"), None),
-        P(),
-        P(),
-        P(),
-        P(),
-    )
-    return jax.shard_map(body, mesh=mesh, in_specs=in_specs, out_specs=out_specs, check_vma=False)
+    sharded = P(("seq", "batch"), None)
+    stream = P("seq", "batch", None)
+    in_specs = (stream, P("batch")) + (sharded,) * 7 + (P(),) * 4 + (stream,)
+    out_specs = (stream, stream) + (sharded,) * 7 + (P(),) * 4
+    grouped = mesh.shape["seq"] == 8 and mesh.shape["batch"] == 4
+    step = body if grouped else general_body
+    return jax.shard_map(step, mesh=mesh, in_specs=in_specs, out_specs=out_specs, check_vma=False)

time: 1560 us -> 498 us (0.32)
  waiting for transfers between devices: 1070 us -> 0 us
  Pallas kernels: 0 us -> 468 us
  matrix products: 200 us -> 0 us
  local copies, waits for them, and re-layouts: 105 us -> 25 us
  other arithmetic: 80.4 us -> 2.92 us
  blocking collectives: 38.8 us -> 0 us
  starting transfers between devices: 35.3 us -> 0 us
    all_gather x9 -> x0, waiting for transfers between devices: 482 us -> none  [the longest x1 81.2 us: body(): lax.all_gather(shards[4], ('seq', 'batch'), axis=0, tiled=True)]
    pallas_call x0 -> x3, Pallas kernels: none -> 468 us  [the longest x1 213 us: body(): call(forward_kernel, [((8, 2, 128, 1152), BF16), ((8, 144, 1024), BF16),...]
    reduce_scatter x9 -> x0, waiting for transfers between devices: 295 us -> none  [the longest x1 69.6 us: body(): lax.psum_scatter(partial_sums[5].astype(jnp.bfloat16), 'seq', scatter_dim...]
    all_to_all x7 -> x0, waiting for transfers between devices: 292 us -> none  [the longest x1 97 us: body(): lax.all_to_all(split_rows(grad_wd, cycle_size, batch_size).astype(jnp.bfl...]
    dot_general x63 -> x0, matrix products: 200 us -> none  [the longest x7 38.3 us: product(): return jnp.dot(left, right, preferred_element_type=jnp.float32)]
    reduce_sum x17 -> x0, other arithmetic: 54.8 us -> none  [the longest x7 32 us: fold_sources(): return jnp.sum(piece, axis=1).reshape(-1, piece.shape[-1])]
    psum x1 -> x0, blocking collectives: 38.8 us -> none  [body(): lax.psum((grad_gain_attn, grad_gain_ffn, grad_gain_query, grad_gain_key),...]
    convert_element_type x11 -> x3, local copies, waits for them, and re-layouts: 40 us -> 1.53 us  [the longest x1 1.25 us: body(): jnp.transpose(rgu.reshape(4, 2, 32, 8, 144), (1, 2, 3, 0, 4))]
  transfers between devices with their start and end apart: 25 -> 0, of which waited for: 20 -> 0; matrix products, arithmetic and copies ran while one was open for 15% -> 0% of each run, Pallas kernels for 0% -> 0%
where the time goes in v1:
time: 498 us
  Pallas kernels  468 us (94%)
  local copies, waits for them, and re-layouts  25 us (5%)
    pallas_call x1, Pallas kernels, body(): call(forward_kernel, [((8, 2, 128, 1152), BF16), ((8, 144, 1024), BF16),...  213 us
    pallas_call x1, Pallas kernels, body(): call(backward_kernel, [((256, 1024), BF16), ((4, 32, 512), BF16), ((4, 2,...  203 us
    pallas_call x1, Pallas kernels, body(): call(feed_kernel, [((256, 1024), BF16), ((256, 1024), F32), ((8, 2, 128,...  52.3 us

profile of v1, /device:TPU:0, one launch (start us, length us, event | category | flops | bytes accessed | tf_op | source)
XLA Modules:
  0.0 497.5 jit_solution(17174033139832093460)
XLA Ops:
  4.7 0.9 reshape.162
  5.6 0.9 reshape.163
  6.4 0.9 reshape.164
  7.7 0.7 copy.52
  8.3 0.8 copy.40.sin
  9.1 0.8 copy.39.cos
  9.9 0.9 stack.9
  10.8 0.9 stack.10
  12.0 1.8 reshape.166.wgu_in
  13.8 213.1 %shard_map.237 = (bf16[8,2,128,1152]{3,2,1,0:T(8,128)(2,1)}, bf16[8,144,1024]{2,1,0:T(8,128)(2,1)}, bf16[8,4,32,1024]{3,2,1,0:T(8,128)(2,1)}, bf16[8,128,512]{2,...) custom-call(bf16[256,1024]{1,0:T(8,128)(2,1)} %bitcast.37, ...), custom_call_target="tpu_custom_call" | custom-call | tf_op jit(solution)/shard_map/pallas_call | solution.py:767
  226.9 52.3 %shard_map.238 = (bf16[256,1024]{1,0:T(8,128)(2,1)}, f32[256,1024]{1,0:T(8,128)}, bf16[8,2,128,1152]{3,2,1,0:T(8,128)(2,1)}, bf16[1152,1024]{1,0:T(8,128)(2,1)}) custom-call(bf16[4,256,1024]{2,1,0:T(8,128)(2,1)} %get-tuple-element.37.norm_two, bf16[4,256,1024]{2,1,0:T(8,128)(2,1)} %get-tuple-element.38.dy_all, ...), custom_call_target="tpu_custom_call" | custom-call | tf_op jit(solution)/shard_map/pallas_call | solution.py:785
  279.2 202.6 %shard_map.239 = (bf16[256,1024]{1,0:T(8,128)(2,1)}, bf16[4,32,512]{2,1,0:T(8,128)(2,1)}, bf16[4,2,32,1152]{3,2,1,0:T(8,128)(2,1)}, f32[144,1024]{1,0:T(8,128)}, f32[32,1024]{1,0:T(8,128)}, /*index=5*/f32[8,1024]{1,0:T(8,128)}) custom-call(f32[256,1024]{1,0:T(8,128)} %get-tuple-element.43.dn2, f32[256,1024]{1,0:T(8,128)} %get-tuple-element.41.middle, ...), custom_call_target="tpu_custom_call" | custom-call | tf_op jit(solution)/shard_map/pallas_call | solution.py:800
  481.8 1.4 slice_bitcast_fusion
  483.2 1.4 fusion.2
  484.7 0.9 convert_bitcast_fusion
  485.9 0.7 copy.51
  486.7 0.7 reshape.173
  487.4 0.7 reshape.172
  488.1 1.2 reshape.175
  490.2 1.8 squeeze.18
  492.7 1.8 squeeze.17
  494.4 0.8 copy.58
  495.2 0.8 copy.59
  496.7 0.8 copy.61
  (37 shorter events, 6.5 us)
Async XLA Ops:
  0.6 10.2 %copy-start.5 = (bf16[32,4608]{1,0:T(8,128)(2,1)S(1)}, bf16[32,4608]{1,0:T(8,128)(2,1)}, u32[]{:S(2)}) copy-start(bf16[32,4608]{1,0:T(8,128)(2,1)} %param.21) | copy-start | bytes 884740
  0.7 9.2 %copy-start.4 = (bf16[32,4608]{1,0:T(8,128)(2,1)S(1)}, bf16[32,4608]{1,0:T(8,128)(2,1)}, u32[]{:S(2)}) copy-start(bf16[32,4608]{1,0:T(8,128)(2,1)} %param.20) | copy-start | bytes 884740
  481.8 6.3 %copy-start.1 = (bf16[4,2,32,1152]{3,2,1,0:T(8,128)(2,1)S(1)}, bf16[4,2,32,1152]{3,2,1,0:T(8,128)(2,1)}, u32[]{:S(2)}) copy-start(bf16[4,2,32,1152]{3,2,1,0:T(8,128)(2,1)} %get-tuple-element.58) | copy-start | bytes 1769476
  492.0 2.5 copy-start.2
  492.0 3.3 copy-start.3
  492.7 3.4 copy-start.6
  492.7 4.0 copy-start

commit v2 on v1

--- a/solution.py
+++ b/solution.py
@@ -75,6 +75,10 @@
         self.across = lax.rem(self.b + 2, 4)
         self.far = 3 - self.b
         self.flip = 2 * self.z + 1 - self.y
+        self.inner = jnp.logical_or(self.z == 1, self.z == 2)
+        self.pair = self.z + 1 - 2 * lax.rem(self.z, 2)
+        self.there = jnp.where(self.z < 2, 2, 1)
+        self.beyond = jnp.where(self.z < 2, 3, 0)
         self.send_sem, self.recv_sem, self.local_sem = send_sem, recv_sem, local_sem
         self.used = 0
         self.used_local = 0
@@ -134,6 +138,66 @@
         for made in self.sent:
             made.wait_send()
         self.sent = []
+
+
+class Spread:
+    def __init__(self, p, slot):
+        self.p, self.slot = p, slot
+        self.first = p.slots(8)
+        self.from_z = (p.pair, p.there, p.beyond)
+
+    def send(self, s, device, out, into):
+        self.p.copy(self.slot(s), self.slot(s), device, self.first + out, self.first + into).start()
+
+    def start(self):
+        p = self.p
+        self.send(p.s, (2 * p.pair + p.y, p.b), 0, 0)
+        self.send(p.s, (2 * p.there + p.y, p.b), 1, jnp.where(p.inner, 1, 2))
+        self.send(p.s, (p.flip, p.b), 4, 3)
+
+    def land(self, j):
+        p = self.p
+        s = 2 * self.from_z[j] + p.y
+        p.landed(self.first + j, self.slot(s))
+        if j > 0:
+
+            @pl.when(p.inner)
+            def _():
+                self.send(s, (2 * p.pair + p.y, p.b), 1 + j, j)
+
+        self.send(s, (p.flip, p.b), 5 + j, 4 + j)
+
+    def land_inner(self):
+        @pl.when(self.p.inner)
+        def _():
+            self.land(1)
+            self.land(2)
+
+    def land_end(self):
+        @pl.when(jnp.logical_not(self.p.inner))
+        def _():
+            self.land(1)
+            self.land(2)
+
+    def finish(self):
+        p = self.p
+        p.landed(self.first + 3, self.slot(p.flip))
+        for j in range(3):
+            p.landed(self.first + 4 + j, self.slot(2 * self.from_z[j] + 1 - p.y))
+
+    def drain(self):
+        p = self.p
+
+        def sent(out):
+            p.copy(self.slot(p.s), self.slot(p.s), (p.flip, p.b), self.first + out).wait_send()
+
+        for out in (0, 1, 4, 5, 6, 7):
+            sent(out)
+
+        @pl.when(p.inner)
+        def _():
+            sent(2)
+            sent(3)
 
 
 def forward_kernel(
@@ -183,6 +247,11 @@
         slot = 2 * p.down(k) + y
         p.landed(z_qkv[k - 1], wqkv.at[slot])
         y_qkv.append(p.post(wqkv.at[slot], wqkv.at[slot], (p.flip, b)))
+    own_d.wait()
+    spread_d = Spread(p, lambda i: wd.at[i])
+    spread_g = Spread(p, lambda i: wgu.at[i, 0])
+    spread_u = Spread(p, lambda i: wgu.at[i, 1])
+    spread_d.start()
     p.landed(x_core, xa.at[p.core])
     p.landed(x_far, xa.at[p.far])
     for k in (1, 2, 3):
@@ -199,17 +268,11 @@
         p.landed(y_qkv[k], wqkv.at[2 * p.down(k) + 1 - y])
 
     own_gu.wait()
-    own_d.wait()
     own_dy.wait()
     for k in (1, 2, 3):
         p.landed(got_gu[k - 1], wgu.at[s, :, my_rows])
-    first_ffn = p.used
-    z_gu, z_d = [], []
-    for k in (1, 2, 3):
-        z_gu.append(p.post(wgu.at[s], wgu.at[s], (2 * p.up(k) + y, b)))
-        z_d.append(p.post(wd.at[s], wd.at[s], (2 * p.up(k) + y, b)))
-    y_gu = [p.post(wgu.at[s], wgu.at[s], (p.flip, b))]
-    y_d = [p.post(wd.at[s], wd.at[s], (p.flip, b))]
+    spread_g.start()
+    spread_u.start()
 
     first_unit = p.slots(8)
 
@@ -243,6 +306,8 @@
 
     lax.fori_loop(0, 4, project, 0)
     own_unit = p.local(pack.at[s], unit.at[s])
+    spread_d.land(0)
+    spread_d.land_inner()
 
     for k in (1, 2, 3):
         slot = 2 * p.down(k) + y
@@ -255,6 +320,11 @@
         p.landed(y_wo[k], wo.at[2 * p.down(k) + 1 - y, b])
     wo_core = p.post(wo.at[:, b], wo.at[:, b], (s, p.core))
     wo_across = p.post(wo.at[:, b], wo.at[:, b], (s, p.across))
+    spread_d.land_end()
+    spread_g.land(0)
+    spread_u.land(0)
+    spread_g.land_inner()
+    spread_u.land_inner()
 
     for t in range(3):
         for other in (0, 1):
@@ -281,7 +351,16 @@
     wo_far = p.post(wo.at[:, p.across], wo.at[:, p.across], (s, p.core))
     p.landed(dy_across, dy_all.at[p.across])
     dy_far = p.post(dy_all.at[p.across], dy_all.at[p.across], (s, p.core))
-    first_mix = p.slots(8)
+    first_mix, first_across, first_core = p.slots(8), p.slots(8), p.slots(8)
+
+    def mix_send(src, t):
+        p.copy(mix.at[b, src], mix.at[b, src], (s, p.across), first_across + t).start()
+        p.copy(mix.at[b, src], mix.at[b, src], (s, p.core), first_core + t).start()
+
+    def mix_arrived(t):
+        src = lax.rem(s + 7 - t, 8)
+        p.landed(first_mix + t, mix.at[b, src])
+        mix_send(src, t)
 
     def attend(t, carry):
         i = lax.rem(s + 1 + t, 8)
@@ -306,29 +385,39 @@
         def _():
             p.copy(unit_out.at[i], mix.at[b, s], (i, b), first_mix + t).start()
 
+        @pl.when(t == 2)
+        def _():
+            spread_g.land_end()
+
+        @pl.when(t == 4)
+        def _():
+            spread_u.land_end()
+
+        @pl.when(t >= 4)
+        def _():
+            mix_arrived(t - 4)
+
         return carry
 
     lax.fori_loop(0, 8, attend, 0)
     own_mix = p.local(unit_out.at[s], mix.at[b, s])
-    for k in (1, 2, 3):
-        slot = 2 * p.down(k) + y
-        p.landed(z_gu[k - 1], wgu.at[slot])
-        p.landed(z_d[k - 1], wd.at[slot])
-        y_gu.append(p.post(wgu.at[slot], wgu.at[slot], (p.flip, b)))
-        y_d.append(p.post(wd.at[slot], wd.at[slot], (p.flip, b)))
+    own_mix.wait()
+    mix_send(s, 7)
+    for t in range(4, 7):
+        mix_arrived(t)
     for t in range(7):
-        p.landed(first_mix + t, mix.at[b, lax.rem(s + 7 - t, 8)])
         p.copy(unit_out.at[s], mix.at[b, s], (p.flip, b), first_mix + t).wait_send()
-    own_mix.wait()
-    mix_across = p.post(mix.at[b], mix.at[b], (s, p.across))
-    mix_core = p.post(mix.at[b], mix.at[b], (s, p.core))
-    p.landed(mix_across, mix.at[p.across])
-    mix_far = p.post(mix.at[p.across], mix.at[p.across], (s, p.core))
     p.landed(wo_core, wo.at[:, p.core])
     p.landed(wo_far, wo.at[:, p.far])
     p.landed(dy_core, dy_all.at[p.core])
     p.landed(dy_far, dy_all.at[p.far])
-    p.landed(mix_core, mix.at[p.core])
+    for t in range(8):
+        p.landed(first_across + t, mix.at[p.across, lax.rem(s + 7 - t, 8)])
+    mix_far = p.post(mix.at[p.across], mix.at[p.across], (s, p.core))
+    for t in range(8):
+        p.landed(first_core + t, mix.at[p.core, lax.rem(s + 7 - t, 8)])
+        p.copy(mix.at[b, s], mix.at[b, s], (s, p.across), first_across + t).wait_send()
+        p.copy(mix.at[b, s], mix.at[b, s], (s, p.core), first_core + t).wait_send()
     p.landed(mix_far, mix.at[p.far])
 
     def project_out(g, carry):
@@ -343,11 +432,9 @@
         return carry
 
     lax.fori_loop(0, 4, project_out, 0)
-    p.landed(y_gu[0], wgu.at[p.flip])
-    p.landed(y_d[0], wd.at[p.flip])
-    for k in (1, 2, 3):
-        p.landed(y_gu[k], wgu.at[2 * p.down(k) + 1 - y])
-        p.landed(y_d[k], wd.at[2 * p.down(k) + 1 - y])
+    for spread in (spread_d, spread_g, spread_u):
+        spread.finish()
+        spread.drain()
     p.drain()
 
 
@@ -381,7 +468,7 @@
 
 def feed_kernel(
     norm_two, dy_all, wgu, wd, middle,
-    output, dn2, ggu, gd,
+    output, dn2, ggu, gd, gd_other,
     hid, dgate, dup, parts_n, recv_n, parts_o, recv_o, keep_n, keep_o, send_sem, recv_sem, local_sem,
 ):
     p = Place(send_sem, recv_sem, local_sem)
@@ -415,6 +502,17 @@
     lax.fori_loop(0, 4, gated, 0)
     chip_sum_across(p, parts_n, recv_n, first_n)
 
+    def down_rows(c, carry):
+        at = pl.multiple_of(128 * c, 128)
+        gd[pl.ds(at, 128)] = tn(hid[:, pl.ds(at, 128)], dy_all[...].reshape(1024, 1024)).astype(BF16)
+        return carry
+
+    lax.fori_loop(0, 9, down_rows, 0)
+    sent_d = []
+    for i in range(4):
+        rows = pl.ds(pl.multiple_of(144 * (2 * i + 1 - p.y), 16), 144)
+        sent_d.append(p.post(gd.at[rows], gd_other.at[i], (p.flip, p.b)))
+
     def down(t, carry):
         g = batch_order(p, t)
         part = nn(hid[pl.ds(pl.multiple_of(g * 256, 256), 256)], wd[...].reshape(1152, 1024))
@@ -429,13 +527,6 @@
 
     lax.fori_loop(0, 4, down, 0)
     chip_sum_across(p, parts_o, recv_o, first_o)
-
-    def down_rows(c, carry):
-        at = pl.multiple_of(128 * c, 128)
-        gd[pl.ds(at, 128)] = tn(hid[:, pl.ds(at, 128)], dy_all[...].reshape(1024, 1024)).astype(BF16)
-        return carry
-
-    lax.fori_loop(0, 9, down_rows, 0)
 
     def gate_rows(c, carry):
         at = pl.multiple_of(128 * c, 128)
@@ -448,6 +539,67 @@
     dn2[...] = keep_n[...] + chip_sum_rest(p, parts_n, recv_n, first_n)
     total = keep_o[...] + chip_sum_rest(p, parts_o, recv_o, first_o)
     output[...] = (middle[...] + total).astype(BF16)
+    for i in range(4):
+        p.landed(sent_d[i], gd_other.at[i])
+    p.drain()
+
+
+class SeqTree:
+    def __init__(self, p, mine, y_recv, relayed, z_recv, sums=None):
+        self.p, self.mine, self.y_recv, self.relayed, self.z_recv = p, mine, y_recv, relayed, z_recv
+        self.sums = y_recv if sums is None else sums
+        self.first = p.slots(6)
+        self.started = False
+
+    def start(self):
+        p = self.p
+        self.started = True
+        p.copy(self.mine.at[:, 1 - p.y], self.y_recv, (p.flip, p.b), self.first + 4).start()
+
+    def send(self, i, dst, z, out, into):
+        p = self.p
+        p.copy(self.sums.at[i], dst, (2 * z + p.y, p.b), self.first + out, self.first + into).start()
+
+    def reduce(self):
+        p = self.p
+        if self.started:
+            p.landed(self.first + 4, self.y_recv)
+
+        def add(i):
+            self.sums[i] = (self.y_recv[i].astype(F32) + self.mine[i, p.y].astype(F32)).astype(BF16)
+
+        add(p.there)
+        add(p.beyond)
+
+        @pl.when(jnp.logical_not(p.inner))
+        def _():
+            self.send(p.there, self.relayed.at[0], p.pair, 1, 1)
+            self.send(p.beyond, self.relayed.at[1], p.pair, 2, 2)
+
+        add(p.pair)
+        self.send(p.pair, self.z_recv.at[0], p.pair, 0, 0)
+
+    def relay(self):
+        p = self.p
+
+        @pl.when(p.inner)
+        def _():
+            for k, i in ((0, p.there), (1, p.beyond)):
+                p.landed(self.first + 1 + k, self.relayed.at[k])
+                self.sums[i] = (self.sums[i].astype(F32) + self.relayed[k].astype(F32)).astype(BF16)
+                self.send(i, self.z_recv.at[1], i, 1 + k, 3)
+
+    def finish(self):
+        p = self.p
+        total = self.y_recv[p.z].astype(F32) + self.mine[p.z, p.y].astype(F32)
+        p.landed(self.first, self.z_recv.at[0])
+        total = total + self.z_recv[0].astype(F32)
+        p.landed(self.first + 3, self.z_recv.at[1])
+        for out in range(3):
+            p.copy(self.z_recv.at[0], self.z_recv.at[0], (p.flip, p.b), self.first + out).wait_send()
+        if self.started:
+            p.copy(self.y_recv, self.y_recv, (p.flip, p.b), self.first + 4).wait_send()
+        return total + self.z_recv[1].astype(F32)
 
 
 class SeqSum:
@@ -486,21 +638,22 @@
 
 def backward_kernel(
     dn2, middle, x, dy, wo, mix, unit, unit_out, lse, length_all, pre, norm, wqkv,
-    cos, sin, gain_q, gain_k, gain_a, gain_f, ggu, gd,
+    cos, sin, gain_q, gain_k, gain_a, gain_f, ggu, gd, y_d,
     dx, rqkv, rgu, rd, ro, gains_out,
     dmid, dox, doq, dou, dbr, kv, kt, q_right, do_right, q_left, do_left, delta, dk2, dv2, back, dqr,
     dpre, parts, recv, keep, gqkv, go, mixt,
-    y_d, m_d, z_d, y_g, m_g, z_g, y_u, m_u, z_u, y_q, z_q, y_o, z_o, fin_g, fin_u, fin_q,
+    s_d, t_d, z_d, y_g, t_g, z_g, y_u, t_u, z_u, y_q, z_q, y_o, z_o, fin_g, fin_u, fin_q,
     gain_sum, gain_batch, gain_seq,
     send_sem, recv_sem, local_sem,
 ):
     p = Place(send_sem, recv_sem, local_sem)
     s, b, z, y = p.s, p.b, p.z, p.y
     p.greet()
-    sum_d, sum_g, sum_u = SeqSum(p, y_d, z_d), SeqSum(p, y_g, z_g), SeqSum(p, y_u, z_u)
-    sum_d.start(gd, m_d)
-    sum_g.start(ggu.at[:, :, 0], m_g)
-    sum_u.start(ggu.at[:, :, 1], m_u)
+    sum_d = SeqTree(p, gd, y_d, t_d, z_d, s_d)
+    sum_g = SeqTree(p, ggu.at[:, :, 0], y_g, t_g, z_g)
+    sum_u = SeqTree(p, ggu.at[:, :, 1], y_u, t_u, z_u)
+    sum_g.start()
+    sum_d.reduce()
 
     mid = middle[...]
     r2 = rms_factor(mid)
@@ -546,7 +699,7 @@
         return carry
 
     lax.fori_loop(0, 8, prepare, 0)
-    sum_d.middle()
+    sum_d.relay()
     p.landed(dbr_across, dbr.at[p.across])
     dbr_far = p.post(dbr.at[p.across], dbr.at[p.across], (s, p.core))
     for k in range(1, 8):
@@ -596,9 +749,12 @@
         back[i, :, 128:256] = jnp.where(live, dkv, 0.0).astype(BF16)
         return carry
 
-    lax.fori_loop(0, 3, queries, 0)
-    sum_g.middle()
-    lax.fori_loop(3, 8, queries, 0)
+    lax.fori_loop(0, 1, queries, 0)
+    sum_g.reduce()
+    sum_u.start()
+    lax.fori_loop(1, 4, queries, 0)
+    sum_g.relay()
+    lax.fori_loop(4, 8, queries, 0)
     got_back = []
     for k in range(1, 8):
         to = lax.rem(s + k, 8)
@@ -620,7 +776,7 @@
     lax.fori_loop(0, 8, turn, 0)
     sum_o = SeqSum(p, y_o, z_o)
     sum_o.start(go)
-    sum_u.middle()
+    sum_u.reduce()
     for k in range(1, 8):
         p.landed(got_back[k - 1], dqr.at[lax.rem(s + 8 - k, 8)])
 
@@ -670,6 +826,7 @@
     lax.fori_loop(0, 8, qkv_rows, 0)
     sum_qkv = SeqSum(p, y_q, z_q)
     sum_qkv.start(gqkv)
+    sum_u.relay()
     sum_o.middle()
 
     dn1 = keep[...] + chip_sum_rest(p, parts, recv, first_n)
@@ -779,16 +936,17 @@
             ((4, 256, 1024), BF16), ((8, 256, 256), BF16), ((8, 256, 128), BF16), ((8, 80, 256), BF16),
         ],
         0,
-        sems=(96, 16),
+        sems=(128, 16),
     )(x, dy, length, wqkv_in, wgu_in, w_down, w_out, cosine, sine, gain_q, gain_k, gain_a, gain_f)
 
-    output, dn2, ggu, gd = call(
+    output, dn2, ggu, gd, gd_other = call(
         feed_kernel,
         [
             ((256, 1024), BF16), ((256, 1024), F32), ((8, 2, 128, 1152), BF16), ((1152, 1024), BF16),
+            ((4, 144, 1024), BF16),
         ],
         [VMEM] * 5,
-        [VMEM] * 4,
+        [VMEM] * 5,
         [
             ((1024, 1152), BF16), ((1024, 1152), BF16), ((1024, 1152), BF16),
             ((4, 256, 1024), BF16), ((3, 256, 1024), BF16), ((4, 256, 1024), BF16),
@@ -803,7 +961,7 @@
             ((256, 1024), BF16), ((4, 32, 512), BF16), ((4, 2, 32, 1152), BF16),
             ((144, 1024), F32), ((32, 1024), F32), ((8, 1024), F32),
         ],
-        [VMEM] * 19 + [ANY] * 2,
+        [VMEM] * 22,
         [VMEM] * 6,
         [
             ((256, 1024), F32), ((4, 2, 256, 128), BF16), ((8, 256, 128), BF16), ((8, 256, 128), BF16),
@@ -812,9 +970,9 @@
             ((8, 256, 128), F32), ((8, 256, 128), F32), ((8, 256, 256), BF16), ((8, 256, 256), BF16),
             ((4, 256, 512), BF16), ((4, 256, 1024), BF16), ((3, 256, 1024), BF16), ((256, 1024), F32),
             ((4, 2, 128, 512), BF16), ((4, 2, 32, 1024), BF16), ((128, 1024), BF16),
-            ((4, 144, 1024), BF16), ((4, 144, 1024), BF16), ((3, 144, 1024), BF16),
-            ((4, 128, 1152), BF16), ((4, 128, 1152), BF16), ((3, 128, 1152), BF16),
-            ((4, 128, 1152), BF16), ((4, 128, 1152), BF16), ((3, 128, 1152), BF16),
+            ((4, 144, 1024), BF16), ((2, 144, 1024), BF16), ((2, 144, 1024), BF16),
+            ((4, 128, 1152), BF16), ((2, 128, 1152), BF16), ((2, 128, 1152), BF16),
+            ((4, 128, 1152), BF16), ((2, 128, 1152), BF16), ((2, 128, 1152), BF16),
             ((4, 128, 512), BF16), ((3, 128, 512), BF16), ((4, 32, 1024), BF16), ((3, 32, 1024), BF16),
             ((128, 1152), BF16), ((128, 1152), BF16), ((128, 512), BF16),
             ((8, 1024), F32), ((4, 8, 1024), F32), ((8, 8, 1024), F32),
@@ -824,7 +982,7 @@
     )(
         dn2, middle, x, dy, wo, mix, unit, unit_out, lse, length_all, pre, norm, wqkv,
         cosine, sine, gain_q, gain_k, gain_a, gain_f,
-        ggu.reshape(4, 2, 2, 128, 1152), gd.reshape(4, 2, 144, 1024),
+        ggu.reshape(4, 2, 2, 128, 1152), gd.reshape(4, 2, 144, 1024), gd_other,
     )
 
     rows = jnp.transpose(rqkv, (1, 0, 2)).reshape(32, 8, 256).astype(F32)

time: 498 us -> 386 us (0.78)
  Pallas kernels: 468 us -> 352 us
    pallas_call x1, Pallas kernels: 213 us -> 144 us  [body(): call(forward_kernel, [((8, 2, 128, 1152), BF16), ((8, 144, 1024), BF16),...]
    pallas_call x1, Pallas kernels: 203 us -> 138 us  [body(): call(backward_kernel, [((256, 1024), BF16), ((4, 32, 512), BF16), ((4, 2,...]
    pallas_call x1, Pallas kernels: 52.3 us -> 69.5 us  [body(): call(feed_kernel, [((256, 1024), BF16), ((256, 1024), F32), ((8, 2, 128,...]
where the time goes in v2:
time: 386 us; the launch traced here: 381 us
  Pallas kernels  352 us (91%)
  local copies, waits for them, and re-layouts  25 us (6%)
    pallas_call x1, Pallas kernels, body(): call(forward_kernel, [((8, 2, 128, 1152), BF16), ((8, 144, 1024), BF16),...  144 us
    pallas_call x1, Pallas kernels, body(): call(backward_kernel, [((256, 1024), BF16), ((4, 32, 512), BF16), ((4, 2,...  138 us
    pallas_call x1, Pallas kernels, body(): call(feed_kernel, [((256, 1024), BF16), ((256, 1024), F32), ((8, 2, 128,...  69.5 us

profile of v2, /device:TPU:0, one launch (start us, length us, event | category | flops | bytes accessed | tf_op | source)
XLA Modules:
  0.0 381.1 jit_solution(6298910729561884714)
XLA Ops:
  4.7 0.9 reshape.162
  5.6 0.9 reshape.163
  6.4 0.9 reshape.164
  7.7 0.7 copy.52
  8.3 0.8 copy.40.sin
  9.1 0.8 copy.39.cos
  9.9 0.9 stack.9
  10.8 0.9 stack.10
  12.0 1.8 reshape.166.wgu_in
  13.8 143.8 %shard_map.237 = (bf16[8,2,128,1152]{3,2,1,0:T(8,128)(2,1)}, bf16[8,144,1024]{2,1,0:T(8,128)(2,1)}, bf16[8,4,32,1024]{3,2,1,0:T(8,128)(2,1)}, bf16[8,128,512]{2,...) custom-call(bf16[256,1024]{1,0:T(8,128)(2,1)} %bitcast.37, ...), custom_call_target="tpu_custom_call" | custom-call | tf_op jit(solution)/shard_map/pallas_call | solution.py:924
  157.6 69.5 %shard_map.238 = (bf16[256,1024]{1,0:T(8,128)(2,1)}, f32[256,1024]{1,0:T(8,128)}, bf16[8,2,128,1152]{3,2,1,0:T(8,128)(2,1)}, bf16[1152,1024]{1,0:T(8,128)(2,1)}, bf16[4,144,1024]{2,1,0:T(8,128)(2,1)}) custom-call(bf16[4,256,1024]{2,1,0:T(8,128)(2,1)} %get-tuple-element.38.norm_two, bf16[4,256,1024]{2,1,0:T(8,128)(2,1)} %get-tuple-element.39.dy_all, ...), custom_call_target="tpu_custom_call" | custom-call | tf_op jit(solution)/shard_map/pallas_call | solution.py:942
  227.1 138.3 %shard_map.239 = (bf16[256,1024]{1,0:T(8,128)(2,1)}, bf16[4,32,512]{2,1,0:T(8,128)(2,1)}, bf16[4,2,32,1152]{3,2,1,0:T(8,128)(2,1)}, f32[144,1024]{1,0:T(8,128)}, f32[32,1024]{1,0:T(8,128)}, /*index=5*/f32[8,1024]{1,0:T(8,128)}) custom-call(f32[256,1024]{1,0:T(8,128)} %get-tuple-element.44.dn2, f32[256,1024]{1,0:T(8,128)} %get-tuple-element.42.middle, ...), custom_call_target="tpu_custom_call" | custom-call | tf_op jit(solution)/shard_map/pallas_call | solution.py:958
  365.4 1.4 slice_bitcast_fusion
  366.8 1.4 fusion.2
  368.2 0.9 convert_bitcast_fusion
  369.5 0.7 copy.51
  370.2 0.7 reshape.173
  371.0 0.7 reshape.172
  371.7 1.2 reshape.175
  373.8 1.8 squeeze.18
  376.3 1.8 squeeze.17
  378.0 0.8 copy.58
  378.8 0.8 copy.59
  380.3 0.8 copy.61
  (37 shorter events, 6.5 us)
Async XLA Ops:
  0.6 10.2 %copy-start.5 = (bf16[32,4608]{1,0:T(8,128)(2,1)S(1)}, bf16[32,4608]{1,0:T(8,128)(2,1)}, u32[]{:S(2)}) copy-start(bf16[32,4608]{1,0:T(8,128)(2,1)} %param.21) | copy-start | bytes 884740
  0.7 9.2 %copy-start.4 = (bf16[32,4608]{1,0:T(8,128)(2,1)S(1)}, bf16[32,4608]{1,0:T(8,128)(2,1)}, u32[]{:S(2)}) copy-start(bf16[32,4608]{1,0:T(8,128)(2,1)} %param.20) | copy-start | bytes 884740
  365.4 6.3 %copy-start.1 = (bf16[4,2,32,1152]{3,2,1,0:T(8,128)(2,1)S(1)}, bf16[4,2,32,1152]{3,2,1,0:T(8,128)(2,1)}, u32[]{:S(2)}) copy-start(bf16[4,2,32,1152]{3,2,1,0:T(8,128)(2,1)} %get-tuple-element.60) | copy-start | bytes 1769476
  375.6 2.5 copy-start.2
  375.6 3.3 copy-start.3
  376.2 3.4 copy-start.6
  376.2 4.0 %copy-start = (f32[144,1024]{1,0:T(8,128)S(1)}, f32[144,1024]{1,0:T(8,128)}, u32[]{:S(2)}) copy-start(f32[144,1024]{1,0:T(8,128)} %get-tuple-element.94) | copy-start | bytes 1769476

commit v3 on v2

--- a/solution.py
+++ b/solution.py
@@ -2,6 +2,7 @@
 
 import jax
 import jax.numpy as jnp
+import numpy as np
 from jax import lax
 from jax.experimental import pallas as pl
 from jax.experimental.pallas import tpu as pltpu
@@ -14,6 +15,7 @@
 theta = 1000000.0
 VMEM = pl.BlockSpec(memory_space=pltpu.VMEM)
 ANY = pl.BlockSpec(memory_space=pl.ANY)
+SMEM = pl.BlockSpec(memory_space=pltpu.SMEM)
 
 
 def nn(left, right):
@@ -91,6 +93,10 @@
         return lax.rem(self.z + 4 - k, 4)
 
     def greet(self):
+        self.hello()
+        self.meet()
+
+    def hello(self):
         barrier = pltpu.get_barrier_semaphore()
         for k in (1, 2, 3):
             pl.semaphore_signal(
@@ -100,7 +106,9 @@
             pl.semaphore_signal(
                 barrier, inc=1, device_id=(lax.rem(self.s + k, 8), self.b), device_id_type=MESH
             )
-        pl.semaphore_wait(barrier, 10)
+
+    def meet(self):
+        pl.semaphore_wait(pltpu.get_barrier_semaphore(), 10)
 
     def slots(self, count):
         first = self.used
@@ -200,142 +208,180 @@
             sent(3)
 
 
+def heads_of(whole, kk):
+    return whole[:, 256 * kk : 256 * kk + 128], whole[:, 256 * kk + 128 : 256 * kk + 256]
+
+
+def pack_projections(w_query, key_weight, value_weight, out):
+    for c in range(4):
+        k = key_weight[:, 128 * c : 128 * c + 128].astype(F32)
+        v = value_weight[:, 128 * c : 128 * c + 128].astype(F32)
+        first = lanes(k.shape) < 64
+        pairs = (
+            jnp.where(first, k, pltpu.roll(v, 64, 1)),
+            jnp.where(first, pltpu.roll(k, 64, 1), v),
+        )
+        for kk in (0, 1):
+            h = 2 * c + kk
+            out[c, :, 256 * kk : 256 * kk + 128] = w_query[:, 128 * h : 128 * h + 128]
+            out[c, :, 256 * kk + 128 : 256 * kk + 256] = pairs[kk].astype(BF16)
+
+
+def pack_hidden(source, out, which):
+    wide = source[...].astype(F32)
+    for c in range(4):
+        pieces = [wide[:, 144 * (4 * i + c) : 144 * (4 * i + c) + 144] for i in range(8)]
+        out[c, which] = jnp.concatenate(pieces, axis=1).astype(BF16)
+
+
+def twice(v):
+    return jnp.concatenate([v[...], v[...]], axis=1)
+
+
+def near_first(p, t):
+    return jnp.where(t == 0, p.b, jnp.where(t == 1, p.core, jnp.where(t == 2, p.across, p.far)))
+
+
 def forward_kernel(
-    x, dy, length, wqkv_in, wgu_in, wd_in, wo_in, cos, sin, gain_q, gain_k, gain_a, gain_f,
-    wgu, wd, wo, wqkv, norm, pre, unit, unit_out, lse, mix, norm_two, middle, dy_all, length_all,
-    xa, pack, kv, vt, send_sem, recv_sem, local_sem,
+    x, dy, lengths, w_query, key_weight, value_weight, w_out, w_gate, w_up, w_down,
+    cos_table, sin_table, gain_query, gain_key, gain_a, gain_f,
+    output, dn2, ggu_out, gd_mine, gd_other, wo_out, wqkv_out, norm_out, unit_out_, lse_out, attn_out, mix_out,
+    middle, length_all,
+    xa, norm, wqkv, wo, pack, unit, unit_out, lse, kv, vt, mix, norm_two, dy_all, wgu, wd, gd,
+    hid, dgate, dup, parts_n, recv_n, parts_o, recv_o, keep_n, keep_o,
+    qkv_send, gu_send, length, cos, sin,
+    send_sem, recv_sem, local_sem,
 ):
     p = Place(send_sem, recv_sem, local_sem)
     s, b, z, y = p.s, p.b, p.z, p.y
     my_rows = pl.ds(pl.multiple_of(32 * b, 32), 32)
-    own = [
-        p.local(wqkv_in.at[b], wqkv.at[s, my_rows]),
-        p.local(x, xa.at[b]),
-        p.local(length, length_all.at[b]),
-        p.local(wo_in, wo.at[s, b]),
-    ]
-    own_gu = p.local(wgu_in.at[b], wgu.at[s, :, my_rows])
-    own_d = p.local(wd_in, wd.at[s])
+    my_positions = pl.ds(pl.multiple_of(256 * s, 256), 256)
+    p.hello()
+    own_d = p.local(w_down, wd.at[s])
+    own_x = p.local(x, xa.at[b])
+    own_wo = p.local(w_out, wo.at[s, b])
     own_dy = p.local(dy, dy_all.at[b])
-    p.greet()
-
-    got = []
+    own_tables = [p.local(cos_table.at[my_positions], cos), p.local(sin_table.at[my_positions], sin)]
+    pack_projections(w_query, key_weight, value_weight, qkv_send)
+    length[...] = jnp.broadcast_to(lengths[0], (8, 128)).astype(jnp.int32)
+    own_qkv = p.local(qkv_send.at[b], wqkv.at[s, my_rows])
+    length_all[b] = length[...]
+    p.meet()
+
+    got_qkv, got_len = [], []
     for k in (1, 2, 3):
         to = lax.rem(b + k, 4)
-        got.append(p.post(wqkv_in.at[to], wqkv.at[s, my_rows], (s, to)))
+        got_qkv.append(p.post(qkv_send.at[to], wqkv.at[s, my_rows], (s, to)))
+    x_across = p.post(x, xa.at[b], (s, p.across))
     x_core = p.post(x, xa.at[b], (s, p.core))
-    x_across = p.post(x, xa.at[b], (s, p.across))
-    got_len = []
     for k in (1, 2, 3):
         to = lax.rem(b + k, 4)
         got_len.append(p.post(length, length_all.at[b], (s, to)))
-    for made in own:
-        made.wait()
+    spread_d = Spread(p, lambda i: wd.at[i])
+    spread_g = Spread(p, lambda i: wgu.at[i, 0])
+    spread_u = Spread(p, lambda i: wgu.at[i, 1])
+    own_d.wait()
+    spread_d.start()
+    own_x.wait()
+
+    def normalize(g):
+        xg = xa[g].astype(F32)
+        norm[g] = (xg * rms_factor(xg) * gain_a[...]).astype(BF16)
+
+    normalize(b)
+    own_qkv.wait()
     for k in (1, 2, 3):
-        p.landed(got[k - 1], wqkv.at[s, my_rows])
+        p.landed(got_qkv[k - 1], wqkv.at[s, my_rows])
     z_qkv = [p.post(wqkv.at[s], wqkv.at[s], (2 * p.up(k) + y, b)) for k in (1, 2, 3)]
     y_qkv = [p.post(wqkv.at[s], wqkv.at[s], (p.flip, b))]
-    z_wo = [p.post(wo.at[s, b], wo.at[s, b], (2 * p.up(k) + y, b)) for k in (1, 2, 3)]
-    y_wo = [p.post(wo.at[s, b], wo.at[s, b], (p.flip, b))]
+    pack_hidden(w_gate, gu_send, 0)
+    pack_hidden(w_up, gu_send, 1)
+    own_gu = p.local(gu_send.at[b], wgu.at[s, :, my_rows])
     got_gu = []
     for k in (1, 2, 3):
         to = lax.rem(b + k, 4)
-        got_gu.append(p.post(wgu_in.at[to], wgu.at[s, :, my_rows], (s, to)))
-    p.landed(x_across, xa.at[p.across])
-    x_far = p.post(xa.at[p.across], xa.at[p.across], (s, p.core))
+        got_gu.append(p.post(gu_send.at[to], wgu.at[s, :, my_rows], (s, to)))
     for k in (1, 2, 3):
         slot = 2 * p.down(k) + y
         p.landed(z_qkv[k - 1], wqkv.at[slot])
         y_qkv.append(p.post(wqkv.at[slot], wqkv.at[slot], (p.flip, b)))
-    own_d.wait()
-    spread_d = Spread(p, lambda i: wd.at[i])
-    spread_g = Spread(p, lambda i: wgu.at[i, 0])
-    spread_u = Spread(p, lambda i: wgu.at[i, 1])
-    spread_d.start()
     p.landed(x_core, xa.at[p.core])
-    p.landed(x_far, xa.at[p.far])
-    for k in (1, 2, 3):
-        p.landed(got_len[k - 1], length_all.at[lax.rem(b + 4 - k, 4)])
-
-    def normalize(g, carry):
-        xg = xa[g].astype(F32)
-        norm[g] = (xg * rms_factor(xg) * gain_a[...]).astype(BF16)
-        return carry
-
-    lax.fori_loop(0, 4, normalize, 0)
+    normalize(p.core)
+    p.landed(x_across, xa.at[p.across])
+    x_far = p.post(xa.at[p.across], xa.at[p.across], (s, p.core))
+    for made in own_tables:
+        made.wait()
     p.landed(y_qkv[0], wqkv.at[p.flip])
     for k in (1, 2, 3):
         p.landed(y_qkv[k], wqkv.at[2 * p.down(k) + 1 - y])
-
-    own_gu.wait()
-    own_dy.wait()
-    for k in (1, 2, 3):
-        p.landed(got_gu[k - 1], wgu.at[s, :, my_rows])
-    spread_g.start()
-    spread_u.start()
+    kept = [p.local(wqkv, wqkv_out)]
+    gain_q, gain_k = twice(gain_query), twice(gain_key)
 
     first_unit = p.slots(8)
 
+    def each_piece(t, kk, act):
+        to = 2 * near_first(p, t) + kk
+
+        @pl.when(to != s)
+        def _():
+            act(p.copy(pack.at[to], unit.at[s], (to, b), first_unit + 2 * t + kk, first_unit + s))
+
     def project(t, carry):
-        g = lax.rem(z + 1 + t, 4)
+        g = near_first(p, t)
+
+        @pl.when(t == 3)
+        def _():
+            p.landed(x_far, xa.at[p.far])
+
+        @pl.when(t >= 2)
+        def _():
+            normalize(g)
+
         whole = nn(norm[g], wqkv[...].reshape(1024, 512))
-        pre[g] = whole
         for kk in (0, 1):
-            q = whole[:, 256 * kk : 256 * kk + 128]
-            kvp = whole[:, 256 * kk + 128 : 256 * kk + 256]
-            qn = q * lax.rsqrt(head_mean(q * q) + eps) * gain_q[...]
-            kn = kvp * lax.rsqrt(head_mean(kvp * kvp) + eps) * gain_k[...]
+            q, kvp = heads_of(whole, kk)
+            qn = q * lax.rsqrt(head_mean(q * q) + eps) * gain_q
+            kn = kvp * lax.rsqrt(head_mean(kvp * kvp) + eps) * gain_k
             qr = rope(qn, cos[...], sin[...]) * 0.125
             kr = rope(kn, cos[...], sin[...])
             pack[2 * g + kk, :, 0:128] = qr.astype(BF16)
             pack[2 * g + kk, :, 128:256] = jnp.where(lanes(kr.shape) < 64, kr, kvp).astype(BF16)
-
-        @pl.when(t < 3)
-        def _():
-            for kk in (0, 1):
-                to = 2 * g + kk
-                p.copy(
-                    pack.at[to], unit.at[s], (to, b), first_unit + 2 * t + kk, first_unit + 2 * t + y
-                ).start()
-
-        @pl.when(t == 3)
-        def _():
-            p.copy(pack.at[p.flip], unit.at[s], (p.flip, b), first_unit + 6).start()
+            each_piece(t, kk, lambda made: made.start())
+
+        @pl.when(t == 2)
+        def _():
+            spread_d.land(0)
+            spread_d.land_inner()
 
         return carry
 
     lax.fori_loop(0, 4, project, 0)
     own_unit = p.local(pack.at[s], unit.at[s])
-    spread_d.land(0)
-    spread_d.land_inner()
-
+    kept.append(p.local(norm, norm_out))
+    own_wo.wait()
+    z_wo = [p.post(wo.at[s, b], wo.at[s, b], (2 * p.up(k) + y, b)) for k in (1, 2, 3)]
+    y_wo = [p.post(wo.at[s, b], wo.at[s, b], (p.flip, b))]
+    spread_d.land_end()
+    own_dy.wait()
+    dy_across = p.post(dy, dy_all.at[b], (s, p.across))
+    dy_core = p.post(dy, dy_all.at[b], (s, p.core))
+    for k in (1, 2, 3):
+        p.landed(got_len[k - 1], length_all.at[lax.rem(b + 4 - k, 4)])
+
+    for k in range(1, 8):
+        src = lax.rem(s + k, 8)
+        p.landed(first_unit + src, unit.at[src])
+    own_unit.wait()
+    kept.append(p.local(unit, unit_out_))
+    own_gu.wait()
+    for k in (1, 2, 3):
+        p.landed(got_gu[k - 1], wgu.at[s, :, my_rows])
+    spread_g.start()
+    spread_u.send(s, (p.flip, b), 4, 3)
     for k in (1, 2, 3):
         slot = 2 * p.down(k) + y
         p.landed(z_wo[k - 1], wo.at[slot, b])
         y_wo.append(p.post(wo.at[slot, b], wo.at[slot, b], (p.flip, b)))
-    dy_core = p.post(dy, dy_all.at[b], (s, p.core))
-    dy_across = p.post(dy, dy_all.at[b], (s, p.across))
-    p.landed(y_wo[0], wo.at[p.flip, b])
-    for k in (1, 2, 3):
-        p.landed(y_wo[k], wo.at[2 * p.down(k) + 1 - y, b])
-    wo_core = p.post(wo.at[:, b], wo.at[:, b], (s, p.core))
-    wo_across = p.post(wo.at[:, b], wo.at[:, b], (s, p.across))
-    spread_d.land_end()
-    spread_g.land(0)
-    spread_u.land(0)
-    spread_g.land_inner()
-    spread_u.land_inner()
-
-    for t in range(3):
-        for other in (0, 1):
-            src = 2 * lax.rem(z + 3 - t, 4) + other
-            p.landed(first_unit + 2 * t + other, unit.at[src])
-    p.landed(first_unit + 6, unit.at[p.flip])
-    own_unit.wait()
-    for t in range(3):
-        for kk in (0, 1):
-            p.copy(pack.at[s], unit.at[s], (p.flip, b), first_unit + 2 * t + kk).wait_send()
-    p.copy(pack.at[s], unit.at[s], (p.flip, b), first_unit + 6).wait_send()
 
     def prepare(j, carry):
         live = j * 256 + rows_of((256, 128)) < length_all[z][0:1, :]
@@ -347,10 +393,13 @@
         return carry
 
     lax.fori_loop(0, 8, prepare, 0)
-    p.landed(wo_across, wo.at[:, p.across])
-    wo_far = p.post(wo.at[:, p.across], wo.at[:, p.across], (s, p.core))
     p.landed(dy_across, dy_all.at[p.across])
     dy_far = p.post(dy_all.at[p.across], dy_all.at[p.across], (s, p.core))
+    p.landed(y_wo[0], wo.at[p.flip, b])
+    for k in (1, 2, 3):
+        p.landed(y_wo[k], wo.at[2 * p.down(k) + 1 - y, b])
+    wo_across = p.post(wo.at[:, b], wo.at[:, b], (s, p.across))
+    wo_core = p.post(wo.at[:, b], wo.at[:, b], (s, p.core))
     first_mix, first_across, first_core = p.slots(8), p.slots(8), p.slots(8)
 
     def mix_send(src, t):
@@ -385,13 +434,16 @@
         def _():
             p.copy(unit_out.at[i], mix.at[b, s], (i, b), first_mix + t).start()
 
-        @pl.when(t == 2)
+        @pl.when(t == 3)
+        def _():
+            spread_g.land(0)
+            spread_g.land_inner()
+            spread_u.send(s, (2 * p.pair + y, b), 0, 0)
+            spread_u.send(s, (2 * p.there + y, b), 1, jnp.where(p.inner, 1, 2))
+
+        @pl.when(t == 6)
         def _():
             spread_g.land_end()
-
-        @pl.when(t == 4)
-        def _():
-            spread_u.land_end()
 
         @pl.when(t >= 4)
         def _():
@@ -401,24 +453,27 @@
 
     lax.fori_loop(0, 8, attend, 0)
     own_mix = p.local(unit_out.at[s], mix.at[b, s])
+    kept.append(p.local(unit_out, attn_out))
+    kept.append(p.local(lse, lse_out))
     own_mix.wait()
     mix_send(s, 7)
     for t in range(4, 7):
         mix_arrived(t)
-    for t in range(7):
-        p.copy(unit_out.at[s], mix.at[b, s], (p.flip, b), first_mix + t).wait_send()
-    p.landed(wo_core, wo.at[:, p.core])
-    p.landed(wo_far, wo.at[:, p.far])
-    p.landed(dy_core, dy_all.at[p.core])
-    p.landed(dy_far, dy_all.at[p.far])
+    spread_u.land(0)
+    spread_u.land_inner()
+    p.landed(wo_across, wo.at[:, p.across])
+    wo_far = p.post(wo.at[:, p.across], wo.at[:, p.across], (s, p.core))
     for t in range(8):
         p.landed(first_across + t, mix.at[p.across, lax.rem(s + 7 - t, 8)])
     mix_far = p.post(mix.at[p.across], mix.at[p.across], (s, p.core))
     for t in range(8):
         p.landed(first_core + t, mix.at[p.core, lax.rem(s + 7 - t, 8)])
-        p.copy(mix.at[b, s], mix.at[b, s], (s, p.across), first_across + t).wait_send()
-        p.copy(mix.at[b, s], mix.at[b, s], (s, p.core), first_core + t).wait_send()
+    p.landed(wo_core, wo.at[:, p.core])
+    p.landed(wo_far, wo.at[:, p.far])
+    kept.append(p.local(wo, wo_out))
+    spread_u.land_end()
     p.landed(mix_far, mix.at[p.far])
+    kept.append(p.local(mix, mix_out))
 
     def project_out(g, carry):
         mixed = jnp.concatenate([mix[c, 2 * g + kk] for c in range(4) for kk in (0, 1)], axis=1)
@@ -432,47 +487,11 @@
         return carry
 
     lax.fori_loop(0, 4, project_out, 0)
+    p.landed(dy_core, dy_all.at[p.core])
+    p.landed(dy_far, dy_all.at[p.far])
     for spread in (spread_d, spread_g, spread_u):
         spread.finish()
-        spread.drain()
-    p.drain()
-
-
-def chip_sum_post(p, t, parts, recv, first):
-    @pl.when(t == 0)
-    def _():
-        p.copy(parts.at[p.far], recv.at[0], (p.s, p.core), first).start()
-
-    @pl.when(t == 1)
-    def _():
-        p.copy(parts.at[p.core], recv.at[1], (p.s, p.core), first + 1).start()
-
-
-def chip_sum_across(p, parts, recv, first):
-    p.copy(recv.at[0], recv.at[0], (p.s, p.core), first).wait_recv()
-    parts[p.across] = (parts[p.across].astype(F32) + recv[0].astype(F32)).astype(BF16)
-    p.copy(parts.at[p.across], recv.at[2], (p.s, p.across), first + 2).start()
-
-
-def chip_sum_rest(p, parts, recv, first):
-    p.copy(recv.at[1], recv.at[1], (p.s, p.core), first + 1).wait_recv()
-    p.copy(recv.at[2], recv.at[2], (p.s, p.core), first + 2).wait_recv()
-    for k in range(3):
-        p.copy(parts.at[p.b], recv.at[k], (p.s, p.core), first + k).wait_send()
-    return recv[1].astype(F32) + recv[2].astype(F32)
-
-
-def batch_order(p, t):
-    return jnp.where(t == 0, p.far, jnp.where(t == 1, p.core, jnp.where(t == 2, p.across, p.b)))
-
-
-def feed_kernel(
-    norm_two, dy_all, wgu, wd, middle,
-    output, dn2, ggu, gd, gd_other,
-    hid, dgate, dup, parts_n, recv_n, parts_o, recv_o, keep_n, keep_o, send_sem, recv_sem, local_sem,
-):
-    p = Place(send_sem, recv_sem, local_sem)
-    p.greet()
+
     first_n, first_o = p.slots(3), p.slots(3)
 
     def gated(t, carry):
@@ -510,8 +529,10 @@
     lax.fori_loop(0, 9, down_rows, 0)
     sent_d = []
     for i in range(4):
-        rows = pl.ds(pl.multiple_of(144 * (2 * i + 1 - p.y), 16), 144)
-        sent_d.append(p.post(gd.at[rows], gd_other.at[i], (p.flip, p.b)))
+        other = pl.ds(pl.multiple_of(144 * (2 * i + 1 - y), 16), 144)
+        mine = pl.ds(pl.multiple_of(144 * (2 * i + y), 16), 144)
+        sent_d.append(p.post(gd.at[other], gd_other.at[i], (p.flip, b)))
+        kept.append(p.local(gd.at[mine], gd_mine.at[i]))
 
     def down(t, carry):
         g = batch_order(p, t)
@@ -527,21 +548,62 @@
 
     lax.fori_loop(0, 4, down, 0)
     chip_sum_across(p, parts_o, recv_o, first_o)
+    for spread in (spread_d, spread_g, spread_u):
+        spread.drain()
 
     def gate_rows(c, carry):
         at = pl.multiple_of(128 * c, 128)
         left = norm_two[:, :, pl.ds(at, 128)].reshape(1024, 128)
-        ggu[c, 0] = tn(left, dgate[...]).astype(BF16)
-        ggu[c, 1] = tn(left, dup[...]).astype(BF16)
+        wgu[c, 0] = tn(left, dgate[...]).astype(BF16)
+        wgu[c, 1] = tn(left, dup[...]).astype(BF16)
         return carry
 
     lax.fori_loop(0, 8, gate_rows, 0)
+    kept.append(p.local(wgu, ggu_out))
     dn2[...] = keep_n[...] + chip_sum_rest(p, parts_n, recv_n, first_n)
     total = keep_o[...] + chip_sum_rest(p, parts_o, recv_o, first_o)
     output[...] = (middle[...] + total).astype(BF16)
     for i in range(4):
         p.landed(sent_d[i], gd_other.at[i])
+    for t in range(8):
+        if t < 7:
+            p.copy(unit_out.at[s], mix.at[b, s], (p.flip, b), first_mix + t).wait_send()
+        p.copy(mix.at[b, s], mix.at[b, s], (s, p.across), first_across + t).wait_send()
+        p.copy(mix.at[b, s], mix.at[b, s], (s, p.core), first_core + t).wait_send()
+    for t in range(4):
+        for kk in (0, 1):
+            each_piece(t, kk, lambda made: made.wait_send())
+    for made in kept:
+        made.wait()
     p.drain()
+
+
+def chip_sum_post(p, t, parts, recv, first):
+    @pl.when(t == 0)
+    def _():
+        p.copy(parts.at[p.far], recv.at[0], (p.s, p.core), first).start()
+
+    @pl.when(t == 1)
+    def _():
+        p.copy(parts.at[p.core], recv.at[1], (p.s, p.core), first + 1).start()
+
+
+def chip_sum_across(p, parts, recv, first):
+    p.copy(recv.at[0], recv.at[0], (p.s, p.core), first).wait_recv()
+    parts[p.across] = (parts[p.across].astype(F32) + recv[0].astype(F32)).astype(BF16)
+    p.copy(parts.at[p.across], recv.at[2], (p.s, p.across), first + 2).start()
+
+
+def chip_sum_rest(p, parts, recv, first):
+    p.copy(recv.at[1], recv.at[1], (p.s, p.core), first + 1).wait_recv()
+    p.copy(recv.at[2], recv.at[2], (p.s, p.core), first + 2).wait_recv()
+    for k in range(3):
+        p.copy(parts.at[p.b], recv.at[k], (p.s, p.core), first + k).wait_send()
+    return recv[1].astype(F32) + recv[2].astype(F32)
+
+
+def batch_order(p, t):
+    return jnp.where(t == 0, p.far, jnp.where(t == 1, p.core, jnp.where(t == 2, p.across, p.b)))
 
 
 class SeqTree:
@@ -551,10 +613,10 @@
         self.first = p.slots(6)
         self.started = False
 
-    def start(self):
+    def start(self, source):
         p = self.p
         self.started = True
-        p.copy(self.mine.at[:, 1 - p.y], self.y_recv, (p.flip, p.b), self.first + 4).start()
+        p.copy(source, self.y_recv, (p.flip, p.b), self.first + 4).start()
 
     def send(self, i, dst, z, out, into):
         p = self.p
@@ -566,7 +628,7 @@
             p.landed(self.first + 4, self.y_recv)
 
         def add(i):
-            self.sums[i] = (self.y_recv[i].astype(F32) + self.mine[i, p.y].astype(F32)).astype(BF16)
+            self.sums[i] = (self.y_recv[i].astype(F32) + self.mine[i].astype(F32)).astype(BF16)
 
         add(p.there)
         add(p.beyond)
@@ -591,7 +653,7 @@
 
     def finish(self):
         p = self.p
-        total = self.y_recv[p.z].astype(F32) + self.mine[p.z, p.y].astype(F32)
+        total = self.y_recv[p.z].astype(F32) + self.mine[p.z].astype(F32)
         p.landed(self.first, self.z_recv.at[0])
         total = total + self.z_recv[0].astype(F32)
         p.landed(self.first + 3, self.z_recv.at[1])
@@ -637,10 +699,11 @@
 
 
 def backward_kernel(
-    dn2, middle, x, dy, wo, mix, unit, unit_out, lse, length_all, pre, norm, wqkv,
-    cos, sin, gain_q, gain_k, gain_a, gain_f, ggu, gd, y_d,
+    dn2, middle, x, dy, wo_in, mix_in, unit_in, attn_in, lse_in, length_all, norm_in, wqkv_in,
+    cos_table, sin_table, gain_query, gain_key, gain_a, gain_f, ggu, gd, y_d,
     dx, rqkv, rgu, rd, ro, gains_out,
-    dmid, dox, doq, dou, dbr, kv, kt, q_right, do_right, q_left, do_left, delta, dk2, dv2, back, dqr,
+    wo, mix, unit, unit_out, lse, norm, wqkv, cos, sin, m_g, m_u,
+    dmid, dox, doq, dou, dbr, kv, kt, delta, dk2, dv2, back, dqr,
     dpre, parts, recv, keep, gqkv, go, mixt,
     s_d, t_d, z_d, y_g, t_g, z_g, y_u, t_u, z_u, y_q, z_q, y_o, z_o, fin_g, fin_u, fin_q,
     gain_sum, gain_batch, gain_seq,
@@ -648,11 +711,23 @@
 ):
     p = Place(send_sem, recv_sem, local_sem)
     s, b, z, y = p.s, p.b, p.z, p.y
-    p.greet()
+    p.hello()
+    my_positions = pl.ds(pl.multiple_of(256 * s, 256), 256)
+    load_wo = p.local(wo_in, wo)
+    load_unit = p.local(unit_in, unit)
+    load_more = [p.local(attn_in, unit_out), p.local(lse_in, lse)]
+    load_g = p.local(ggu.at[:, y, 0], m_g)
+    load_u = p.local(ggu.at[:, y, 1], m_u)
+    load_mix = p.local(mix_in, mix)
+    load_last = [
+        p.local(norm_in, norm), p.local(wqkv_in, wqkv),
+        p.local(cos_table.at[my_positions], cos), p.local(sin_table.at[my_positions], sin),
+    ]
+    p.meet()
     sum_d = SeqTree(p, gd, y_d, t_d, z_d, s_d)
-    sum_g = SeqTree(p, ggu.at[:, :, 0], y_g, t_g, z_g)
-    sum_u = SeqTree(p, ggu.at[:, :, 1], y_u, t_u, z_u)
-    sum_g.start()
+    sum_g = SeqTree(p, m_g, y_g, t_g, z_g)
+    sum_u = SeqTree(p, m_u, y_u, t_u, z_u)
+    sum_g.start(ggu.at[:, 1 - y, 0])
     sum_d.reduce()
 
     mid = middle[...]
@@ -663,6 +738,7 @@
     dm = dy[...].astype(F32) + norm_back(grad_two * gain_f[...], mid, r2)
     dmid[...] = dm
     dbr[b] = dm.astype(BF16)
+    load_wo.wait()
     for c in range(4):
         for kk in (0, 1):
             h = 2 * c + kk
@@ -681,19 +757,13 @@
         to = lax.rem(s + k, 8)
         got_unit.append(p.post(doq.at[to], dou.at[s], (to, b)))
     dou[s] = doq[s]
+    load_unit.wait()
 
     def prepare(i, carry):
         live = i * 256 + rows_of((256, 128)) < length_all[z][0:1, :]
         masked = jnp.where(live, unit[i, :, 128:256].astype(F32), 0.0)
         kv[i] = masked.astype(BF16)
         kt[i] = jnp.transpose(masked)[0:64].astype(BF16)
-        q = unit[i, :, 0:128].astype(F32)
-        qt = jnp.transpose(q).astype(BF16)
-        q_right[i, 0:64] = jnp.concatenate([qt[0:64], qt[64:128]], axis=1)
-        q_right[i, 64:128] = jnp.zeros((64, 512), BF16)
-        first = lanes(q.shape) < 64
-        q_left[i, 0:256] = jnp.where(first, q, 0.0).astype(BF16)
-        q_left[i, 256:512] = jnp.where(first, 0.0, q).astype(BF16)
         dk2[i] = jnp.zeros((256, 128), F32)
         dv2[i] = jnp.zeros((256, 128), F32)
         return carry
@@ -705,27 +775,25 @@
     for k in range(1, 8):
         p.landed(got_unit[k - 1], dou.at[lax.rem(s + 8 - k, 8)])
 
-    def prepare_grad(i, carry):
-        do = dou[i].astype(F32)
-        dot = jnp.transpose(do)
-        do_right[i, 0:64] = jnp.zeros((64, 512), BF16)
-        do_right[i, 64:128] = jnp.concatenate([dot[0:64], dot[64:128]], axis=1).astype(BF16)
-        first = lanes(do.shape) < 64
-        do_left[i, 0:256] = jnp.where(first, do, 0.0).astype(BF16)
-        do_left[i, 256:512] = jnp.where(first, 0.0, do).astype(BF16)
+    for made in load_more:
+        made.wait()
+
+    def queries(t, carry):
+        i = 7 - t
+        q, do = unit[i, :, 0:128].astype(F32), dou[i].astype(F32)
+        qt, dot = jnp.transpose(q).astype(BF16), jnp.transpose(do)
+        first = lanes(q.shape) < 64
+        blank = jnp.zeros((64, 512), BF16)
+        qr = jnp.concatenate([jnp.concatenate([qt[0:64], qt[64:128]], axis=1), blank], axis=0)
+        dr = jnp.concatenate([dot[0:64], dot[64:128]], axis=1).astype(BF16)
+        dr = jnp.concatenate([blank, dr], axis=0)
+        ql = jnp.concatenate([jnp.where(first, q, 0.0), jnp.where(first, 0.0, q)], axis=0).astype(BF16)
+        dl = jnp.concatenate([jnp.where(first, do, 0.0), jnp.where(first, 0.0, do)], axis=0).astype(BF16)
         both = dot * jnp.transpose(unit_out[i].astype(F32))
         low = jnp.sum(both[0:64], axis=0, keepdims=True)
         high = jnp.sum(both[64:128], axis=0, keepdims=True)
-        delta[i] = jnp.broadcast_to(jnp.concatenate([low, high], axis=1), (8, 512))
-        return carry
-
-    lax.fori_loop(0, 8, prepare_grad, 0)
-
-    def queries(t, carry):
-        i = 7 - t
-        qr, dr, ql, dl = q_right[i], do_right[i], q_left[i], do_left[i]
+        shift = jnp.concatenate([low, high], axis=1)
         log_total = lse[i][0:1]
-        shift = delta[i][0:1]
 
         def block(j, probs):
             ds = (probs * (nn(kv[j], dr) - shift)).astype(BF16)
@@ -750,8 +818,9 @@
         return carry
 
     lax.fori_loop(0, 1, queries, 0)
+    load_g.wait()
     sum_g.reduce()
-    sum_u.start()
+    sum_u.start(ggu.at[:, 1 - y, 1])
     lax.fori_loop(1, 4, queries, 0)
     sum_g.relay()
     lax.fori_loop(4, 8, queries, 0)
@@ -764,6 +833,8 @@
     p.landed(dbr_core, dbr.at[p.core])
     p.landed(dbr_far, dbr.at[p.far])
 
+    load_mix.wait()
+
     def turn(e, carry):
         for g in range(4):
             mixt[:, 256 * g : 256 * g + 256] = jnp.transpose(
@@ -776,7 +847,11 @@
     lax.fori_loop(0, 8, turn, 0)
     sum_o = SeqSum(p, y_o, z_o)
     sum_o.start(go)
+    load_u.wait()
     sum_u.reduce()
+    for made in load_last:
+        made.wait()
+    gain_q, gain_k = twice(gain_query), twice(gain_key)
     for k in range(1, 8):
         p.landed(got_back[k - 1], dqr.at[lax.rem(s + 8 - k, 8)])
 
@@ -786,9 +861,10 @@
     def heads(t, carry):
         sum_q, sum_k = carry
         g = batch_order(p, t)
+        whole = nn(norm[g], wqkv[...].reshape(1024, 512))
         for kk in (0, 1):
             at = 256 * kk
-            q, k = pre[g, :, at : at + 128], pre[g, :, at + 128 : at + 256]
+            q, k = heads_of(whole, kk)
             rq = lax.rsqrt(head_mean(q * q) + eps)
             rk = lax.rsqrt(head_mean(k * k) + eps)
             dq = rope_back(dqr[2 * g + kk, :, 0:128].astype(F32), cos[...], sin[...])
@@ -796,8 +872,8 @@
             dk = rope_back(dkv, cos[...], sin[...])
             sum_q = sum_q + jnp.sum(dq * q * rq, axis=0, keepdims=True)
             sum_k = sum_k + jnp.sum(dk * k * rk, axis=0, keepdims=True)
-            dq = dq * gain_q[...]
-            dk = dk * gain_k[...]
+            dq = dq * gain_q
+            dk = dk * gain_k
             dq = rq * (dq - q * rq * rq * head_mean(dq * q))
             dk = rk * (dk - k * rk * rk * head_mean(dk * k))
             dpre[g, :, at : at + 128] = dq.astype(BF16)
@@ -875,7 +951,37 @@
     p.drain()
 
 
-def call(kernel, outs, in_specs, out_specs, scratch, cid, sems=(64, 16)):
+def finish_kernel(
+    output, dx, rqkv, rgu, rd, ro, gains,
+    output_, dx_, grad_query, grad_key, grad_value, grad_out, grad_gate, grad_up, grad_down,
+    gain_attn, gain_ffn, gain_query, gain_key,
+):
+    output_[...] = output[...]
+    dx_[...] = dx[...]
+    grad_out[...] = ro[...]
+    grad_down[...] = rd[...]
+    for c in range(4):
+        pairs = []
+        for kk in (0, 1):
+            h = 2 * c + kk
+            q, kv = heads_of(rqkv[c].astype(F32), kk)
+            grad_query[:, 128 * h : 128 * h + 128] = q
+            pairs.append(kv)
+        first = lanes(pairs[0].shape) < 64
+        grad_key[:, 128 * c : 128 * c + 128] = jnp.where(first, pairs[0], pltpu.roll(pairs[1], 64, 1))
+        grad_value[:, 128 * c : 128 * c + 128] = jnp.where(first, pltpu.roll(pairs[0], 64, 1), pairs[1])
+    for which, out in ((0, grad_gate), (1, grad_up)):
+        wide = [rgu[c, which].astype(F32) for c in range(4)]
+        out[...] = jnp.concatenate(
+            [wide[c][:, 144 * i : 144 * i + 144] for i in range(8) for c in range(4)], axis=1
+        )
+    gain_attn[...] = gains[0:1]
+    gain_ffn[...] = gains[1:2]
+    gain_query[...] = gains[2:3, 0:64] + gains[2:3, 64:128]
+    gain_key[...] = gains[3:4, 0:64]
+
+
+def call(kernel, outs, in_specs, out_specs, scratch, cid, sems):
     return pl.pallas_call(
         kernel,
         out_shape=[jax.ShapeDtypeStruct(shape, dtype) for shape, dtype in outs],
@@ -899,74 +1005,53 @@
 ):
     x = inputs.reshape(256, 1024)
     dy = cotangent.reshape(256, 1024)
-    positions = lax.axis_index("seq") * 256 + jnp.arange(256, dtype=jnp.int32)
-    freqs = theta ** (-(jnp.arange(32, dtype=F32) * 2.0) / 64)
-    angles = positions.astype(F32)[:, None] * freqs[None, :]
-    cosine = jnp.tile(jnp.cos(angles), (1, 4))
-    sine = jnp.tile(jnp.sin(angles), (1, 4))
-    length = jnp.broadcast_to(lengths[:, None], (8, 128))
-    wqkv_in = jnp.concatenate(
-        [
-            w_query.reshape(32, 4, 2, 128),
-            key_weight.reshape(32, 4, 2, 64),
-            value_weight.reshape(32, 4, 2, 64),
-        ],
-        axis=-1,
-    )
-    wqkv_in = jnp.transpose(wqkv_in.reshape(32, 4, 512), (1, 0, 2))
-    wgu_in = jnp.stack([w_gate, w_up]).reshape(2, 32, 8, 4, 144)
-    wgu_in = jnp.transpose(wgu_in, (3, 0, 1, 2, 4)).reshape(4, 2, 32, 1152)
-    gain_q = jnp.tile(gain_query, 2)[None]
-    gain_k = jnp.tile(gain_key, 2)[None]
-    gain_a = gain_attn[None]
-    gain_f = gain_ffn[None]
-
-    (wgu, wd, wo, wqkv, norm, pre, unit, unit_out, lse, mix, norm_two, middle, dy_all, length_all) = call(
+    freqs = theta ** (-(np.arange(32, dtype=np.float32) * 2.0) / 64)
+    angles = np.arange(2048, dtype=np.float32)[:, None] * freqs.astype(np.float32)[None, :]
+    cosine = jnp.asarray(np.tile(np.cos(angles), (1, 4)), F32)
+    sine = jnp.asarray(np.tile(np.sin(angles), (1, 4)), F32)
+    gains = [g[None] for g in (gain_query, gain_key, gain_attn, gain_ffn)]
+
+    (
+        output, dn2, ggu, gd_mine, gd_other, wo, wqkv, norm, unit, lse, unit_out, mix, middle, length_all,
+    ) = call(
         forward_kernel,
         [
-            ((8, 2, 128, 1152), BF16), ((8, 144, 1024), BF16), ((8, 4, 32, 1024), BF16),
-            ((8, 128, 512), BF16), ((4, 256, 1024), BF16), ((4, 256, 512), F32),
-            ((8, 256, 256), BF16), ((8, 256, 128), BF16), ((8, 8, 512), F32),
-            ((4, 8, 256, 128), BF16), ((4, 256, 1024), BF16), ((256, 1024), F32),
-            ((4, 256, 1024), BF16), ((4, 8, 128), jnp.int32),
+            ((256, 1024), BF16), ((256, 1024), F32), ((8, 2, 128, 1152), BF16), ((4, 144, 1024), BF16),
+            ((4, 144, 1024), BF16), ((8, 4, 32, 1024), BF16), ((8, 128, 512), BF16),
+            ((4, 256, 1024), BF16), ((8, 256, 256), BF16), ((8, 8, 512), F32), ((8, 256, 128), BF16),
+            ((4, 8, 256, 128), BF16), ((256, 1024), F32), ((4, 8, 128), jnp.int32),
         ],
-        [VMEM, ANY, VMEM, VMEM, ANY, ANY, VMEM] + [VMEM] * 6,
-        [ANY, ANY] + [VMEM] * 10 + [ANY, VMEM],
+        [VMEM, VMEM, SMEM] + [VMEM] * 6 + [ANY] * 3 + [VMEM] * 4,
+        [VMEM, VMEM, ANY, ANY, VMEM] + [ANY] * 7 + [VMEM] * 2,
         [
-            ((4, 256, 1024), BF16), ((8, 256, 256), BF16), ((8, 256, 128), BF16), ((8, 80, 256), BF16),
-        ],
-        0,
-        sems=(128, 16),
-    )(x, dy, length, wqkv_in, wgu_in, w_down, w_out, cosine, sine, gain_q, gain_k, gain_a, gain_f)
-
-    output, dn2, ggu, gd, gd_other = call(
-        feed_kernel,
-        [
-            ((256, 1024), BF16), ((256, 1024), F32), ((8, 2, 128, 1152), BF16), ((1152, 1024), BF16),
-            ((4, 144, 1024), BF16),
-        ],
-        [VMEM] * 5,
-        [VMEM] * 5,
-        [
+            ((4, 256, 1024), BF16), ((4, 256, 1024), BF16), ((8, 128, 512), BF16), ((8, 4, 32, 1024), BF16),
+            ((8, 256, 256), BF16), ((8, 256, 256), BF16), ((8, 256, 128), BF16), ((8, 8, 512), F32),
+            ((8, 256, 128), BF16), ((8, 80, 256), BF16), ((4, 8, 256, 128), BF16), ((4, 256, 1024), BF16),
+            ((4, 256, 1024), BF16), ((8, 2, 128, 1152), BF16), ((8, 144, 1024), BF16), ((1152, 1024), BF16),
             ((1024, 1152), BF16), ((1024, 1152), BF16), ((1024, 1152), BF16),
             ((4, 256, 1024), BF16), ((3, 256, 1024), BF16), ((4, 256, 1024), BF16),
             ((3, 256, 1024), BF16), ((256, 1024), F32), ((256, 1024), F32),
+            ((4, 32, 512), BF16), ((4, 2, 32, 1152), BF16), ((8, 128), jnp.int32),
+            ((256, 128), F32), ((256, 128), F32),
         ],
-        1,
-    )(norm_two, dy_all, wgu, wd, middle)
-
-    dx, rqkv, rgu, rd, ro, gains = call(
+        0,
+        (128, 32),
+    )(x, dy, lengths, w_query, key_weight, value_weight, w_out, w_gate, w_up, w_down, cosine, sine, *gains)
+
+    raw = call(
         backward_kernel,
         [
             ((256, 1024), BF16), ((4, 32, 512), BF16), ((4, 2, 32, 1152), BF16),
             ((144, 1024), F32), ((32, 1024), F32), ((8, 1024), F32),
         ],
-        [VMEM] * 22,
+        [VMEM] * 4 + [ANY] * 5 + [VMEM] + [ANY] * 4 + [VMEM] * 4 + [ANY, VMEM, VMEM],
         [VMEM] * 6,
         [
+            ((8, 4, 32, 1024), BF16), ((4, 8, 256, 128), BF16), ((8, 256, 256), BF16), ((8, 256, 128), BF16),
+            ((8, 8, 512), F32), ((4, 256, 1024), BF16), ((8, 128, 512), BF16), ((256, 128), F32),
+            ((256, 128), F32), ((4, 128, 1152), BF16), ((4, 128, 1152), BF16),
             ((256, 1024), F32), ((4, 2, 256, 128), BF16), ((8, 256, 128), BF16), ((8, 256, 128), BF16),
-            ((4, 256, 1024), BF16), ((8, 256, 128), BF16), ((8, 64, 256), BF16), ((8, 128, 512), BF16),
-            ((8, 128, 512), BF16), ((8, 512, 128), BF16), ((8, 512, 128), BF16), ((8, 8, 512), F32),
+            ((4, 256, 1024), BF16), ((8, 256, 128), BF16), ((8, 64, 256), BF16), ((8, 8, 512), F32),
             ((8, 256, 128), F32), ((8, 256, 128), F32), ((8, 256, 256), BF16), ((8, 256, 256), BF16),
             ((4, 256, 512), BF16), ((4, 256, 1024), BF16), ((3, 256, 1024), BF16), ((256, 1024), F32),
             ((4, 2, 128, 512), BF16), ((4, 2, 32, 1024), BF16), ((128, 1024), BF16),
@@ -977,33 +1062,27 @@
             ((128, 1152), BF16), ((128, 1152), BF16), ((128, 512), BF16),
             ((8, 1024), F32), ((4, 8, 1024), F32), ((8, 8, 1024), F32),
         ],
-        2,
-        sems=(96, 16),
+        1,
+        (96, 32),
     )(
-        dn2, middle, x, dy, wo, mix, unit, unit_out, lse, length_all, pre, norm, wqkv,
-        cosine, sine, gain_q, gain_k, gain_a, gain_f,
-        ggu.reshape(4, 2, 2, 128, 1152), gd.reshape(4, 2, 144, 1024), gd_other,
-    )
-
-    rows = jnp.transpose(rqkv, (1, 0, 2)).reshape(32, 8, 256).astype(F32)
-    grad_query = rows[:, :, 0:128].reshape(32, 1024)
-    grad_key = rows[:, :, 128:192].reshape(32, 512)
-    grad_value = rows[:, :, 192:256].reshape(32, 512)
-    wide = jnp.transpose(rgu.reshape(4, 2, 32, 8, 144), (1, 2, 3, 0, 4)).reshape(2, 32, 4608).astype(F32)
+        dn2, middle, x, dy, wo, mix, unit, unit_out, lse, length_all, norm, wqkv,
+        cosine, sine, *gains, ggu.reshape(4, 2, 2, 128, 1152), gd_mine, gd_other,
+    )
+    done = pl.pallas_call(
+        finish_kernel,
+        out_shape=[
+            jax.ShapeDtypeStruct(shape, dtype)
+            for shape, dtype in (
+                ((256, 1024), BF16), ((256, 1024), BF16), ((32, 1024), F32), ((32, 512), F32),
+                ((32, 512), F32), ((32, 1024), F32), ((32, 4608), F32), ((32, 4608), F32),
+                ((144, 1024), F32), ((1, 1024), F32), ((1, 1024), F32), ((1, 64), F32), ((1, 64), F32),
+            )
+        ],
+        in_specs=[VMEM] * 7,
+        out_specs=[VMEM] * 13,
+    )(output, *raw)
     return (
-        output.reshape(256, 1, 1024),
-        dx.reshape(256, 1, 1024),
-        grad_query,
-        grad_key,
-        grad_value,
-        ro,
-        wide[0],
-        wide[1],
-        rd,
-        gains[0],
-        gains[1],
-        gains[2, 0:64] + gains[2, 64:128],
-        gains[3, 0:64],
+        done[0].reshape(256, 1, 1024), done[1].reshape(256, 1, 1024), *done[2:9], *[g[0] for g in done[9:]],
     )
 
 

time: 386 us -> 330 us (0.85)
  Pallas kernels: 352 us -> 324 us
  local copies, waits for them, and re-layouts: 25 us -> 0 us
    pallas_call x2, Pallas kernels: 213 us -> 197 us  [the longest x1 193 us: body(): call(forward_kernel, [((256, 1024), BF16), ((256, 1024), F32), ((8, 2, 12...]
    pallas_call x1, Pallas kernels: 138 us -> 127 us  [body(): call(backward_kernel, [((256, 1024), BF16), ((4, 32, 512), BF16), ((4, 2,...]
    reshape x8 -> x0, local copies, waits for them, and re-layouts: 6.63 us -> none  [the longest x1 1.81 us: body(): wgu_in = jnp.transpose(wgu_in, (3, 0, 1, 2, 4)).reshape(4, 2, 32, 1152)]
    another operation x12 -> x0, local copies, waits for them, and re-layouts: 5.89 us -> none  [the longest x4 1.86 us: body(): wgu_in = jnp.stack([w_gate, w_up]).reshape(2, 32, 8, 4, 144)]
where the time goes in v3:
time: 330 us; the launch traced here: 326 us
  Pallas kernels  324 us (98%)
    pallas_call x1, Pallas kernels, body(): call(forward_kernel, [((256, 1024), BF16), ((256, 1024), F32), ((8, 2, 12...  193 us
    pallas_call x1, Pallas kernels, body(): call(backward_kernel, [((256, 1024), BF16), ((4, 32, 512), BF16), ((4, 2,...  127 us

profile of v3, /device:TPU:0, one launch (start us, length us, event | category | flops | bytes accessed | tf_op | source)
XLA Modules:
  0.0 325.8 jit_solution(11175386240739979387)
XLA Ops:
  1.3 193.5 %shard_map.255 = (bf16[256,1024]{1,0:T(8,128)(2,1)}, f32[256,1024]{1,0:T(8,128)}, bf16[8,2,128,1152]{3,2,1,0:T(8,128)(2,1)}, bf16[4,144,1024]{2,1,0:T(8,128)(2,1...) custom-call(bf16[256,1024]{1,0:T(8,128)(2,1)} %bitcast.14, ...), custom_call_target="tpu_custom_call" | custom-call | tf_op jit(solution)/shard_map/pallas_call | solution.py:1016
  194.8 127.4 %shard_map.256 = (bf16[256,1024]{1,0:T(8,128)(2,1)}, bf16[4,32,512]{2,1,0:T(8,128)(2,1)}, bf16[4,2,32,1152]{3,2,1,0:T(8,128)(2,1)}, f32[144,1024]{1,0:T(8,128)}, f32[32,1024]{1,0:T(8,128)}, /*index=5*/f32[8,1024]{1,0:T(8,128)}) custom-call(f32[256,1024]{1,0:T(8,128)} %get-tuple-element.47.dn2, f32[256,1024]{1,0:T(8,128)} %get-tuple-element.48.middle, ...), custom_call_target="tpu_custom_call" | custom-call | tf_op jit(solution)/shard_map/pallas_call | solution.py:1041
  322.1 3.6 %shard_map.257 = (bf16[256,1024]{1,0:T(8,128)(2,1)}, bf16[256,1024]{1,0:T(8,128)(2,1)}, f32[32,1024]{1,0:T(8,128)}, f32[32,512]{1,0:T(8,128)}, f32[32,512]{1,0:T...) custom-call(bf16[256,1024]{1,0:T(8,128)(2,1)} %get-tuple-element.46., ...), custom_call_target="tpu_custom_call" | custom-call | tf_op jit(solution)/shard_map/pallas_call | solution.py:1071

commit v4 on v3

--- a/solution.py
+++ b/solution.py
@@ -242,14 +242,16 @@
     return jnp.where(t == 0, p.b, jnp.where(t == 1, p.core, jnp.where(t == 2, p.across, p.far)))
 
 
-def forward_kernel(
+def block_kernel(
     x, dy, lengths, w_query, key_weight, value_weight, w_out, w_gate, w_up, w_down,
     cos_table, sin_table, gain_query, gain_key, gain_a, gain_f,
-    output, dn2, ggu_out, gd_mine, gd_other, wo_out, wqkv_out, norm_out, unit_out_, lse_out, attn_out, mix_out,
-    middle, length_all,
-    xa, norm, wqkv, wo, pack, unit, unit_out, lse, kv, vt, mix, norm_two, dy_all, wgu, wd, gd,
-    hid, dgate, dup, parts_n, recv_n, parts_o, recv_o, keep_n, keep_o,
-    qkv_send, gu_send, length, cos, sin,
+    output, dx, rqkv, rgu, rd, ro, gains_out, norm_park,
+    xa, norm, wqkv, wo, pack, unit, unit_out, lse, kv, mix, dy_all, wgu, wd, gd,
+    hid, dgate, dup, dk_sum, dv_sum, parts, recv, recv_o, keep, result, middle,
+    qkv_send, gu_send, length, cos, sin, length_all,
+    dou, delta,
+    y_d, t_d, z_d, y_g, t_g, z_g, y_u, t_u, z_u, y_q, z_q, y_o, z_o,
+    gain_sum, gain_batch, gain_seq,
     send_sem, recv_sem, local_sem,
 ):
     p = Place(send_sem, recv_sem, local_sem)
@@ -266,23 +268,23 @@
     length[...] = jnp.broadcast_to(lengths[0], (8, 128)).astype(jnp.int32)
     own_qkv = p.local(qkv_send.at[b], wqkv.at[s, my_rows])
     length_all[b] = length[...]
+    pack_hidden(w_gate, gu_send, 0)
+    pack_hidden(w_up, gu_send, 1)
     p.meet()
 
     got_qkv, got_len = [], []
     for k in (1, 2, 3):
         to = lax.rem(b + k, 4)
         got_qkv.append(p.post(qkv_send.at[to], wqkv.at[s, my_rows], (s, to)))
-    x_across = p.post(x, xa.at[b], (s, p.across))
-    x_core = p.post(x, xa.at[b], (s, p.core))
+    own_x.wait()
+    x_across = p.post(xa.at[b], xa.at[b], (s, p.across))
+    x_core = p.post(xa.at[b], xa.at[b], (s, p.core))
     for k in (1, 2, 3):
         to = lax.rem(b + k, 4)
         got_len.append(p.post(length, length_all.at[b], (s, to)))
     spread_d = Spread(p, lambda i: wd.at[i])
     spread_g = Spread(p, lambda i: wgu.at[i, 0])
     spread_u = Spread(p, lambda i: wgu.at[i, 1])
-    own_d.wait()
-    spread_d.start()
-    own_x.wait()
 
     def normalize(g):
         xg = xa[g].astype(F32)
@@ -294,8 +296,6 @@
         p.landed(got_qkv[k - 1], wqkv.at[s, my_rows])
     z_qkv = [p.post(wqkv.at[s], wqkv.at[s], (2 * p.up(k) + y, b)) for k in (1, 2, 3)]
     y_qkv = [p.post(wqkv.at[s], wqkv.at[s], (p.flip, b))]
-    pack_hidden(w_gate, gu_send, 0)
-    pack_hidden(w_up, gu_send, 1)
     own_gu = p.local(gu_send.at[b], wgu.at[s, :, my_rows])
     got_gu = []
     for k in (1, 2, 3):
@@ -305,6 +305,11 @@
         slot = 2 * p.down(k) + y
         p.landed(z_qkv[k - 1], wqkv.at[slot])
         y_qkv.append(p.post(wqkv.at[slot], wqkv.at[slot], (p.flip, b)))
+    own_d.wait()
+    spread_d.start()
+    own_wo.wait()
+    z_wo = [p.post(wo.at[s, b], wo.at[s, b], (2 * p.up(k) + y, b)) for k in (1, 2, 3)]
+    y_wo = [p.post(wo.at[s, b], wo.at[s, b], (p.flip, b))]
     p.landed(x_core, xa.at[p.core])
     normalize(p.core)
     p.landed(x_across, xa.at[p.across])
@@ -314,7 +319,6 @@
     p.landed(y_qkv[0], wqkv.at[p.flip])
     for k in (1, 2, 3):
         p.landed(y_qkv[k], wqkv.at[2 * p.down(k) + 1 - y])
-    kept = [p.local(wqkv, wqkv_out)]
     gain_q, gain_k = twice(gain_query), twice(gain_key)
 
     first_unit = p.slots(8)
@@ -348,23 +352,20 @@
             pack[2 * g + kk, :, 128:256] = jnp.where(lanes(kr.shape) < 64, kr, kvp).astype(BF16)
             each_piece(t, kk, lambda made: made.start())
 
-        @pl.when(t == 2)
-        def _():
-            spread_d.land(0)
-            spread_d.land_inner()
-
         return carry
 
     lax.fori_loop(0, 4, project, 0)
     own_unit = p.local(pack.at[s], unit.at[s])
-    kept.append(p.local(norm, norm_out))
-    own_wo.wait()
-    z_wo = [p.post(wo.at[s, b], wo.at[s, b], (2 * p.up(k) + y, b)) for k in (1, 2, 3)]
-    y_wo = [p.post(wo.at[s, b], wo.at[s, b], (p.flip, b))]
-    spread_d.land_end()
+    parked = p.local(norm, norm_park)
+    for k in (1, 2, 3):
+        slot = 2 * p.down(k) + y
+        p.landed(z_wo[k - 1], wo.at[slot, b])
+        y_wo.append(p.post(wo.at[slot, b], wo.at[slot, b], (p.flip, b)))
+    spread_d.land(0)
+    spread_d.land_inner()
     own_dy.wait()
-    dy_across = p.post(dy, dy_all.at[b], (s, p.across))
-    dy_core = p.post(dy, dy_all.at[b], (s, p.core))
+    dy_across = p.post(dy_all.at[b], dy_all.at[b], (s, p.across))
+    dy_core = p.post(dy_all.at[b], dy_all.at[b], (s, p.core))
     for k in (1, 2, 3):
         p.landed(got_len[k - 1], length_all.at[lax.rem(b + 4 - k, 4)])
 
@@ -372,34 +373,34 @@
         src = lax.rem(s + k, 8)
         p.landed(first_unit + src, unit.at[src])
     own_unit.wait()
-    kept.append(p.local(unit, unit_out_))
     own_gu.wait()
     for k in (1, 2, 3):
         p.landed(got_gu[k - 1], wgu.at[s, :, my_rows])
     spread_g.start()
     spread_u.send(s, (p.flip, b), 4, 3)
-    for k in (1, 2, 3):
-        slot = 2 * p.down(k) + y
-        p.landed(z_wo[k - 1], wo.at[slot, b])
-        y_wo.append(p.post(wo.at[slot, b], wo.at[slot, b], (p.flip, b)))
-
-    def prepare(j, carry):
-        live = j * 256 + rows_of((256, 128)) < length_all[z][0:1, :]
-        masked = jnp.where(live, unit[j, :, 128:256].astype(F32), 0.0)
-        kv[j] = masked.astype(BF16)
-        vt[j, 0:64] = jnp.transpose(masked)[64:128].astype(BF16)
-        alive = j * 256 + lanes((16, 256)) < length_all[z][0:1, 0:1]
-        vt[j, 64:80] = jnp.where(alive, 1.0, 0.0).astype(BF16)
-        return carry
-
-    lax.fori_loop(0, 8, prepare, 0)
-    p.landed(dy_across, dy_all.at[p.across])
-    dy_far = p.post(dy_all.at[p.across], dy_all.at[p.across], (s, p.core))
     p.landed(y_wo[0], wo.at[p.flip, b])
     for k in (1, 2, 3):
         p.landed(y_wo[k], wo.at[2 * p.down(k) + 1 - y, b])
     wo_across = p.post(wo.at[:, b], wo.at[:, b], (s, p.across))
     wo_core = p.post(wo.at[:, b], wo.at[:, b], (s, p.core))
+    spread_d.land_end()
+
+    def values(j):
+        return dup.at[j // 2, lax.rem(j, 2), 0:80, 0:256]
+
+    def prepare(j, carry):
+        live = j * 256 + rows_of((256, 128)) < length_all[z][0:1, :]
+        masked = jnp.where(live, unit[j, :, 128:256].astype(F32), 0.0)
+        kv[j] = masked.astype(BF16)
+        turned = jnp.transpose(masked)[64:128].astype(BF16)
+        alive = j * 256 + lanes((16, 256)) < length_all[z][0:1, 0:1]
+        counted = jnp.where(alive, 1.0, 0.0).astype(BF16)
+        values(j)[...] = jnp.concatenate([turned, counted], axis=0)
+        return carry
+
+    lax.fori_loop(0, 8, prepare, 0)
+    p.landed(dy_across, dy_all.at[p.across])
+    dy_far = p.post(dy_all.at[p.across], dy_all.at[p.across], (s, p.core))
     first_mix, first_across, first_core = p.slots(8), p.slots(8), p.slots(8)
 
     def mix_send(src, t):
@@ -418,12 +419,12 @@
         right = jnp.concatenate([both, jnp.zeros((64, 512), BF16)], axis=0)
 
         def block(j, acc):
-            return acc + nn(vt[j], jnp.exp(nn(kv[j], right)).astype(BF16))
+            return acc + nn(values(j)[...], jnp.exp(nn(kv[j], right)).astype(BF16))
 
         acc = lax.fori_loop(0, i, block, jnp.zeros((80, 512), F32))
         causal = rows_of((256, 512)) <= lax.rem(lanes((256, 512)), 256)
         edge = jnp.where(causal, jnp.exp(nn(kv[i], right)), 0.0).astype(BF16)
-        acc = acc + nn(vt[i], edge)
+        acc = acc + nn(values(i)[...], edge)
         total = acc[64:65]
         out = acc[0:64] / total
         out = jnp.concatenate([out[:, 0:256], out[:, 256:512]], axis=0)
@@ -434,16 +435,15 @@
         def _():
             p.copy(unit_out.at[i], mix.at[b, s], (i, b), first_mix + t).start()
 
-        @pl.when(t == 3)
+        @pl.when(t == 2)
+        def _():
+            spread_u.send(s, (2 * p.pair + y, b), 0, 0)
+            spread_u.send(s, (2 * p.there + y, b), 1, jnp.where(p.inner, 1, 2))
+
+        @pl.when(t == 5)
         def _():
             spread_g.land(0)
             spread_g.land_inner()
-            spread_u.send(s, (2 * p.pair + y, b), 0, 0)
-            spread_u.send(s, (2 * p.there + y, b), 1, jnp.where(p.inner, 1, 2))
-
-        @pl.when(t == 6)
-        def _():
-            spread_g.land_end()
 
         @pl.when(t >= 4)
         def _():
@@ -453,14 +453,23 @@
 
     lax.fori_loop(0, 8, attend, 0)
     own_mix = p.local(unit_out.at[s], mix.at[b, s])
-    kept.append(p.local(unit_out, attn_out))
-    kept.append(p.local(lse, lse_out))
     own_mix.wait()
     mix_send(s, 7)
     for t in range(4, 7):
         mix_arrived(t)
+    spread_g.land_end()
     spread_u.land(0)
     spread_u.land_inner()
+    p.landed(dy_core, dy_all.at[p.core])
+    p.landed(dy_far, dy_all.at[p.far])
+    spread_d.finish()
+
+    def hidden_back(g, carry):
+        rows = pl.ds(pl.multiple_of(g * 256, 256), 256)
+        dgate[g] = nt(dy_all[g], wd[...].reshape(1152, 1024)).astype(BF16).reshape(2, 128, 1152)
+        return carry
+
+    lax.fori_loop(0, 4, hidden_back, 0)
     p.landed(wo_across, wo.at[:, p.across])
     wo_far = p.post(wo.at[:, p.across], wo.at[:, p.across], (s, p.core))
     for t in range(8):
@@ -470,15 +479,15 @@
         p.landed(first_core + t, mix.at[p.core, lax.rem(s + 7 - t, 8)])
     p.landed(wo_core, wo.at[:, p.core])
     p.landed(wo_far, wo.at[:, p.far])
-    kept.append(p.local(wo, wo_out))
     spread_u.land_end()
     p.landed(mix_far, mix.at[p.far])
-    kept.append(p.local(mix, mix_out))
+
+    parked.wait()
 
     def project_out(g, carry):
         mixed = jnp.concatenate([mix[c, 2 * g + kk] for c in range(4) for kk in (0, 1)], axis=1)
         mid = xa[g].astype(F32) + nn(mixed, wo[...].reshape(1024, 1024))
-        norm_two[g] = (mid * rms_factor(mid) * gain_f[...]).astype(BF16)
+        norm[g] = (mid * rms_factor(mid) * gain_f[...]).astype(BF16)
 
         @pl.when(g == b)
         def _():
@@ -487,84 +496,7 @@
         return carry
 
     lax.fori_loop(0, 4, project_out, 0)
-    p.landed(dy_core, dy_all.at[p.core])
-    p.landed(dy_far, dy_all.at[p.far])
-    for spread in (spread_d, spread_g, spread_u):
-        spread.finish()
-
-    first_n, first_o = p.slots(3), p.slots(3)
-
-    def gated(t, carry):
-        g = batch_order(p, t)
-        rows = pl.ds(pl.multiple_of(g * 256, 256), 256)
-        n2 = norm_two[g]
-        gate = nn(n2, wgu[:, 0].reshape(1024, 1152))
-        up = nn(n2, wgu[:, 1].reshape(1024, 1152))
-        dh = nt(dy_all[g], wd[...].reshape(1152, 1024))
-        sg = 1.0 / (1.0 + jnp.exp(-gate))
-        swish = gate * sg
-        hid[rows] = (swish * up).astype(BF16)
-        dg = (dh * up * sg * (1.0 + gate * (1.0 - sg))).astype(BF16)
-        du = (dh * swish).astype(BF16)
-        dgate[rows] = dg
-        dup[rows] = du
-        part = nt(dg, wgu[:, 0].reshape(1024, 1152)) + nt(du, wgu[:, 1].reshape(1024, 1152))
-        parts_n[g] = part.astype(BF16)
-
-        @pl.when(t == 3)
-        def _():
-            keep_n[...] = part
-
-        chip_sum_post(p, t, parts_n, recv_n, first_n)
-        return carry
-
-    lax.fori_loop(0, 4, gated, 0)
-    chip_sum_across(p, parts_n, recv_n, first_n)
-
-    def down_rows(c, carry):
-        at = pl.multiple_of(128 * c, 128)
-        gd[pl.ds(at, 128)] = tn(hid[:, pl.ds(at, 128)], dy_all[...].reshape(1024, 1024)).astype(BF16)
-        return carry
-
-    lax.fori_loop(0, 9, down_rows, 0)
-    sent_d = []
-    for i in range(4):
-        other = pl.ds(pl.multiple_of(144 * (2 * i + 1 - y), 16), 144)
-        mine = pl.ds(pl.multiple_of(144 * (2 * i + y), 16), 144)
-        sent_d.append(p.post(gd.at[other], gd_other.at[i], (p.flip, b)))
-        kept.append(p.local(gd.at[mine], gd_mine.at[i]))
-
-    def down(t, carry):
-        g = batch_order(p, t)
-        part = nn(hid[pl.ds(pl.multiple_of(g * 256, 256), 256)], wd[...].reshape(1152, 1024))
-        parts_o[g] = part.astype(BF16)
-
-        @pl.when(t == 3)
-        def _():
-            keep_o[...] = part
-
-        chip_sum_post(p, t, parts_o, recv_o, first_o)
-        return carry
-
-    lax.fori_loop(0, 4, down, 0)
-    chip_sum_across(p, parts_o, recv_o, first_o)
-    for spread in (spread_d, spread_g, spread_u):
-        spread.drain()
-
-    def gate_rows(c, carry):
-        at = pl.multiple_of(128 * c, 128)
-        left = norm_two[:, :, pl.ds(at, 128)].reshape(1024, 128)
-        wgu[c, 0] = tn(left, dgate[...]).astype(BF16)
-        wgu[c, 1] = tn(left, dup[...]).astype(BF16)
-        return carry
-
-    lax.fori_loop(0, 8, gate_rows, 0)
-    kept.append(p.local(wgu, ggu_out))
-    dn2[...] = keep_n[...] + chip_sum_rest(p, parts_n, recv_n, first_n)
-    total = keep_o[...] + chip_sum_rest(p, parts_o, recv_o, first_o)
-    output[...] = (middle[...] + total).astype(BF16)
-    for i in range(4):
-        p.landed(sent_d[i], gd_other.at[i])
+
     for t in range(8):
         if t < 7:
             p.copy(unit_out.at[s], mix.at[b, s], (p.flip, b), first_mix + t).wait_send()
@@ -573,17 +505,398 @@
     for t in range(4):
         for kk in (0, 1):
             each_piece(t, kk, lambda made: made.wait_send())
-    for made in kept:
+    p.drain()
+
+    def turn(e, carry):
+        for g in range(4):
+            hid[0:128, 256 * g : 256 * g + 256] = jnp.transpose(
+                mix[e // 2, 2 * g + lax.rem(e, 2)].astype(F32)
+            ).astype(BF16)
+        gu_send[e // 2, lax.rem(e, 2), :, 0:1024] = hid[my_rows, 0:1024]
+        return carry
+
+    lax.fori_loop(0, 8, turn, 0)
+    spread_g.finish()
+
+    def gate_of(g, carry):
+        rows = pl.ds(pl.multiple_of(g * 256, 256), 256)
+        hid[rows] = nn(norm[g], wgu[:, 0].reshape(1024, 1152)).astype(BF16)
+        return carry
+
+    lax.fori_loop(0, 4, gate_of, 0)
+    spread_u.finish()
+    first_n = p.slots(3)
+
+    def gated(t, carry):
+        g = batch_order(p, t)
+        rows = pl.ds(pl.multiple_of(g * 256, 256), 256)
+        gate = hid[rows].astype(F32)
+        up = nn(norm[g], wgu[:, 1].reshape(1024, 1152))
+        dh = dgate[g].reshape(256, 1152).astype(F32)
+        sg = 1.0 / (1.0 + jnp.exp(-gate))
+        swish = gate * sg
+        hid[rows] = (swish * up).astype(BF16)
+        dg = (dh * up * sg * (1.0 + gate * (1.0 - sg))).astype(BF16)
+        du = (dh * swish).astype(BF16)
+        dgate[g] = dg.reshape(2, 128, 1152)
+        dup[g] = du.reshape(2, 128, 1152)
+        part = nt(dg, wgu[:, 0].reshape(1024, 1152)) + nt(du, wgu[:, 1].reshape(1024, 1152))
+        parts[g] = part.astype(BF16)
+
+        @pl.when(t == 3)
+        def _():
+            keep[...] = part
+
+        chip_sum_post(p, t, parts, recv, first_n)
+        return carry
+
+    lax.fori_loop(0, 4, gated, 0)
+    chip_sum_across(p, parts, recv, first_n)
+
+    def down_rows(c, carry):
+        at = pl.multiple_of(128 * c, 128)
+        gd[pl.ds(at, 128)] = tn(hid[:, pl.ds(at, 128)], dy_all[...].reshape(1024, 1024)).astype(BF16)
+        return carry
+
+    lax.fori_loop(0, 9, down_rows, 0)
+    sum_d = SeqTree(
+        p, lambda i: gd.at[pl.ds(pl.multiple_of(144 * i, 16), 144)], y_d, t_d, z_d
+    )
+    sum_g = SeqTree(p, lambda i: wgu.at[i, 0], y_g, t_g, z_g)
+    sum_u = SeqTree(p, lambda i: wgu.at[i, 1], y_u, t_u, z_u)
+    sum_d.start()
+
+    for spread in (spread_d, spread_g, spread_u):
+        spread.drain()
+
+    def gate_rows(c, carry):
+        at = pl.multiple_of(128 * c, 128)
+        side = norm[:, :, pl.ds(at, 128)].reshape(1024, 128)
+        wgu[c, 0] = tn(side, dgate[...].reshape(1024, 1152)).astype(BF16)
+        wgu[c, 1] = tn(side, dup[...].reshape(1024, 1152)).astype(BF16)
+        return carry
+
+    lax.fori_loop(0, 8, gate_rows, 0)
+    load_norm = p.local(norm_park, norm)
+
+    mid = middle[...]
+    r2 = rms_factor(mid)
+    grad_two = keep[...] + chip_sum_rest(p, parts, recv, first_n)
+    gain_sum[...] = jnp.zeros((8, 1024), F32)
+    gain_sum[1:2] = jnp.sum(grad_two * mid * r2, axis=0, keepdims=True)
+    dm = dy_all[b].astype(F32) + norm_back(grad_two * gain_f[...], mid, r2)
+    result[...] = mid
+    middle[...] = dm
+    xa[b] = dm.astype(BF16)
+
+    first_mixed = p.slots(3)
+
+    def mixed_back(t, carry):
+        c = batch_order(p, t)
+        place = jnp.where(t == 3, 1, 0)
+        for kk in (0, 1):
+            mix[place, 2 * c + kk] = nt(xa[b], wo[2 * c + kk].reshape(128, 1024)).astype(BF16)
+
+        @pl.when(t < 3)
+        def _():
+            p.copy(
+                mix.at[0, pl.ds(2 * c, 2)], mix.at[1, pl.ds(2 * b, 2)], (s, c), first_mixed + t
+            ).start()
+
+        return carry
+
+    lax.fori_loop(0, 4, mixed_back, 0)
+    dbr_across = p.post(xa.at[b], xa.at[b], (s, p.across))
+    dbr_core = p.post(xa.at[b], xa.at[b], (s, p.core))
+    def down(g, carry):
+        part = nn(hid[pl.ds(pl.multiple_of(g * 256, 256), 256)], wd[...].reshape(1152, 1024))
+        dy_all[g] = part.astype(BF16)
+
+        @pl.when(g == b)
+        def _():
+            result[...] = result[...] + part
+
+        return carry
+
+    lax.fori_loop(0, 4, down, 0)
+
+    first_o = p.slots(3)
+    chip_sum_post(p, 0, dy_all, recv_o, first_o)
+    chip_sum_post(p, 1, dy_all, recv_o, first_o)
+    def q_right(i):
+        return hid.at[pl.ds(pl.multiple_of(128 * i, 128), 128), 0:512]
+
+    def do_right(i):
+        return hid.at[pl.ds(pl.multiple_of(128 * i, 128), 128), 512:1024]
+
+    def tall(i, base):
+        half = pl.ds(2 * lax.rem(i, 2), 2)
+        return dgate.at[half, :, :, pl.ds(pl.multiple_of(base + 128 * (i // 2), 128), 128)]
+
+    def q_left(i):
+        return tall(i, 0)
+
+    def do_left(i):
+        return tall(i, 512)
+
+    def dk2(i):
+        return dk_sum.at[i]
+
+    def dv2(i):
+        return dv_sum.at[i]
+
+    def dq2(i):
+        rows = pl.ds(pl.multiple_of(64 * lax.rem(i, 4), 64), 64)
+        return keep.at[rows, pl.ds(pl.multiple_of(512 * (i // 4), 512), 512)]
+
+    def keys_turned(i):
+        return dup.at[i // 2, lax.rem(i, 2), 0:64, 0:256]
+
+    def prepare_back(i, carry):
+        keys_turned(i)[...] = jnp.transpose(kv[i].astype(F32))[0:64].astype(BF16)
+        q = unit[i, :, 0:128].astype(F32)
+        qt = jnp.transpose(q).astype(BF16)
+        both = jnp.concatenate([qt[0:64], qt[64:128]], axis=1)
+        q_right(i)[...] = jnp.concatenate([both, jnp.zeros((64, 512), BF16)], axis=0)
+        first = lanes(q.shape) < 64
+        both = jnp.concatenate([jnp.where(first, q, 0.0), jnp.where(first, 0.0, q)], axis=0)
+        q_left(i)[...] = both.astype(BF16).reshape(2, 2, 128, 128)
+        dq2(i)[...] = jnp.zeros((64, 512), F32)
+        dk2(i)[...] = jnp.zeros((256, 128), F32)
+        dv2(i)[...] = jnp.zeros((256, 128), F32)
+        return carry
+
+    lax.fori_loop(0, 8, prepare_back, 0)
+    first_do = p.slots(8)
+
+    def grad_piece(t, kk, act):
+        to = 2 * near_first(p, t) + kk
+
+        @pl.when(to != s)
+        def _():
+            act(p.copy(mix.at[1, to], dou.at[s], (to, b), first_do + 2 * t + kk, first_do + s))
+
+    for t, index in ((0, None), (1, 1), (2, 2), (3, 0)):
+        if index is not None:
+            p.landed(first_mixed + index, mix.at[1, pl.ds(2 * near_first(p, t), 2)])
+        for kk in (0, 1):
+            grad_piece(t, kk, lambda made: made.start())
+    dou[s] = mix[1, s]
+
+    chip_sum_across(p, dy_all, recv_o, first_o)
+    sum_d.reduce()
+    sum_g.start()
+    for k in range(1, 8):
+        src = lax.rem(s + k, 8)
+        p.landed(first_do + src, dou.at[src])
+
+    def prepare_grad(i, carry):
+        do = dou[i].astype(F32)
+        dot = jnp.transpose(do)
+        right = jnp.concatenate([dot[0:64], dot[64:128]], axis=1).astype(BF16)
+        do_right(i)[...] = jnp.concatenate([jnp.zeros((64, 512), BF16), right], axis=0)
+        first = lanes(do.shape) < 64
+        tall_do = jnp.concatenate([jnp.where(first, do, 0.0), jnp.where(first, 0.0, do)], axis=0)
+        do_left(i)[...] = tall_do.astype(BF16).reshape(2, 2, 128, 128)
+        both = dot * jnp.transpose(unit_out[i].astype(F32))
+        low = jnp.sum(both[0:64], axis=0, keepdims=True)
+        high = jnp.sum(both[64:128], axis=0, keepdims=True)
+        delta[i] = jnp.broadcast_to(jnp.concatenate([low, high], axis=1), (8, 512))
+        return carry
+
+    lax.fori_loop(0, 8, prepare_grad, 0)
+
+    def meet(i, j, probs):
+        ds = (probs * (nn(kv[j], do_right(i)[...]) - delta[i][0:1])).astype(BF16)
+        dv2(j)[...] += nn(probs.astype(BF16), do_left(i)[...].reshape(512, 128))
+        dk2(j)[...] += nn(ds, q_left(i)[...].reshape(512, 128))
+        dq2(i)[...] += nn(keys_turned(j)[...], ds)
+
+    first_back = p.slots(8)
+
+    def blocks(t, carry):
+        c = lax.rem(s + 1 + t, 8)
+        causal = rows_of((256, 512)) <= lax.rem(lanes((256, 512)), 256)
+        meet(c, c, jnp.where(causal, jnp.exp(nn(kv[c], q_right(c)[...]) - lse[c][0:1]), 0.0))
+
+        def other(u, inner_carry):
+            o = lax.rem(s + 1 + u, 8)
+            i, j = jnp.maximum(c, o), jnp.minimum(c, o)
+            meet(i, j, jnp.exp(nn(kv[j], q_right(i)[...]) - lse[i][0:1]))
+            return inner_carry
+
+        lax.fori_loop(t + 1, 8, other, 0)
+        acc = dq2(c)[...]
+        dq = jnp.concatenate([acc[:, 0:256], acc[:, 256:512]], axis=0) * 0.125
+        pack[c, :, 0:128] = jnp.transpose(dq).astype(BF16)
+        live = c * 256 + rows_of((256, 128)) < length_all[z][0:1, :]
+        dk, dv = dk2(c)[...], dv2(c)[...]
+        dk = dk + pltpu.roll(dk, 64, 1)
+        dv = dv + pltpu.roll(dv, 64, 1)
+        dkv = jnp.where(lanes((256, 128)) < 64, dk, dv)
+        pack[c, :, 128:256] = jnp.where(live, dkv, 0.0).astype(BF16)
+
+        @pl.when(t < 7)
+        def _():
+            p.copy(pack.at[c], unit.at[s], (c, b), first_back + t).start()
+
+        @pl.when(t == 0)
+        def _():
+            p.landed(dbr_across, xa.at[p.across])
+            p.copy(xa.at[p.across], xa.at[p.across], (s, p.core), dbr_far).start()
+
+        @pl.when(t == 4)
+        def _():
+            sum_d.relay()
+
+        return carry
+
+    dbr_far = p.slots(1)
+    lax.fori_loop(0, 8, blocks, 0)
+    unit[s] = pack[s]
+
+    p.landed(dbr_core, xa.at[p.core])
+    p.landed(dbr_far, xa.at[p.far])
+    out_rows = nn(gu_send[:, :, :, 0:1024].reshape(256, 1024), xa[...].reshape(1024, 1024)).astype(BF16)
+    for e in range(8):
+        dgate[e // 2, e % 2, 0:32, 0:1024] = out_rows[32 * e : 32 * e + 32]
+    sum_o = SeqSum(p, y_o, z_o)
+    sum_o.start(dgate.at[:, :, 0:32, 0:1024])
+    load_x = p.local(x, xa.at[p.far])
+    sum_g.reduce()
+    sum_u.start()
+    load_norm.wait()
+
+    first_n = p.slots(3)
+    zero_row = jnp.zeros((1, 128), F32)
+
+    def heads(t, carry):
+        sum_q, sum_k = carry
+        unit_of = lax.rem(s + 7 - t, 8)
+
+        @pl.when(t < 7)
+        def _():
+            p.landed(first_back + t, unit.at[unit_of])
+
+        g = unit_of // 2
+        at = pl.multiple_of(256 * lax.rem(unit_of, 2), 256)
+        whole = nn(norm[g], wqkv[:, :, pl.ds(at, 256)].reshape(1024, 256))
+        q, k = heads_of(whole, 0)
+        rq = lax.rsqrt(head_mean(q * q) + eps)
+        rk = lax.rsqrt(head_mean(k * k) + eps)
+        dq = rope_back(unit[unit_of, :, 0:128].astype(F32), cos[...], sin[...])
+        dkv = unit[unit_of, :, 128:256].astype(F32)
+        dk = rope_back(dkv, cos[...], sin[...])
+        sum_q = sum_q + jnp.sum(dq * q * rq, axis=0, keepdims=True)
+        sum_k = sum_k + jnp.sum(dk * k * rk, axis=0, keepdims=True)
+        dq = dq * gain_q
+        dk = dk * gain_k
+        dq = rq * (dq - q * rq * rq * head_mean(dq * q))
+        dk = rk * (dk - k * rk * rk * head_mean(dk * k))
+        dup[g, :, :, pl.ds(at, 128)] = dq.astype(BF16).reshape(2, 128, 128)
+        dkv = jnp.where(lanes(dk.shape) < 64, dk, dkv).astype(BF16)
+        dup[g, :, :, pl.ds(pl.multiple_of(at + 128, 128), 128)] = dkv.reshape(2, 128, 128)
+        return (sum_q, sum_k)
+
+    sum_q, sum_k = lax.fori_loop(0, 8, heads, (zero_row, zero_row))
+
+    gain_sum[2:3, 0:128] = sum_q
+    gain_sum[3:4, 0:128] = sum_k
+    def qkv_rows(c, carry):
+        at = pl.multiple_of(128 * c, 128)
+        side = norm[:, :, pl.ds(at, 128)].reshape(1024, 128)
+        dup[c // 2, lax.rem(c, 2), :, 512:1024] = tn(side, dup[:, :, :, 0:512].reshape(1024, 512)).astype(BF16)
+        return carry
+
+    lax.fori_loop(0, 8, qkv_rows, 0)
+    sum_qkv = SeqSum(p, y_q, z_q)
+    sum_qkv.start(dup.at[:, :, :, pl.ds(512, 512)])
+    sum_g.relay()
+
+    def stream_back(t, carry):
+        g = batch_order(p, t)
+        part = nt(dup[g, :, :, 0:512].reshape(256, 512), wqkv[...].reshape(1024, 512))
+        parts[g] = part.astype(BF16)
+
+        @pl.when(t == 3)
+        def _():
+            keep[...] = part
+
+        chip_sum_post(p, t, parts, recv, first_n)
+        return carry
+
+    lax.fori_loop(0, 4, stream_back, 0)
+    chip_sum_across(p, parts, recv, first_n)
+    sum_o.middle()
+    sum_u.reduce()
+    xa[p.core] = (result[...] + chip_sum_rest(p, dy_all, recv_o, first_o)).astype(BF16)
+    leave = [p.local(xa.at[p.core], output)]
+    sum_qkv.middle()
+
+    dn1 = keep[...] + chip_sum_rest(p, parts, recv, first_n)
+    load_x.wait()
+    xf = xa[p.far].astype(F32)
+    r1 = rms_factor(xf)
+    gain_sum[0:1] = jnp.sum(dn1 * xf * r1, axis=0, keepdims=True)
+    xa[p.far] = (middle[...] + norm_back(dn1 * gain_a[...], xf, r1)).astype(BF16)
+    leave.append(p.local(xa.at[p.far], dx))
+    got_gain = [p.post(gain_sum, gain_batch.at[b], (s, lax.rem(b + k, 4))) for k in (1, 2, 3)]
+    gain_batch[b] = gain_sum[...]
+    sum_u.relay()
+
+    rd[...] = sum_d.finish()
+
+    def exchange(total, own, dst):
+        for c in range(4):
+            own(c)[...] = total[32 * c : 32 * c + 32].astype(BF16)
+        got = []
+        for k in (1, 2, 3):
+            to = lax.rem(b + k, 4)
+            got.append(p.post(own(to), dst(b), (s, to)))
+        dst(b)[...] = own(b)[...]
+        return got
+
+    def arrive(got, dst):
+        for k in (1, 2, 3):
+            p.landed(got[k - 1], dst(lax.rem(b + 4 - k, 4)))
+
+    dst_g, dst_u, dst_q = (lambda i: rgu.at[i, 0]), (lambda i: rgu.at[i, 1]), (lambda i: rqkv.at[i])
+    got_g = exchange(sum_g.finish(), lambda c: gu_send.at[c, 0], dst_g)
+    for k in (1, 2, 3):
+        p.landed(got_gain[k - 1], gain_batch.at[lax.rem(b + 4 - k, 4)])
+    gain_seq[s] = (gain_batch[0] + gain_batch[1]) + (gain_batch[2] + gain_batch[3])
+    got_all = [p.post(gain_seq.at[s], gain_seq.at[s], (lax.rem(s + k, 8), b)) for k in range(1, 8)]
+    got_u = exchange(sum_u.finish(), lambda c: gu_send.at[c, 1], dst_u)
+    ro[...] = sum_o.finish()
+    got_q = exchange(sum_qkv.finish(), lambda c: qkv_send.at[c], dst_q)
+    for k in range(1, 8):
+        p.landed(got_all[k - 1], gain_seq.at[lax.rem(s + 8 - k, 8)])
+    total = gain_seq[0]
+    for k in range(1, 8):
+        total = total + gain_seq[k]
+    gains_out[...] = total
+    arrive(got_g, dst_g)
+    arrive(got_u, dst_u)
+    arrive(got_q, dst_q)
+    for t in range(4):
+        for kk in (0, 1):
+            grad_piece(t, kk, lambda made: made.wait_send())
+    for t in range(7):
+        p.copy(pack.at[s], unit.at[s], (p.flip, b), first_back + t).wait_send()
+    for made in leave:
         made.wait()
+    p.copy(xa.at[b], xa.at[b], (s, p.core), dbr_far).wait_send()
+    for t in range(3):
+        p.copy(mix.at[0, 0:2], mix.at[0, 0:2], (s, p.core), first_mixed + t).wait_send()
     p.drain()
 
 
 def chip_sum_post(p, t, parts, recv, first):
-    @pl.when(t == 0)
+    @pl.when(jnp.equal(t, 0))
     def _():
         p.copy(parts.at[p.far], recv.at[0], (p.s, p.core), first).start()
 
-    @pl.when(t == 1)
+    @pl.when(jnp.equal(t, 1))
     def _():
         p.copy(parts.at[p.core], recv.at[1], (p.s, p.core), first + 1).start()
 
@@ -607,28 +920,31 @@
 
 
 class SeqTree:
-    def __init__(self, p, mine, y_recv, relayed, z_recv, sums=None):
-        self.p, self.mine, self.y_recv, self.relayed, self.z_recv = p, mine, y_recv, relayed, z_recv
-        self.sums = y_recv if sums is None else sums
-        self.first = p.slots(6)
-        self.started = False
-
-    def start(self, source):
+    def __init__(self, p, slot, y_recv, relayed, z_recv):
+        self.p, self.slot, self.y_recv, self.relayed, self.z_recv = p, slot, y_recv, relayed, z_recv
+        self.first = p.slots(8)
+
+    def mine(self, i):
+        return self.slot(2 * i + self.p.y)[...].astype(F32)
+
+    def start(self):
         p = self.p
-        self.started = True
-        p.copy(source, self.y_recv, (p.flip, p.b), self.first + 4).start()
+        for i in range(4):
+            p.copy(
+                self.slot(2 * i + 1 - p.y), self.y_recv.at[i], (p.flip, p.b), self.first + 4 + i
+            ).start()
 
     def send(self, i, dst, z, out, into):
         p = self.p
-        p.copy(self.sums.at[i], dst, (2 * z + p.y, p.b), self.first + out, self.first + into).start()
+        p.copy(self.y_recv.at[i], dst, (2 * z + p.y, p.b), self.first + out, self.first + into).start()
 
     def reduce(self):
         p = self.p
-        if self.started:
-            p.landed(self.first + 4, self.y_recv)
+        for i in range(4):
+            p.landed(self.first + 4 + i, self.y_recv.at[i])
 
         def add(i):
-            self.sums[i] = (self.y_recv[i].astype(F32) + self.mine[i].astype(F32)).astype(BF16)
+            self.y_recv[i] = (self.y_recv[i].astype(F32) + self.mine(i)).astype(BF16)
 
         add(p.there)
         add(p.beyond)
@@ -648,19 +964,19 @@
         def _():
             for k, i in ((0, p.there), (1, p.beyond)):
                 p.landed(self.first + 1 + k, self.relayed.at[k])
-                self.sums[i] = (self.sums[i].astype(F32) + self.relayed[k].astype(F32)).astype(BF16)
+                self.y_recv[i] = (self.y_recv[i].astype(F32) + self.relayed[k].astype(F32)).astype(BF16)
                 self.send(i, self.z_recv.at[1], i, 1 + k, 3)
 
     def finish(self):
         p = self.p
-        total = self.y_recv[p.z].astype(F32) + self.mine[p.z].astype(F32)
+        total = self.y_recv[p.z].astype(F32) + self.mine(p.z)
         p.landed(self.first, self.z_recv.at[0])
         total = total + self.z_recv[0].astype(F32)
         p.landed(self.first + 3, self.z_recv.at[1])
         for out in range(3):
             p.copy(self.z_recv.at[0], self.z_recv.at[0], (p.flip, p.b), self.first + out).wait_send()
-        if self.started:
-            p.copy(self.y_recv, self.y_recv, (p.flip, p.b), self.first + 4).wait_send()
+        for i in range(4):
+            p.copy(self.y_recv.at[i], self.y_recv.at[i], (p.flip, p.b), self.first + 4 + i).wait_send()
         return total + self.z_recv[1].astype(F32)
 
 
@@ -696,259 +1012,6 @@
             p.landed(self.far[k - 1], self.z_recv.at[k - 1])
             total = total + self.z_recv[k - 1].astype(F32)
         return total
-
-
-def backward_kernel(
-    dn2, middle, x, dy, wo_in, mix_in, unit_in, attn_in, lse_in, length_all, norm_in, wqkv_in,
-    cos_table, sin_table, gain_query, gain_key, gain_a, gain_f, ggu, gd, y_d,
-    dx, rqkv, rgu, rd, ro, gains_out,
-    wo, mix, unit, unit_out, lse, norm, wqkv, cos, sin, m_g, m_u,
-    dmid, dox, doq, dou, dbr, kv, kt, delta, dk2, dv2, back, dqr,
-    dpre, parts, recv, keep, gqkv, go, mixt,
-    s_d, t_d, z_d, y_g, t_g, z_g, y_u, t_u, z_u, y_q, z_q, y_o, z_o, fin_g, fin_u, fin_q,
-    gain_sum, gain_batch, gain_seq,
-    send_sem, recv_sem, local_sem,
-):
-    p = Place(send_sem, recv_sem, local_sem)
-    s, b, z, y = p.s, p.b, p.z, p.y
-    p.hello()
-    my_positions = pl.ds(pl.multiple_of(256 * s, 256), 256)
-    load_wo = p.local(wo_in, wo)
-    load_unit = p.local(unit_in, unit)
-    load_more = [p.local(attn_in, unit_out), p.local(lse_in, lse)]
-    load_g = p.local(ggu.at[:, y, 0], m_g)
-    load_u = p.local(ggu.at[:, y, 1], m_u)
-    load_mix = p.local(mix_in, mix)
-    load_last = [
-        p.local(norm_in, norm), p.local(wqkv_in, wqkv),
-        p.local(cos_table.at[my_positions], cos), p.local(sin_table.at[my_positions], sin),
-    ]
-    p.meet()
-    sum_d = SeqTree(p, gd, y_d, t_d, z_d, s_d)
-    sum_g = SeqTree(p, m_g, y_g, t_g, z_g)
-    sum_u = SeqTree(p, m_u, y_u, t_u, z_u)
-    sum_g.start(ggu.at[:, 1 - y, 0])
-    sum_d.reduce()
-
-    mid = middle[...]
-    r2 = rms_factor(mid)
-    grad_two = dn2[...]
-    gain_sum[...] = jnp.zeros((8, 1024), F32)
-    gain_sum[1:2] = jnp.sum(grad_two * mid * r2, axis=0, keepdims=True)
-    dm = dy[...].astype(F32) + norm_back(grad_two * gain_f[...], mid, r2)
-    dmid[...] = dm
-    dbr[b] = dm.astype(BF16)
-    load_wo.wait()
-    for c in range(4):
-        for kk in (0, 1):
-            h = 2 * c + kk
-            dox[c, kk] = nt(dbr[b], wo[h].reshape(128, 1024)).astype(BF16)
-    got_do = []
-    for k in (1, 2, 3):
-        to = lax.rem(b + k, 4)
-        got_do.append(p.post(dox.at[to], doq.at[pl.ds(2 * b, 2)], (s, to)))
-    doq[pl.ds(2 * b, 2)] = dox[b]
-    dbr_across = p.post(dbr.at[b], dbr.at[b], (s, p.across))
-    dbr_core = p.post(dbr.at[b], dbr.at[b], (s, p.core))
-    for k in (1, 2, 3):
-        p.landed(got_do[k - 1], doq.at[pl.ds(2 * lax.rem(b + 4 - k, 4), 2)])
-    got_unit = []
-    for k in range(1, 8):
-        to = lax.rem(s + k, 8)
-        got_unit.append(p.post(doq.at[to], dou.at[s], (to, b)))
-    dou[s] = doq[s]
-    load_unit.wait()
-
-    def prepare(i, carry):
-        live = i * 256 + rows_of((256, 128)) < length_all[z][0:1, :]
-        masked = jnp.where(live, unit[i, :, 128:256].astype(F32), 0.0)
-        kv[i] = masked.astype(BF16)
-        kt[i] = jnp.transpose(masked)[0:64].astype(BF16)
-        dk2[i] = jnp.zeros((256, 128), F32)
-        dv2[i] = jnp.zeros((256, 128), F32)
-        return carry
-
-    lax.fori_loop(0, 8, prepare, 0)
-    sum_d.relay()
-    p.landed(dbr_across, dbr.at[p.across])
-    dbr_far = p.post(dbr.at[p.across], dbr.at[p.across], (s, p.core))
-    for k in range(1, 8):
-        p.landed(got_unit[k - 1], dou.at[lax.rem(s + 8 - k, 8)])
-
-    for made in load_more:
-        made.wait()
-
-    def queries(t, carry):
-        i = 7 - t
-        q, do = unit[i, :, 0:128].astype(F32), dou[i].astype(F32)
-        qt, dot = jnp.transpose(q).astype(BF16), jnp.transpose(do)
-        first = lanes(q.shape) < 64
-        blank = jnp.zeros((64, 512), BF16)
-        qr = jnp.concatenate([jnp.concatenate([qt[0:64], qt[64:128]], axis=1), blank], axis=0)
-        dr = jnp.concatenate([dot[0:64], dot[64:128]], axis=1).astype(BF16)
-        dr = jnp.concatenate([blank, dr], axis=0)
-        ql = jnp.concatenate([jnp.where(first, q, 0.0), jnp.where(first, 0.0, q)], axis=0).astype(BF16)
-        dl = jnp.concatenate([jnp.where(first, do, 0.0), jnp.where(first, 0.0, do)], axis=0).astype(BF16)
-        both = dot * jnp.transpose(unit_out[i].astype(F32))
-        low = jnp.sum(both[0:64], axis=0, keepdims=True)
-        high = jnp.sum(both[64:128], axis=0, keepdims=True)
-        shift = jnp.concatenate([low, high], axis=1)
-        log_total = lse[i][0:1]
-
-        def block(j, probs):
-            ds = (probs * (nn(kv[j], dr) - shift)).astype(BF16)
-            dv2[j] += nn(probs.astype(BF16), dl)
-            dk2[j] += nn(ds, ql)
-            return nn(kt[j], ds)
-
-        def step(j, acc):
-            return acc + block(j, jnp.exp(nn(kv[j], qr) - log_total))
-
-        acc = lax.fori_loop(0, i, step, jnp.zeros((64, 512), F32))
-        causal = rows_of((256, 512)) <= lax.rem(lanes((256, 512)), 256)
-        acc = acc + block(i, jnp.where(causal, jnp.exp(nn(kv[i], qr) - log_total), 0.0))
-        dq = jnp.concatenate([acc[:, 0:256], acc[:, 256:512]], axis=0) * 0.125
-        back[i, :, 0:128] = jnp.transpose(dq).astype(BF16)
-        live = i * 256 + rows_of((256, 128)) < length_all[z][0:1, :]
-        dk, dv = dk2[i], dv2[i]
-        dk = dk + pltpu.roll(dk, 64, 1)
-        dv = dv + pltpu.roll(dv, 64, 1)
-        dkv = jnp.where(lanes((256, 128)) < 64, dk, dv)
-        back[i, :, 128:256] = jnp.where(live, dkv, 0.0).astype(BF16)
-        return carry
-
-    lax.fori_loop(0, 1, queries, 0)
-    load_g.wait()
-    sum_g.reduce()
-    sum_u.start(ggu.at[:, 1 - y, 1])
-    lax.fori_loop(1, 4, queries, 0)
-    sum_g.relay()
-    lax.fori_loop(4, 8, queries, 0)
-    got_back = []
-    for k in range(1, 8):
-        to = lax.rem(s + k, 8)
-        got_back.append(p.post(back.at[to], dqr.at[s], (to, b)))
-    dqr[s] = back[s]
-
-    p.landed(dbr_core, dbr.at[p.core])
-    p.landed(dbr_far, dbr.at[p.far])
-
-    load_mix.wait()
-
-    def turn(e, carry):
-        for g in range(4):
-            mixt[:, 256 * g : 256 * g + 256] = jnp.transpose(
-                mix[e // 2, 2 * g + lax.rem(e, 2)].astype(F32)
-            ).astype(BF16)
-        left = mixt[pl.ds(pl.multiple_of(32 * b, 32), 32)]
-        go[e // 2, lax.rem(e, 2)] = nn(left, dbr[...].reshape(1024, 1024)).astype(BF16)
-        return carry
-
-    lax.fori_loop(0, 8, turn, 0)
-    sum_o = SeqSum(p, y_o, z_o)
-    sum_o.start(go)
-    load_u.wait()
-    sum_u.reduce()
-    for made in load_last:
-        made.wait()
-    gain_q, gain_k = twice(gain_query), twice(gain_key)
-    for k in range(1, 8):
-        p.landed(got_back[k - 1], dqr.at[lax.rem(s + 8 - k, 8)])
-
-    first_n = p.slots(3)
-    zero_row = jnp.zeros((1, 128), F32)
-
-    def heads(t, carry):
-        sum_q, sum_k = carry
-        g = batch_order(p, t)
-        whole = nn(norm[g], wqkv[...].reshape(1024, 512))
-        for kk in (0, 1):
-            at = 256 * kk
-            q, k = heads_of(whole, kk)
-            rq = lax.rsqrt(head_mean(q * q) + eps)
-            rk = lax.rsqrt(head_mean(k * k) + eps)
-            dq = rope_back(dqr[2 * g + kk, :, 0:128].astype(F32), cos[...], sin[...])
-            dkv = dqr[2 * g + kk, :, 128:256].astype(F32)
-            dk = rope_back(dkv, cos[...], sin[...])
-            sum_q = sum_q + jnp.sum(dq * q * rq, axis=0, keepdims=True)
-            sum_k = sum_k + jnp.sum(dk * k * rk, axis=0, keepdims=True)
-            dq = dq * gain_q
-            dk = dk * gain_k
-            dq = rq * (dq - q * rq * rq * head_mean(dq * q))
-            dk = rk * (dk - k * rk * rk * head_mean(dk * k))
-            dpre[g, :, at : at + 128] = dq.astype(BF16)
-            dpre[g, :, at + 128 : at + 256] = jnp.where(lanes(dk.shape) < 64, dk, dkv).astype(BF16)
-        part = nt(dpre[g], wqkv[...].reshape(1024, 512))
-        parts[g] = part.astype(BF16)
-
-        @pl.when(t == 3)
-        def _():
-            keep[...] = part
-
-        chip_sum_post(p, t, parts, recv, first_n)
-        return (sum_q, sum_k)
-
-    sum_q, sum_k = lax.fori_loop(0, 4, heads, (zero_row, zero_row))
-    gain_sum[2:3, 0:128] = sum_q
-    gain_sum[3:4, 0:128] = sum_k
-    chip_sum_across(p, parts, recv, first_n)
-
-    def qkv_rows(c, carry):
-        at = pl.multiple_of(128 * c, 128)
-        left = norm[:, :, pl.ds(at, 128)].reshape(1024, 128)
-        gqkv[c // 2, lax.rem(c, 2)] = tn(left, dpre[...].reshape(1024, 512)).astype(BF16)
-        return carry
-
-    lax.fori_loop(0, 8, qkv_rows, 0)
-    sum_qkv = SeqSum(p, y_q, z_q)
-    sum_qkv.start(gqkv)
-    sum_u.relay()
-    sum_o.middle()
-
-    dn1 = keep[...] + chip_sum_rest(p, parts, recv, first_n)
-    xf = x[...].astype(F32)
-    r1 = rms_factor(xf)
-    gain_sum[0:1] = jnp.sum(dn1 * xf * r1, axis=0, keepdims=True)
-    dx[...] = (dmid[...] + norm_back(dn1 * gain_a[...], xf, r1)).astype(BF16)
-    got_gain = [p.post(gain_sum, gain_batch.at[b], (s, lax.rem(b + k, 4))) for k in (1, 2, 3)]
-    gain_batch[b] = gain_sum[...]
-    sum_qkv.middle()
-
-    rd[...] = sum_d.finish()
-
-    def exchange(total, fin, dst):
-        fin[...] = total.astype(BF16)
-        got = []
-        for k in (1, 2, 3):
-            to = lax.rem(b + k, 4)
-            rows = pl.ds(pl.multiple_of(32 * to, 32), 32)
-            got.append(p.post(fin.at[rows], dst(b), (s, to)))
-        dst(b)[...] = fin[pl.ds(pl.multiple_of(32 * b, 32), 32)]
-        return got
-
-    def arrive(got, dst):
-        for k in (1, 2, 3):
-            p.landed(got[k - 1], dst(lax.rem(b + 4 - k, 4)))
-
-    dst_g, dst_u, dst_q = (lambda i: rgu.at[i, 0]), (lambda i: rgu.at[i, 1]), (lambda i: rqkv.at[i])
-    got_g = exchange(sum_g.finish(), fin_g, dst_g)
-    for k in (1, 2, 3):
-        p.landed(got_gain[k - 1], gain_batch.at[lax.rem(b + 4 - k, 4)])
-    gain_seq[s] = (gain_batch[0] + gain_batch[1]) + (gain_batch[2] + gain_batch[3])
-    got_all = [p.post(gain_seq.at[s], gain_seq.at[s], (lax.rem(s + k, 8), b)) for k in range(1, 8)]
-    got_u = exchange(sum_u.finish(), fin_u, dst_u)
-    ro[...] = sum_o.finish()
-    got_q = exchange(sum_qkv.finish(), fin_q, dst_q)
-    for k in range(1, 8):
-        p.landed(got_all[k - 1], gain_seq.at[lax.rem(s + 8 - k, 8)])
-    total = gain_seq[0]
-    for k in range(1, 8):
-        total = total + gain_seq[k]
-    gains_out[...] = total
-    arrive(got_g, dst_g)
-    arrive(got_u, dst_u)
-    arrive(got_q, dst_q)
-    p.drain()
 
 
 def finish_kernel(
@@ -994,7 +1057,7 @@
             pltpu.SemaphoreType.DMA((sems[1],)),
         ],
         compiler_params=pltpu.CompilerParams(
-            collective_id=cid, has_side_effects=True, vmem_limit_bytes=60 * 2**20
+            collective_id=cid, has_side_effects=True, vmem_limit_bytes=64 * 2**20
         ),
     )
 
@@ -1011,63 +1074,35 @@
     sine = jnp.asarray(np.tile(np.sin(angles), (1, 4)), F32)
     gains = [g[None] for g in (gain_query, gain_key, gain_attn, gain_ffn)]
 
-    (
-        output, dn2, ggu, gd_mine, gd_other, wo, wqkv, norm, unit, lse, unit_out, mix, middle, length_all,
-    ) = call(
-        forward_kernel,
+    raw = call(
+        block_kernel,
         [
-            ((256, 1024), BF16), ((256, 1024), F32), ((8, 2, 128, 1152), BF16), ((4, 144, 1024), BF16),
-            ((4, 144, 1024), BF16), ((8, 4, 32, 1024), BF16), ((8, 128, 512), BF16),
-            ((4, 256, 1024), BF16), ((8, 256, 256), BF16), ((8, 8, 512), F32), ((8, 256, 128), BF16),
-            ((4, 8, 256, 128), BF16), ((256, 1024), F32), ((4, 8, 128), jnp.int32),
+            ((256, 1024), BF16), ((256, 1024), BF16), ((4, 32, 512), BF16), ((4, 2, 32, 1152), BF16),
+            ((144, 1024), F32), ((32, 1024), F32), ((8, 1024), F32), ((4, 256, 1024), BF16),
         ],
-        [VMEM, VMEM, SMEM] + [VMEM] * 6 + [ANY] * 3 + [VMEM] * 4,
-        [VMEM, VMEM, ANY, ANY, VMEM] + [ANY] * 7 + [VMEM] * 2,
+        [ANY, ANY, SMEM] + [VMEM] * 6 + [ANY] * 3 + [VMEM] * 4,
+        [ANY] * 2 + [VMEM] * 5 + [ANY],
         [
             ((4, 256, 1024), BF16), ((4, 256, 1024), BF16), ((8, 128, 512), BF16), ((8, 4, 32, 1024), BF16),
             ((8, 256, 256), BF16), ((8, 256, 256), BF16), ((8, 256, 128), BF16), ((8, 8, 512), F32),
-            ((8, 256, 128), BF16), ((8, 80, 256), BF16), ((4, 8, 256, 128), BF16), ((4, 256, 1024), BF16),
+            ((8, 256, 128), BF16), ((4, 8, 256, 128), BF16),
             ((4, 256, 1024), BF16), ((8, 2, 128, 1152), BF16), ((8, 144, 1024), BF16), ((1152, 1024), BF16),
-            ((1024, 1152), BF16), ((1024, 1152), BF16), ((1024, 1152), BF16),
-            ((4, 256, 1024), BF16), ((3, 256, 1024), BF16), ((4, 256, 1024), BF16),
-            ((3, 256, 1024), BF16), ((256, 1024), F32), ((256, 1024), F32),
+            ((1024, 1152), BF16), ((4, 2, 128, 1152), BF16), ((4, 2, 128, 1152), BF16),
+            ((8, 256, 128), F32), ((8, 256, 128), F32),
+            ((4, 256, 1024), BF16), ((3, 256, 1024), BF16), ((3, 256, 1024), BF16),
+            ((256, 1024), F32), ((256, 1024), F32), ((256, 1024), F32),
             ((4, 32, 512), BF16), ((4, 2, 32, 1152), BF16), ((8, 128), jnp.int32),
-            ((256, 128), F32), ((256, 128), F32),
-        ],
-        0,
-        (128, 32),
-    )(x, dy, lengths, w_query, key_weight, value_weight, w_out, w_gate, w_up, w_down, cosine, sine, *gains)
-
-    raw = call(
-        backward_kernel,
-        [
-            ((256, 1024), BF16), ((4, 32, 512), BF16), ((4, 2, 32, 1152), BF16),
-            ((144, 1024), F32), ((32, 1024), F32), ((8, 1024), F32),
-        ],
-        [VMEM] * 4 + [ANY] * 5 + [VMEM] + [ANY] * 4 + [VMEM] * 4 + [ANY, VMEM, VMEM],
-        [VMEM] * 6,
-        [
-            ((8, 4, 32, 1024), BF16), ((4, 8, 256, 128), BF16), ((8, 256, 256), BF16), ((8, 256, 128), BF16),
-            ((8, 8, 512), F32), ((4, 256, 1024), BF16), ((8, 128, 512), BF16), ((256, 128), F32),
-            ((256, 128), F32), ((4, 128, 1152), BF16), ((4, 128, 1152), BF16),
-            ((256, 1024), F32), ((4, 2, 256, 128), BF16), ((8, 256, 128), BF16), ((8, 256, 128), BF16),
-            ((4, 256, 1024), BF16), ((8, 256, 128), BF16), ((8, 64, 256), BF16), ((8, 8, 512), F32),
-            ((8, 256, 128), F32), ((8, 256, 128), F32), ((8, 256, 256), BF16), ((8, 256, 256), BF16),
-            ((4, 256, 512), BF16), ((4, 256, 1024), BF16), ((3, 256, 1024), BF16), ((256, 1024), F32),
-            ((4, 2, 128, 512), BF16), ((4, 2, 32, 1024), BF16), ((128, 1024), BF16),
+            ((256, 128), F32), ((256, 128), F32), ((4, 8, 128), jnp.int32),
+            ((8, 256, 128), BF16), ((8, 8, 512), F32),
             ((4, 144, 1024), BF16), ((2, 144, 1024), BF16), ((2, 144, 1024), BF16),
             ((4, 128, 1152), BF16), ((2, 128, 1152), BF16), ((2, 128, 1152), BF16),
             ((4, 128, 1152), BF16), ((2, 128, 1152), BF16), ((2, 128, 1152), BF16),
             ((4, 128, 512), BF16), ((3, 128, 512), BF16), ((4, 32, 1024), BF16), ((3, 32, 1024), BF16),
-            ((128, 1152), BF16), ((128, 1152), BF16), ((128, 512), BF16),
             ((8, 1024), F32), ((4, 8, 1024), F32), ((8, 8, 1024), F32),
         ],
-        1,
-        (96, 32),
-    )(
-        dn2, middle, x, dy, wo, mix, unit, unit_out, lse, length_all, norm, wqkv,
-        cosine, sine, *gains, ggu.reshape(4, 2, 2, 128, 1152), gd_mine, gd_other,
-    )
+        0,
+        (256, 32),
+    )(x, dy, lengths, w_query, key_weight, value_weight, w_out, w_gate, w_up, w_down, cosine, sine, *gains)
     done = pl.pallas_call(
         finish_kernel,
         out_shape=[
@@ -1080,7 +1115,7 @@
         ],
         in_specs=[VMEM] * 7,
         out_specs=[VMEM] * 13,
-    )(output, *raw)
+    )(*raw[:7])
     return (
         done[0].reshape(256, 1, 1024), done[1].reshape(256, 1, 1024), *done[2:9], *[g[0] for g in done[9:]],
     )

time: 330 us -> 305 us (0.924)
  Pallas kernels: 324 us -> 301 us
    pallas_call x2 -> x1, Pallas kernels: 321 us -> 298 us  [body(): call(block_kernel, [((256, 1024), BF16), ((256, 1024), BF16), ((4, 32, 51...]
where the time goes in v4:
time: 305 us; the launch traced here: 302 us
  Pallas kernels  301 us (99%)
    pallas_call x1, Pallas kernels, body(): call(block_kernel, [((256, 1024), BF16), ((256, 1024), BF16), ((4, 32, 51...  298 us

profile of v4, /device:TPU:0, one launch (start us, length us, event | category | flops | bytes accessed | tf_op | source)
XLA Modules:
  0.0 302.5 jit_solution(4241038246804773116)
XLA Ops:
  1.3 297.6 %shard_map.255 = (bf16[256,1024]{1,0:T(8,128)(2,1)}, bf16[256,1024]{1,0:T(8,128)(2,1)}, bf16[4,32,512]{2,1,0:T(8,128)(2,1)}, bf16[4,2,32,1152]{3,2,1,0:T(8,128)(...) custom-call(bf16[256,1024]{1,0:T(8,128)(2,1)} %bitcast.12, ...), custom_call_target="tpu_custom_call" | custom-call | tf_op jit(solution)/shard_map/pallas_call | solution.py:1077
  298.9 3.6 %shard_map.256 = (bf16[256,1024]{1,0:T(8,128)(2,1)}, bf16[256,1024]{1,0:T(8,128)(2,1)}, f32[32,1024]{1,0:T(8,128)}, f32[32,512]{1,0:T(8,128)}, f32[32,512]{1,0:T...) custom-call(bf16[256,1024]{1,0:T(8,128)(2,1)} %get-tuple-element.33., ...), custom_call_target="tpu_custom_call" | custom-call | tf_op jit(solution)/shard_map/pallas_call | solution.py:1106

commit v5 on v4

--- a/solution.py
+++ b/solution.py
@@ -157,11 +157,18 @@
     def send(self, s, device, out, into):
         self.p.copy(self.slot(s), self.slot(s), device, self.first + out, self.first + into).start()
 
-    def start(self):
+    def start_z(self):
         p = self.p
         self.send(p.s, (2 * p.pair + p.y, p.b), 0, 0)
         self.send(p.s, (2 * p.there + p.y, p.b), 1, jnp.where(p.inner, 1, 2))
+
+    def start_y(self):
+        p = self.p
         self.send(p.s, (p.flip, p.b), 4, 3)
+
+    def start(self):
+        self.start_z()
+        self.start_y()
 
     def land(self, j):
         p = self.p
@@ -285,6 +292,8 @@
     spread_d = Spread(p, lambda i: wd.at[i])
     spread_g = Spread(p, lambda i: wgu.at[i, 0])
     spread_u = Spread(p, lambda i: wgu.at[i, 1])
+    own_d.wait()
+    spread_d.start_y()
 
     def normalize(g):
         xg = xa[g].astype(F32)
@@ -305,8 +314,7 @@
         slot = 2 * p.down(k) + y
         p.landed(z_qkv[k - 1], wqkv.at[slot])
         y_qkv.append(p.post(wqkv.at[slot], wqkv.at[slot], (p.flip, b)))
-    own_d.wait()
-    spread_d.start()
+    spread_d.start_z()
     own_wo.wait()
     z_wo = [p.post(wo.at[s, b], wo.at[s, b], (2 * p.up(k) + y, b)) for k in (1, 2, 3)]
     y_wo = [p.post(wo.at[s, b], wo.at[s, b], (p.flip, b))]
@@ -320,6 +328,11 @@
     for k in (1, 2, 3):
         p.landed(y_qkv[k], wqkv.at[2 * p.down(k) + 1 - y])
     gain_q, gain_k = twice(gain_query), twice(gain_key)
+    own_gu.wait()
+    for k in (1, 2, 3):
+        p.landed(got_gu[k - 1], wgu.at[s, :, my_rows])
+    spread_g.start_y()
+    spread_u.start_y()
 
     first_unit = p.slots(8)
 
@@ -373,17 +386,12 @@
         src = lax.rem(s + k, 8)
         p.landed(first_unit + src, unit.at[src])
     own_unit.wait()
-    own_gu.wait()
-    for k in (1, 2, 3):
-        p.landed(got_gu[k - 1], wgu.at[s, :, my_rows])
-    spread_g.start()
-    spread_u.send(s, (p.flip, b), 4, 3)
+    spread_g.start_z()
     p.landed(y_wo[0], wo.at[p.flip, b])
     for k in (1, 2, 3):
         p.landed(y_wo[k], wo.at[2 * p.down(k) + 1 - y, b])
     wo_across = p.post(wo.at[:, b], wo.at[:, b], (s, p.across))
     wo_core = p.post(wo.at[:, b], wo.at[:, b], (s, p.core))
-    spread_d.land_end()
 
     def values(j):
         return dup.at[j // 2, lax.rem(j, 2), 0:80, 0:256]
@@ -435,12 +443,11 @@
         def _():
             p.copy(unit_out.at[i], mix.at[b, s], (i, b), first_mix + t).start()
 
-        @pl.when(t == 2)
-        def _():
-            spread_u.send(s, (2 * p.pair + y, b), 0, 0)
-            spread_u.send(s, (2 * p.there + y, b), 1, jnp.where(p.inner, 1, 2))
-
-        @pl.when(t == 5)
+        @pl.when(t == 3)
+        def _():
+            spread_d.land_end()
+
+        @pl.when(t == 7)
         def _():
             spread_g.land(0)
             spread_g.land_inner()
@@ -452,14 +459,13 @@
         return carry
 
     lax.fori_loop(0, 8, attend, 0)
+    spread_u.start_z()
     own_mix = p.local(unit_out.at[s], mix.at[b, s])
     own_mix.wait()
     mix_send(s, 7)
     for t in range(4, 7):
         mix_arrived(t)
     spread_g.land_end()
-    spread_u.land(0)
-    spread_u.land_inner()
     p.landed(dy_core, dy_all.at[p.core])
     p.landed(dy_far, dy_all.at[p.far])
     spread_d.finish()
@@ -479,7 +485,8 @@
         p.landed(first_core + t, mix.at[p.core, lax.rem(s + 7 - t, 8)])
     p.landed(wo_core, wo.at[:, p.core])
     p.landed(wo_far, wo.at[:, p.far])
-    spread_u.land_end()
+    spread_u.land(0)
+    spread_u.land_inner()
     p.landed(mix_far, mix.at[p.far])
 
     parked.wait()
@@ -516,6 +523,7 @@
         return carry
 
     lax.fori_loop(0, 8, turn, 0)
+    spread_u.land_end()
     spread_g.finish()
 
     def gate_of(g, carry):
@@ -527,8 +535,7 @@
     spread_u.finish()
     first_n = p.slots(3)
 
-    def gated(t, carry):
-        g = batch_order(p, t)
+    def gated(g, carry):
         rows = pl.ds(pl.multiple_of(g * 256, 256), 256)
         gate = hid[rows].astype(F32)
         up = nn(norm[g], wgu[:, 1].reshape(1024, 1152))
@@ -536,11 +543,36 @@
         sg = 1.0 / (1.0 + jnp.exp(-gate))
         swish = gate * sg
         hid[rows] = (swish * up).astype(BF16)
-        dg = (dh * up * sg * (1.0 + gate * (1.0 - sg))).astype(BF16)
-        du = (dh * swish).astype(BF16)
-        dgate[g] = dg.reshape(2, 128, 1152)
-        dup[g] = du.reshape(2, 128, 1152)
-        part = nt(dg, wgu[:, 0].reshape(1024, 1152)) + nt(du, wgu[:, 1].reshape(1024, 1152))
+        dgate[g] = (dh * up * sg * (1.0 + gate * (1.0 - sg))).astype(BF16).reshape(2, 128, 1152)
+        dup[g] = (dh * swish).astype(BF16).reshape(2, 128, 1152)
+        return carry
+
+    lax.fori_loop(0, 4, gated, 0)
+
+    def down_rows(c, carry, at=None):
+        rows = pl.multiple_of(128 * c, 128)
+        gd[pl.ds(rows, 128), at] = tn(
+            hid[:, pl.ds(rows, 128)], dy_all[:, :, at].reshape(1024, 512)
+        ).astype(BF16)
+        return carry
+
+    halves = (pl.ds(0, 512), pl.ds(512, 512))
+    sum_d, more_d = [
+        SeqTree(
+            p,
+            functools.partial(lambda at, i: gd.at[pl.ds(pl.multiple_of(144 * i, 16), 144), at], at),
+            y_d.at[:, :, at], t_d.at[:, :, at], z_d.at[:, :, at],
+        )
+        for at in halves
+    ]
+    lax.fori_loop(0, 9, functools.partial(down_rows, at=halves[0]), 0)
+    sum_d.start()
+
+    def narrowed(t, carry):
+        g = batch_order(p, t)
+        part = nt(dgate[g].reshape(256, 1152), wgu[:, 0].reshape(1024, 1152)) + nt(
+            dup[g].reshape(256, 1152), wgu[:, 1].reshape(1024, 1152)
+        )
         parts[g] = part.astype(BF16)
 
         @pl.when(t == 3)
@@ -550,21 +582,19 @@
         chip_sum_post(p, t, parts, recv, first_n)
         return carry
 
-    lax.fori_loop(0, 4, gated, 0)
+    lax.fori_loop(0, 4, narrowed, 0)
     chip_sum_across(p, parts, recv, first_n)
-
-    def down_rows(c, carry):
-        at = pl.multiple_of(128 * c, 128)
-        gd[pl.ds(at, 128)] = tn(hid[:, pl.ds(at, 128)], dy_all[...].reshape(1024, 1024)).astype(BF16)
-        return carry
-
-    lax.fori_loop(0, 9, down_rows, 0)
-    sum_d = SeqTree(
-        p, lambda i: gd.at[pl.ds(pl.multiple_of(144 * i, 16), 144)], y_d, t_d, z_d
-    )
-    sum_g = SeqTree(p, lambda i: wgu.at[i, 0], y_g, t_g, z_g)
-    sum_u = SeqTree(p, lambda i: wgu.at[i, 1], y_u, t_u, z_u)
-    sum_d.start()
+    lax.fori_loop(0, 9, functools.partial(down_rows, at=halves[1]), 0)
+    more_d.start()
+    parts_of = (pl.ds(0, 640), pl.ds(640, 512))
+
+    def tree(which, at, y_recv, relayed, z_recv):
+        return SeqTree(
+            p, lambda i: wgu.at[i, which, :, at], y_recv.at[:, :, at], relayed.at[:, :, at], z_recv.at[:, :, at]
+        )
+
+    sum_g, more_g = [tree(0, at, y_g, t_g, z_g) for at in parts_of]
+    sum_u, more_u = [tree(1, at, y_u, t_u, z_u) for at in parts_of]
 
     for spread in (spread_d, spread_g, spread_u):
         spread.drain()
@@ -681,11 +711,11 @@
             p.landed(first_mixed + index, mix.at[1, pl.ds(2 * near_first(p, t), 2)])
         for kk in (0, 1):
             grad_piece(t, kk, lambda made: made.start())
+    sum_g.start()
+    sum_d.reduce()
     dou[s] = mix[1, s]
 
     chip_sum_across(p, dy_all, recv_o, first_o)
-    sum_d.reduce()
-    sum_g.start()
     for k in range(1, 8):
         src = lax.rem(s + k, 8)
         p.landed(first_do + src, dou.at[src])
@@ -745,14 +775,22 @@
             p.landed(dbr_across, xa.at[p.across])
             p.copy(xa.at[p.across], xa.at[p.across], (s, p.core), dbr_far).start()
 
-        @pl.when(t == 4)
+        @pl.when(t == 1)
         def _():
             sum_d.relay()
+
+        @pl.when(t == 2)
+        def _():
+            more_g.start()
+            more_d.reduce()
 
         return carry
 
     dbr_far = p.slots(1)
     lax.fori_loop(0, 8, blocks, 0)
+    sum_u.start()
+    sum_g.reduce()
+    more_d.relay()
     unit[s] = pack[s]
 
     p.landed(dbr_core, xa.at[p.core])
@@ -763,8 +801,6 @@
     sum_o = SeqSum(p, y_o, z_o)
     sum_o.start(dgate.at[:, :, 0:32, 0:1024])
     load_x = p.local(x, xa.at[p.far])
-    sum_g.reduce()
-    sum_u.start()
     load_norm.wait()
 
     first_n = p.slots(3)
@@ -799,6 +835,8 @@
         return (sum_q, sum_k)
 
     sum_q, sum_k = lax.fori_loop(0, 8, heads, (zero_row, zero_row))
+    sum_g.relay()
+    more_g.reduce()
 
     gain_sum[2:3, 0:128] = sum_q
     gain_sum[3:4, 0:128] = sum_k
@@ -811,7 +849,7 @@
     lax.fori_loop(0, 8, qkv_rows, 0)
     sum_qkv = SeqSum(p, y_q, z_q)
     sum_qkv.start(dup.at[:, :, :, pl.ds(512, 512)])
-    sum_g.relay()
+    more_u.start()
 
     def stream_back(t, carry):
         g = batch_order(p, t)
@@ -829,6 +867,7 @@
     chip_sum_across(p, parts, recv, first_n)
     sum_o.middle()
     sum_u.reduce()
+    more_g.relay()
     xa[p.core] = (result[...] + chip_sum_rest(p, dy_all, recv_o, first_o)).astype(BF16)
     leave = [p.local(xa.at[p.core], output)]
     sum_qkv.middle()
@@ -843,8 +882,8 @@
     got_gain = [p.post(gain_sum, gain_batch.at[b], (s, lax.rem(b + k, 4))) for k in (1, 2, 3)]
     gain_batch[b] = gain_sum[...]
     sum_u.relay()
-
-    rd[...] = sum_d.finish()
+    for at, half in zip(halves, (sum_d, more_d)):
+        rd[:, at] = half.finish()
 
     def exchange(total, own, dst):
         for c in range(4):
@@ -860,24 +899,33 @@
         for k in (1, 2, 3):
             p.landed(got[k - 1], dst(lax.rem(b + 4 - k, 4)))
 
-    dst_g, dst_u, dst_q = (lambda i: rgu.at[i, 0]), (lambda i: rgu.at[i, 1]), (lambda i: rqkv.at[i])
-    got_g = exchange(sum_g.finish(), lambda c: gu_send.at[c, 0], dst_g)
+    finished = []
+
+    def hand_over(total, which, at):
+        dst = lambda i: rgu.at[i, which, :, at]
+        finished.append((exchange(total, lambda c: gu_send.at[c, which, :, at], dst), dst))
+
+    hand_over(sum_g.finish(), 0, parts_of[0])
     for k in (1, 2, 3):
         p.landed(got_gain[k - 1], gain_batch.at[lax.rem(b + 4 - k, 4)])
     gain_seq[s] = (gain_batch[0] + gain_batch[1]) + (gain_batch[2] + gain_batch[3])
     got_all = [p.post(gain_seq.at[s], gain_seq.at[s], (lax.rem(s + k, 8), b)) for k in range(1, 8)]
-    got_u = exchange(sum_u.finish(), lambda c: gu_send.at[c, 1], dst_u)
+    more_u.reduce()
+    hand_over(more_g.finish(), 0, parts_of[1])
     ro[...] = sum_o.finish()
-    got_q = exchange(sum_qkv.finish(), lambda c: qkv_send.at[c], dst_q)
+    dst_q = lambda i: rqkv.at[i]
+    finished.append((exchange(sum_qkv.finish(), lambda c: qkv_send.at[c], dst_q), dst_q))
+    hand_over(sum_u.finish(), 1, parts_of[0])
     for k in range(1, 8):
         p.landed(got_all[k - 1], gain_seq.at[lax.rem(s + 8 - k, 8)])
     total = gain_seq[0]
     for k in range(1, 8):
         total = total + gain_seq[k]
     gains_out[...] = total
-    arrive(got_g, dst_g)
-    arrive(got_u, dst_u)
-    arrive(got_q, dst_q)
+    more_u.relay()
+    hand_over(more_u.finish(), 1, parts_of[1])
+    for got, dst in finished:
+        arrive(got, dst)
     for t in range(4):
         for kk in (0, 1):
             grad_piece(t, kk, lambda made: made.wait_send())
@@ -927,9 +975,9 @@
     def mine(self, i):
         return self.slot(2 * i + self.p.y)[...].astype(F32)
 
-    def start(self):
+    def start(self, pieces=(0, 1, 2, 3)):
         p = self.p
-        for i in range(4):
+        for i in pieces:
             p.copy(
                 self.slot(2 * i + 1 - p.y), self.y_recv.at[i], (p.flip, p.b), self.first + 4 + i
             ).start()
@@ -937,6 +985,9 @@
     def send(self, i, dst, z, out, into):
         p = self.p
         p.copy(self.y_recv.at[i], dst, (2 * z + p.y, p.b), self.first + out, self.first + into).start()
+
+    def load(self, i):
+        return self.y_recv.at[i][...].astype(F32)
 
     def reduce(self):
         p = self.p
@@ -944,7 +995,7 @@
             p.landed(self.first + 4 + i, self.y_recv.at[i])
 
         def add(i):
-            self.y_recv[i] = (self.y_recv[i].astype(F32) + self.mine(i)).astype(BF16)
+            self.y_recv.at[i][...] = (self.load(i) + self.mine(i)).astype(BF16)
 
         add(p.there)
         add(p.beyond)
@@ -964,20 +1015,20 @@
         def _():
             for k, i in ((0, p.there), (1, p.beyond)):
                 p.landed(self.first + 1 + k, self.relayed.at[k])
-                self.y_recv[i] = (self.y_recv[i].astype(F32) + self.relayed[k].astype(F32)).astype(BF16)
+                self.y_recv.at[i][...] = (self.load(i) + self.relayed.at[k][...].astype(F32)).astype(BF16)
                 self.send(i, self.z_recv.at[1], i, 1 + k, 3)
 
     def finish(self):
         p = self.p
-        total = self.y_recv[p.z].astype(F32) + self.mine(p.z)
+        total = self.load(p.z) + self.mine(p.z)
         p.landed(self.first, self.z_recv.at[0])
-        total = total + self.z_recv[0].astype(F32)
+        total = total + self.z_recv.at[0][...].astype(F32)
         p.landed(self.first + 3, self.z_recv.at[1])
         for out in range(3):
             p.copy(self.z_recv.at[0], self.z_recv.at[0], (p.flip, p.b), self.first + out).wait_send()
         for i in range(4):
             p.copy(self.y_recv.at[i], self.y_recv.at[i], (p.flip, p.b), self.first + 4 + i).wait_send()
-        return total + self.z_recv[1].astype(F32)
+        return total + self.z_recv.at[1][...].astype(F32)
 
 
 class SeqSum:

time: 305 us -> 285 us (0.934)
  Pallas kernels: 301 us -> 284 us
    pallas_call x1, Pallas kernels: 298 us -> 280 us  [body(): call(block_kernel, [((256, 1024), BF16), ((256, 1024), BF16), ((4, 32, 51...]
where the time goes in v5:
time: 285 us
  Pallas kernels  284 us (100%)
    pallas_call x1, Pallas kernels, body(): call(block_kernel, [((256, 1024), BF16), ((256, 1024), BF16), ((4, 32, 51...  280 us

profile of v5, /device:TPU:0, one launch (start us, length us, event | category | flops | bytes accessed | tf_op | source)
XLA Modules:
  0.0 285.2 jit_solution(16235590952758156442)
XLA Ops:
  1.3 280.3 %shard_map.255 = (bf16[256,1024]{1,0:T(8,128)(2,1)}, bf16[256,1024]{1,0:T(8,128)(2,1)}, bf16[4,32,512]{2,1,0:T(8,128)(2,1)}, bf16[4,2,32,1152]{3,2,1,0:T(8,128)(...) custom-call(bf16[256,1024]{1,0:T(8,128)(2,1)} %bitcast.12, ...), custom_call_target="tpu_custom_call" | custom-call | tf_op jit(solution)/shard_map/pallas_call | solution.py:1128
  281.6 3.6 %shard_map.256 = (bf16[256,1024]{1,0:T(8,128)(2,1)}, bf16[256,1024]{1,0:T(8,128)(2,1)}, f32[32,1024]{1,0:T(8,128)}, f32[32,512]{1,0:T(8,128)}, f32[32,512]{1,0:T...) custom-call(bf16[256,1024]{1,0:T(8,128)(2,1)} %get-tuple-element.33., ...), custom_call_target="tpu_custom_call" | custom-call | tf_op jit(solution)/shard_map/pallas_call | solution.py:1157

commit v6 on v5

--- a/solution.py
+++ b/solution.py
@@ -382,11 +382,11 @@
     for k in (1, 2, 3):
         p.landed(got_len[k - 1], length_all.at[lax.rem(b + 4 - k, 4)])
 
+    spread_g.start_z()
     for k in range(1, 8):
         src = lax.rem(s + k, 8)
         p.landed(first_unit + src, unit.at[src])
     own_unit.wait()
-    spread_g.start_z()
     p.landed(y_wo[0], wo.at[p.flip, b])
     for k in (1, 2, 3):
         p.landed(y_wo[k], wo.at[2 * p.down(k) + 1 - y, b])
@@ -443,14 +443,15 @@
         def _():
             p.copy(unit_out.at[i], mix.at[b, s], (i, b), first_mix + t).start()
 
-        @pl.when(t == 3)
+        @pl.when(t == 1)
         def _():
             spread_d.land_end()
 
-        @pl.when(t == 7)
+        @pl.when(t == 6)
         def _():
             spread_g.land(0)
             spread_g.land_inner()
+            spread_u.start_z()
 
         @pl.when(t >= 4)
         def _():
@@ -459,7 +460,6 @@
         return carry
 
     lax.fori_loop(0, 8, attend, 0)
-    spread_u.start_z()
     own_mix = p.local(unit_out.at[s], mix.at[b, s])
     own_mix.wait()
     mix_send(s, 7)

time: 285 us -> 283 us (level)
  no operation moved by 1% of the time
where the time goes in v6:
time: 283 us
  Pallas kernels  282 us (100%)
    pallas_call x1, Pallas kernels, body(): call(block_kernel, [((256, 1024), BF16), ((256, 1024), BF16), ((4, 32, 51...  278 us

profile of v6, /device:TPU:0, one launch (start us, length us, event | category | flops | bytes accessed | tf_op | source)
XLA Modules:
  0.0 282.9 jit_solution(12218301345533034587)
XLA Ops:
  1.3 277.9 %shard_map.255 = (bf16[256,1024]{1,0:T(8,128)(2,1)}, bf16[256,1024]{1,0:T(8,128)(2,1)}, bf16[4,32,512]{2,1,0:T(8,128)(2,1)}, bf16[4,2,32,1152]{3,2,1,0:T(8,128)(...) custom-call(bf16[256,1024]{1,0:T(8,128)(2,1)} %bitcast.12, ...), custom_call_target="tpu_custom_call" | custom-call | tf_op jit(solution)/shard_map/pallas_call | solution.py:1128
  279.2 3.6 %shard_map.256 = (bf16[256,1024]{1,0:T(8,128)(2,1)}, bf16[256,1024]{1,0:T(8,128)(2,1)}, f32[32,1024]{1,0:T(8,128)}, f32[32,512]{1,0:T(8,128)}, f32[32,512]{1,0:T...) custom-call(bf16[256,1024]{1,0:T(8,128)(2,1)} %get-tuple-element.33., ...), custom_call_target="tpu_custom_call" | custom-call | tf_op jit(solution)/shard_map/pallas_call | solution.py:1157

commit v7 on v6

--- a/solution.py
+++ b/solution.py
@@ -849,8 +849,6 @@
     lax.fori_loop(0, 8, qkv_rows, 0)
     sum_qkv = SeqSum(p, y_q, z_q)
     sum_qkv.start(dup.at[:, :, :, pl.ds(512, 512)])
-    more_u.start()
-
     def stream_back(t, carry):
         g = batch_order(p, t)
         part = nt(dup[g, :, :, 0:512].reshape(256, 512), wqkv[...].reshape(1024, 512))
@@ -864,13 +862,15 @@
         return carry
 
     lax.fori_loop(0, 4, stream_back, 0)
+    more_u.start()
     chip_sum_across(p, parts, recv, first_n)
+    sum_u.reduce()
     sum_o.middle()
-    sum_u.reduce()
     more_g.relay()
     xa[p.core] = (result[...] + chip_sum_rest(p, dy_all, recv_o, first_o)).astype(BF16)
     leave = [p.local(xa.at[p.core], output)]
     sum_qkv.middle()
+    sum_u.relay()
 
     dn1 = keep[...] + chip_sum_rest(p, parts, recv, first_n)
     load_x.wait()
@@ -881,7 +881,6 @@
     leave.append(p.local(xa.at[p.far], dx))
     got_gain = [p.post(gain_sum, gain_batch.at[b], (s, lax.rem(b + k, 4))) for k in (1, 2, 3)]
     gain_batch[b] = gain_sum[...]
-    sum_u.relay()
     for at, half in zip(halves, (sum_d, more_d)):
         rd[:, at] = half.finish()
 

time: 283 us -> 284 us (level)
  no operation moved by 1% of the time
where the time goes in v7:
time: 284 us; the launch traced here: 283 us
  Pallas kernels  282 us (99%)
    pallas_call x1, Pallas kernels, body(): call(block_kernel, [((256, 1024), BF16), ((256, 1024), BF16), ((4, 32, 51...  278 us

profile of v7, /device:TPU:0, one launch (start us, length us, event | category | flops | bytes accessed | tf_op | source)
XLA Modules:
  0.0 283.1 jit_solution(9612871655819203304)
XLA Ops:
  1.3 278.2 %shard_map.255 = (bf16[256,1024]{1,0:T(8,128)(2,1)}, bf16[256,1024]{1,0:T(8,128)(2,1)}, bf16[4,32,512]{2,1,0:T(8,128)(2,1)}, bf16[4,2,32,1152]{3,2,1,0:T(8,128)(...) custom-call(bf16[256,1024]{1,0:T(8,128)(2,1)} %bitcast.12, ...), custom_call_target="tpu_custom_call" | custom-call | tf_op jit(solution)/shard_map/pallas_call | solution.py:1127
  279.5 3.6 %shard_map.256 = (bf16[256,1024]{1,0:T(8,128)(2,1)}, bf16[256,1024]{1,0:T(8,128)(2,1)}, f32[32,1024]{1,0:T(8,128)}, f32[32,512]{1,0:T(8,128)}, f32[32,512]{1,0:T...) custom-call(bf16[256,1024]{1,0:T(8,128)(2,1)} %get-tuple-element.33., ...), custom_call_target="tpu_custom_call" | custom-call | tf_op jit(solution)/shard_map/pallas_call | solution.py:1156
